TPU v7x, 32 devices: a whole 2x2x4 slice. The times are simulated.
32 devices in a mesh: order: 4 (over y, x), level: 4 (over z), freq: 2 (over core).
Axes of the slice: x: 2, y: 2, z: 4, core: 2. Of those that a mesh axis runs over, the one named last changes fastest.
Arguments:
- fourier: bfloat16 [16, 16, 4, 128, 512], P('freq', None, 'level', 'order'), parts along dimension 0, may hold values from -6 to 6
- order_slot: int32 [8], replicated, may hold values from 0 to 7, each once
- coeff_self: bfloat16 [6, 8, 64, 128, 128], P(None, 'order', 'level'), may hold values from -0.375 to 0.375
- coeff_pair: bfloat16 [6, 8, 64, 128, 128], P(None, 'order', 'level'), may hold values from -0.375 to 0.375
Outputs:
- butterfly: bfloat16 [16, 64, 128, 512], P(('freq', 'order'), 'level'), parts along dimension 0
There are 2 independent parts, one for each index of `freq`. A program takes and returns all parts, laid end to end along the dimension named above; an argument that names none is the same for every part. Nothing has to cross between parts.
Inputs may be any that keep to these rules, and one draw needn't show every extreme that they name: order_slot is a permutation of the orders.
All inputs are finite; a program needn't handle non-finite values.
Results may differ from a plain program's by a relative error of at most 0.008.
Values may be sent and summed in bfloat16 or wider, within the bound.
No kernel may reach another device: no remote copies, remote signals or barrier semaphores. Data moves between devices by JAX's collectives and lax.ppermute only.
A program may use at most 64 MiB of HBM per device.

v0:
```python
import jax
import jax.numpy as jnp
from jax import lax
from jax.sharding import PartitionSpec as P


def partner_2(value, axis, stride):
    mask = 2**stride
    pairs = [(source, source ^ mask) for source in range(lax.axis_size(axis))]
    return lax.ppermute(value, axis, pairs)


def partner_blocks(values, height):
    extent = values.shape
    halves = values.reshape(
        extent[0], extent[1] >> height + 1, 2, 1 << height, extent[2], extent[3]
    )
    return halves[:, :, ::-1].reshape(extent)


def run_levels(current, factor_self, factor_pair):
    local_bits = current.shape[1].bit_length() - 1
    for height in range(factor_self.shape[0]):
        if height < local_bits:
            partner = partner_blocks(current, height)
        else:
            partner = partner_2(current, "level", height - local_bits)
        mixed_sum = jnp.einsum(
            "sbrq,sbqc->sbrc", factor_self[height], current, preferred_element_type=jnp.float32
        )
        mixed_sum = mixed_sum + jnp.einsum(
            "sbrq,sbqc->sbrc", factor_pair[height], partner, preferred_element_type=jnp.float32
        )
        current = mixed_sum.astype(jnp.bfloat16)
    return current


def local(fourier, order_slot, coeff_self, coeff_pair):
    picked = jnp.take(fourier, order_slot, axis=0)
    order_count = lax.axis_size("order")
    level_count = lax.axis_size("level")
    orders_here = coeff_self.shape[1]
    blocks_here = coeff_self.shape[2]
    cycle_rows = coeff_self.shape[3]
    rows_here = fourier.shape[3]
    columns = fourier.shape[4]
    group_size = blocks_here // level_count
    outgoing = picked.reshape(order_count, orders_here, level_count, group_size, rows_here, columns)
    outgoing = outgoing.transpose(0, 2, 1, 3, 4, 5).reshape(
        order_count * level_count * orders_here, group_size, 1, rows_here, columns
    )
    received = lax.all_to_all(outgoing, ("order", "level"), split_axis=0, concat_axis=2, tiled=True)
    received = received.reshape(
        orders_here, group_size, order_count, level_count, rows_here, columns
    )
    current = received.transpose(0, 1, 3, 2, 4, 5).reshape(
        orders_here, blocks_here, cycle_rows, columns
    )
    result = run_levels(current, coeff_self, coeff_pair)
    return result


def solution(mesh):
    placed = (
        P("freq", None, "level", "order", None),
        P(),
        P(None, "order", "level", None, None),
        P(None, "order", "level", None, None),
    )
    return jax.shard_map(
        local,
        mesh=mesh,
        in_specs=placed,
        out_specs=P(("freq", "order"), "level", None, None),
        check_vma=False,
    )
```

profile of v0, /device:TPU:0, one launch (start us, length us, event | category | flops | bytes accessed | tf_op | source)
XLA Modules:
  0.0 465.5 jit_solution(10266132285699946193)
XLA Ops:
  0.0 0.7 compare_and_fusion
  1.4 5.0 %gather_fusion = bf16[8,16,32,512]{3,2,1,0:T(8,128)(2,1)} fusion(bf16[8,16,32,512]{3,2,1,0:T(8,128)(2,1)} %bitcast.97, s32[1024]{0:T(1024)S(1)} %pad_clamp_fusion), kind=kCustom, calls=%fused_computation | custom fusion | bytes 8388640 | tf_op jit(solution)/shard_map/jit(_take)/gather | solution.py:39
  6.4 2.7 select_bitcast_fusion
  9.7 103.0 %all_to_all.15 = bf16[32,4,1,32,512]{4,3,1,2,0:T(8,128)(2,1)S(1)} all-to-all(bf16[32,4,1,32,512]{4,3,1,2,0:T(8,128)(2,1)S(1)} %bitcast.95), channel_id=1, replica_groups=mesh['order'=4,'level'=4,'freq'=2] {'order','level'}, dimensions={0} | all-to-all | bytes 8388608 | tf_op jit(solution)/shard_map/all_to_all | solution.py:52
  112.6 2.5 copy.29
  115.1 4.6 rev.12
  119.7 3.8 fusion.17
  123.5 4.4 add_convert_fusion.5
  127.9 6.5 %fusion.14 = f32[2,16,512,128]{3,2,1,0:T(8,128)} fusion(bf16[2,16,512,128]{3,2,1,0:T(8,128)(2,1)S(1)} %add_convert_fusion.5, bf16[6,2,16,128,128]{4,3,2,1,0:T(8,128)(2,1)} %param.6), kind=kOutput, calls=%fused_computation.22 | convolution fusion | flops 536870912 | bytes 13631488 | tf_op jit(solution)/shard_map/sbrq,sbqc->sbrc/dot_general | solution.py:28
  134.4 4.6 rev.13
  139.0 6.2 %add_convert_fusion.4 = bf16[2,16,512,128]{3,2,1,0:T(8,128)(2,1)S(1)} fusion(f32[2,16,512,128]{3,2,1,0:T(8,128)} %fusion.14, bf16[2,16,128,512]{2,3,1,0:T(8,128)(2,1)} %bitcast.91, bf16[6,2,16,128,128]{4,3,2,1,0:T(8,128)(2,1)} %param.7), kind=kOutput, calls=%fused_computation.5 | convolution fusion | flops 541065216 | bytes 17825792 | tf_op jit(solution)/shard_map/sbrq,sbqc->sbrc/dot_general | solution.py:31
  145.2 6.5 %fusion.11 = f32[2,16,512,128]{3,2,1,0:T(8,128)} fusion(bf16[2,16,512,128]{3,2,1,0:T(8,128)(2,1)S(1)} %add_convert_fusion.4, bf16[6,2,16,128,128]{4,3,2,1,0:T(8,128)(2,1)} %param.6), kind=kOutput, calls=%fused_computation.19 | convolution fusion | flops 536870912 | bytes 13631488 | tf_op jit(solution)/shard_map/sbrq,sbqc->sbrc/dot_general | solution.py:28
  151.7 4.6 rev.14
  156.3 6.2 %add_convert_fusion.3 = bf16[2,16,512,128]{3,2,1,0:T(8,128)(2,1)S(1)} fusion(f32[2,16,512,128]{3,2,1,0:T(8,128)} %fusion.11, bf16[2,16,128,512]{2,3,1,0:T(8,128)(2,1)} %bitcast.92, bf16[6,2,16,128,128]{4,3,2,1,0:T(8,128)(2,1)} %param.7), kind=kOutput, calls=%fused_computation.4 | convolution fusion | flops 541065216 | bytes 17825792 | tf_op jit(solution)/shard_map/sbrq,sbqc->sbrc/dot_general | solution.py:31
  162.5 6.5 %fusion.8 = f32[2,16,512,128]{3,2,1,0:T(8,128)} fusion(bf16[2,16,512,128]{3,2,1,0:T(8,128)(2,1)S(1)} %add_convert_fusion.3, bf16[6,2,16,128,128]{4,3,2,1,0:T(8,128)(2,1)} %param.6), kind=kOutput, calls=%fused_computation.16 | convolution fusion | flops 536870912 | bytes 13631488 | tf_op jit(solution)/shard_map/sbrq,sbqc->sbrc/dot_general | solution.py:28
  169.0 4.6 rev.15
  173.6 6.2 %add_convert_fusion.2 = bf16[2,16,512,128]{3,2,1,0:T(8,128)(2,1)S(1)} fusion(f32[2,16,512,128]{3,2,1,0:T(8,128)} %fusion.8, bf16[2,16,128,512]{2,3,1,0:T(8,128)(2,1)} %bitcast.93, bf16[6,2,16,128,128]{4,3,2,1,0:T(8,128)(2,1)} %param.7), kind=kOutput, calls=%fused_computation.3 | convolution fusion | flops 541065216 | bytes 17825792 | tf_op jit(solution)/shard_map/sbrq,sbqc->sbrc/dot_general | solution.py:31
  179.9 2.7 fusion.5
  182.6 88.6 %collective-permute-done = bf16[2,16,128,512]{2,3,1,0:T(8,128)(2,1)S(1)} collective-permute-done((bf16[2,16,128,512]{2,3,1,0:T(8,128)(2,1)S(1)}, bf16[2,16,128,512]{2,3,1,0:T(8,128)(2,1)S(1)}, u32[]{:S(2)}, u32[]{:S(2)}) %collective-permute-start) | collective-permute-done | bytes 4194336 | tf_op jit(solution)/shard_map/ppermute | solution.py:10
  271.1 2.5 add_convert_fusion.1
  273.7 2.5 fusion.2
  276.2 178.6 %collective-permute-done.1 = bf16[2,16,128,512]{2,3,1,0:T(8,128)(2,1)S(1)} collective-permute-done((bf16[2,16,128,512]{2,3,1,0:T(8,128)(2,1)S(1)}, bf16[2,16,128,512]{2,3,1,0:T(8,128)(2,1)S(1)}, u32[]{:S(2)}, u32[]{:S(2)}) %collective-permute-start.1) | collective-permute-done | bytes 4194336 | tf_op jit(solution)/shard_map/ppermute | solution.py:10
  454.8 4.5 fusion
  459.3 6.2 %copy.33 = bf16[2,16,128,512]{3,2,1,0:T(8,128)(2,1)} copy(bf16[2,16,128,512]{2,3,1,0:T(8,128)(2,1)} %fusion) | data formatting | bytes 8388608 | tf_op jit(solution)/shard_map/convert_element_type | solution.py:34
  (12 shorter events, 1.5 us)
Async XLA Ops:
  127.9 6.5 %copy-start = (bf16[2,16,512,128]{3,2,1,0:T(8,128)(2,1)}, bf16[2,16,512,128]{3,2,1,0:T(8,128)(2,1)S(1)}, u32[]{:S(2)}) copy-start(bf16[2,16,512,128]{3,2,1,0:T(8,128)(2,1)S(1)} %add_convert_fusion.5) | copy-start | bytes 12582916
  145.2 6.5 %copy-start.1 = (bf16[2,16,512,128]{3,2,1,0:T(8,128)(2,1)}, bf16[2,16,512,128]{3,2,1,0:T(8,128)(2,1)S(1)}, u32[]{:S(2)}) copy-start(bf16[2,16,512,128]{3,2,1,0:T(8,128)(2,1)S(1)} %add_convert_fusion.4) | copy-start | bytes 12582916
  162.5 6.5 %copy-start.2 = (bf16[2,16,512,128]{3,2,1,0:T(8,128)(2,1)}, bf16[2,16,512,128]{3,2,1,0:T(8,128)(2,1)S(1)}, u32[]{:S(2)}) copy-start(bf16[2,16,512,128]{3,2,1,0:T(8,128)(2,1)S(1)} %add_convert_fusion.3) | copy-start | bytes 12582916
  179.8 91.3 %collective-permute-start = (bf16[2,16,128,512]{2,3,1,0:T(8,128)(2,1)S(1)}, bf16[2,16,128,512]{2,3,1,0:T(8,128)(2,1)S(1)}, u32[]{:S(2)}, u32[]{:S(2)}) collective-permute-start(bf16[2,16,128,512]{2,3,1,0:T(8,128)(2,1)S(1)} %bitcast.88), channel_id=1, source_target_pairs={{0,2},{2,0},{4,6},{6,4},{1,3},{3,1},{5,7},{7,5},{8,10},{10,8},{12,... | collective-permute-start | bytes 12582920 | tf_op jit(solution)/shard_map/ppermute | solution.py:10
  273.7 181.2 %collective-permute-start.1 = (bf16[2,16,128,512]{2,3,1,0:T(8,128)(2,1)S(1)}, bf16[2,16,128,512]{2,3,1,0:T(8,128)(2,1)S(1)}, u32[]{:S(2)}, u32[]{:S(2)}) collective-permute-start(bf16[2,16,128,512]{2,3,1,0:T(8,128)(2,1)S(1)} %bitcast.89), channel_id=1, source_target_pairs={{0,4},{2,6},{4,0},{6,2},{1,5},{3,7},{5,1},{7,3},{8,12},{10,14},{12... | collective-permute-start | bytes 12582920 | tf_op jit(solution)/shard_map/ppermute | solution.py:10
where the time goes:
time: 466 us
  waiting for transfers between devices  267 us (57%)
  blocking collectives  103 us (22%)
  matrix products  58.5 us (13%)
  local copies, waits for them, and re-layouts  32.7 us (7%)
    ppermute x2, waiting for transfers between devices, partner_2(): return lax.ppermute(value, axis, pairs)  267 us
    all_to_all x1, blocking collectives, local(): lax.all_to_all(outgoing, ('order', 'level'), split_axis=0, concat_axis=2,...  103 us
    dot_general x6, matrix products, run_levels(): jnp.einsum('sbrq,sbqc->sbrc', factor_pair[height], partner, preferred_ele...  30 us
    dot_general x6, matrix products, run_levels(): jnp.einsum('sbrq,sbqc->sbrc', factor_self[height], current, preferred_ele...  28.4 us
    rev x4, local copies, waits for them, and re-layouts, partner_blocks(): return halves[:, :, ::-1].reshape(extent)  18.3 us
  transfers between devices with their start and end apart: 2, of which 2 were waited for; matrix products, arithmetic and copies ran while one was open for 1% of the time, Pallas kernels for 0%

commit v1 on v0

v1 whole, which is shorter than its diff:
```python
import functools

import jax
import jax.numpy as jnp
from jax import lax
from jax.experimental import pallas as pl
from jax.experimental.pallas import tpu as pltpu
from jax.sharding import PartitionSpec as P

COLUMN_PARTS = 2
VMEM = 48 * 1024 * 1024


def params(steps):
    return pltpu.CompilerParams(
        dimension_semantics=("arbitrary",) * steps, vmem_limit_bytes=VMEM
    )


def cost(flops, moved):
    return pl.CostEstimate(flops=flops, bytes_accessed=moved, transcendentals=0)


def swap(value, axis, mask):
    pairs = [(source, source ^ mask) for source in range(lax.axis_size(axis))]
    return lax.ppermute(value, axis, pairs)


def take_kernel(place_ref, slot_ref, *refs):
    half = len(refs) // 2
    for source, target in zip(refs[:half], refs[half:]):
        target[...] = source[...].reshape(target.shape)


def take_rows(fourier, place, order_slot, slot, part, masks, order_count, width):
    orders, blocks, _, rows, _ = fourier.shape
    slots_here = order_slot.shape[0] // order_count
    level_count = lax.axis_size("level")
    group = blocks // level_count
    block = (1, group, 1, rows, width)

    def source_map(mask, order, place, slots):
        return (slots[order * slots_here + slot], place[0] ^ mask, 0, 0, part)

    return pl.pallas_call(
        take_kernel,
        grid_spec=pltpu.PrefetchScalarGridSpec(
            num_scalar_prefetch=2,
            grid=(order_count,),
            in_specs=[pl.BlockSpec(block, functools.partial(source_map, mask)) for mask in masks],
            out_specs=[
                pl.BlockSpec((1, group, rows, width), lambda order, place, slots: (order, 0, 0, 0))
                for _ in masks
            ],
        ),
        out_shape=[
            jax.ShapeDtypeStruct((order_count, group, rows, width), fourier.dtype) for _ in masks
        ],
        compiler_params=params(1),
        cost_estimate=cost(0, 4 * len(masks) * order_count * group * rows * width),
        name="take_rows",
    )(place, order_slot, *[fourier] * len(masks))


def gather_kernel(masks, place_ref, slot_ref, own_ref, *refs):
    target = refs[-1]
    for mask, source in zip(masks, (own_ref,) + refs[:-1]):
        at = place_ref[0] ^ mask
        target[0, :, pl.ds(at, 1)] = source[...].reshape(target[0, :, pl.ds(0, 1)].shape)


def gather_blocks(fourier, received, place, order_slot, slot, part, order_count, width):
    _, blocks, _, rows, _ = fourier.shape
    slots_here = order_slot.shape[0] // order_count
    level_count = lax.axis_size("level")
    group = blocks // level_count

    def own_map(order, place, slots):
        return (slots[order * slots_here + slot], place[0], 0, 0, part)

    return pl.pallas_call(
        functools.partial(gather_kernel, tuple(range(level_count))),
        grid_spec=pltpu.PrefetchScalarGridSpec(
            num_scalar_prefetch=2,
            grid=(order_count,),
            in_specs=[pl.BlockSpec((1, group, 1, rows, width), own_map)]
            + [
                pl.BlockSpec((1, group, rows, width), lambda order, place, slots: (order, 0, 0, 0))
                for _ in received
            ],
            out_specs=pl.BlockSpec(
                (1, group, level_count, rows, width), lambda order, place, slots: (order, 0, 0, 0, 0)
            ),
        ),
        out_shape=jax.ShapeDtypeStruct(
            (order_count, group, level_count, rows, width), fourier.dtype
        ),
        compiler_params=params(1),
        cost_estimate=cost(0, 4 * order_count * blocks * rows * width),
        name="gather_blocks",
    )(place, order_slot, fourier, *received)


def low_kernel(rows_ref, self_ref, pair_ref, out_ref, state):
    level = pl.program_id(0)
    levels = pl.num_programs(0)
    groups, blocks, rows, width = rows_ref.shape
    bits = blocks.bit_length() - 1

    def block_of(height, block):
        if height == 0:
            return [rows_ref[group, block] for group in range(groups)]
        return [state[block]]

    for height in range(bits):

        @pl.when(level == height)
        def _(height=height):
            target = out_ref if height == bits - 1 else state
            for low in range(blocks):
                high = low ^ (1 << height)
                if high < low:
                    continue
                values = jnp.concatenate(block_of(height, low) + block_of(height, high), axis=0)
                factors = jnp.concatenate(
                    [
                        jnp.concatenate([self_ref[0, 0, low], pair_ref[0, 0, low]], axis=1),
                        jnp.concatenate([pair_ref[0, 0, high], self_ref[0, 0, high]], axis=1),
                    ],
                    axis=0,
                )
                mixed = jnp.dot(factors, values, preferred_element_type=jnp.float32)
                mixed = mixed.astype(target.dtype)
                target[low] = mixed[: mixed.shape[0] // 2]
                target[high] = mixed[mixed.shape[0] // 2 :]


def low_levels(rows, coeff_self, coeff_pair, slot):
    groups, blocks, height, width = rows.shape
    cycle = coeff_self.shape[3]
    bits = blocks.bit_length() - 1
    factor = pl.BlockSpec((1, 1, blocks, cycle, cycle), lambda level: (level, slot, 0, 0, 0))
    return pl.pallas_call(
        low_kernel,
        grid=(bits,),
        in_specs=[
            pl.BlockSpec((groups, blocks, height, width), lambda level: (0, 0, 0, 0)),
            factor,
            factor,
        ],
        out_specs=pl.BlockSpec((blocks, cycle, width), lambda level: (0, 0, 0)),
        out_shape=jax.ShapeDtypeStruct((blocks, cycle, width), rows.dtype),
        scratch_shapes=[pltpu.VMEM((blocks, cycle, width), rows.dtype)],
        compiler_params=params(1),
        cost_estimate=cost(
            4 * bits * blocks * cycle * cycle * width,
            4 * blocks * cycle * width + 4 * bits * blocks * cycle * cycle,
        ),
        name="low_levels",
    )(rows, coeff_self, coeff_pair)


def high_kernel(own_ref, other_ref, self_ref, pair_ref, *refs):
    target = refs[-1]
    lead = len(target.shape) - 3
    for block in range(own_ref.shape[0]):
        factors = jnp.concatenate([self_ref[0, 0, block], pair_ref[0, 0, block]], axis=1)
        values = jnp.concatenate([own_ref[block], other_ref[block]], axis=0)
        mixed = jnp.dot(factors, values, preferred_element_type=jnp.float32)
        target[(0,) * lead + (block,)] = mixed.astype(target.dtype)


def high_level(own, other, coeff_self, coeff_pair, level, slot, final=None):
    blocks, cycle, width = own.shape
    step = min(4, blocks)
    value = pl.BlockSpec((step, cycle, width), lambda at: (at, 0, 0))
    factor = pl.BlockSpec((1, 1, step, cycle, cycle), lambda at: (level, slot, at, 0, 0))
    operands = [own, other, coeff_self, coeff_pair]
    in_specs = [value, value, factor, factor]
    aliases = {}
    if final is None:
        out_spec, out_shape = value, jax.ShapeDtypeStruct(own.shape, own.dtype)
    else:
        result, shape, part = final
        out_spec = pl.BlockSpec((1, step, cycle, width), lambda at: (slot, at, 0, part))
        out_shape = jax.ShapeDtypeStruct(shape, own.dtype)
        if result is not None:
            operands.append(result)
            in_specs.append(pl.BlockSpec(memory_space=pl.ANY))
            aliases = {4: 0}
    return pl.pallas_call(
        high_kernel,
        grid=(blocks // step,),
        in_specs=in_specs,
        out_specs=out_spec,
        out_shape=out_shape,
        input_output_aliases=aliases,
        compiler_params=params(1),
        cost_estimate=cost(
            4 * blocks * cycle * cycle * width,
            6 * blocks * cycle * width + 4 * blocks * cycle * cycle,
        ),
        name="high_level",
    )(*operands)


def local(fourier, order_slot, coeff_self, coeff_pair):
    order_count = lax.axis_size("order")
    level_count = lax.axis_size("level")
    levels, orders_here, blocks_here, cycle_rows, _ = coeff_self.shape
    rows_here, columns = fourier.shape[3:]
    local_bits = blocks_here.bit_length() - 1
    width = columns // COLUMN_PARTS
    place = lax.axis_index("level").astype(jnp.int32).reshape(1)
    chunks = [(slot, part) for slot in range(orders_here) for part in range(COLUMN_PARTS)]
    masks = tuple(range(1, level_count))

    current = []
    for slot, part in chunks:
        outgoing = take_rows(
            fourier, place, order_slot, slot, part, masks, order_count, width
        )
        received = [swap(value, "level", mask) for value, mask in zip(outgoing, masks)]
        blocks = gather_blocks(
            fourier, received, place, order_slot, slot, part, order_count, width
        )
        blocks = blocks.reshape(order_count, blocks_here, rows_here, width)
        rows = lax.all_to_all(blocks, "order", split_axis=0, concat_axis=0, tiled=True)
        if rows_here % 16:
            rows = rows.transpose(1, 0, 2, 3).reshape(1, blocks_here, cycle_rows, width)
        current.append(low_levels(rows, coeff_self, coeff_pair, slot))

    result = None
    shape = (orders_here, blocks_here, cycle_rows, columns)
    for (slot, part), value in zip(chunks, current):
        for level in range(local_bits, levels):
            other = swap(value, "level", 1 << (level - local_bits))
            final = (result, shape, part) if level == levels - 1 else None
            value = high_level(value, other, coeff_self, coeff_pair, level, slot, final)
        result = value
    return result


def solution(mesh):
    placed = (
        P("freq", None, "level", "order", None),
        P(),
        P(None, "order", "level", None, None),
        P(None, "order", "level", None, None),
    )
    return jax.shard_map(
        local,
        mesh=mesh,
        in_specs=placed,
        out_specs=P(("freq", "order"), "level", None, None),
        check_vma=False,
    )
```

time: 466 us -> 377 us (0.81)
  blocking collectives: 103 us -> 0 us
  matrix products: 58.5 us -> 0 us
  Pallas kernels: 0 us -> 54 us
  starting transfers between devices: 0.14 us -> 52.4 us
  local copies, waits for them, and re-layouts: 32.7 us -> 11.3 us
  waiting for transfers between devices: 267 us -> 257 us
    all_to_all x1 -> x0, blocking collectives: 103 us -> none  [local(): lax.all_to_all(outgoing, ('order', 'level'), split_axis=0, concat_axis=2,...]
    dot_general x12 -> x0, matrix products: 58.5 us -> none  [the longest x6 30 us: run_levels(): jnp.einsum('sbrq,sbqc->sbrc', factor_pair[height], partner, preferred_ele...]
    pallas_call x0 -> x20, Pallas kernels: none -> 54 us  [the longest x8 26.9 us: high_level(): pl.pallas_call(high_kernel, grid=(blocks // step,), in_specs=in_specs, ou...]
    ppermute x2 -> x20, starting transfers between devices: 0.14 us -> 36.6 us  [swap(): return lax.ppermute(value, axis, pairs)]
    rev x4 -> x0, local copies, waits for them, and re-layouts: 18.3 us -> none  [partner_blocks(): return halves[:, :, ::-1].reshape(extent)]
    all_to_all x0 -> x4, starting transfers between devices: none -> 15.8 us  [local(): lax.all_to_all(blocks, 'order', split_axis=0, concat_axis=0, tiled=True)]
    unnamed x6 -> x16, local copies, waits for them, and re-layouts: 0.02 us -> 11.3 us
    ppermute x2 -> x20, waiting for transfers between devices: 267 us -> 257 us  [swap(): return lax.ppermute(value, axis, pairs)]
  transfers between devices with their start and end apart: 2 -> 24, of which waited for: 2 -> 15; matrix products, arithmetic and copies ran while one was open for 1% -> 0% of each run, Pallas kernels for 0% -> 13%
where the time goes in v1:
time: 377 us; the launch traced here: 375 us
  waiting for transfers between devices  257 us (68%)
  Pallas kernels  54 us (14%)
  starting transfers between devices  52.4 us (14%)
  local copies, waits for them, and re-layouts  11.3 us (3%)
    ppermute x20, waiting for transfers between devices, swap(): return lax.ppermute(value, axis, pairs)  257 us
    ppermute x20, starting transfers between devices, swap(): return lax.ppermute(value, axis, pairs)  36.6 us
    pallas_call x8, Pallas kernels, high_level(): pl.pallas_call(high_kernel, grid=(blocks // step,), in_specs=in_specs, ou...  26.9 us
    pallas_call x4, Pallas kernels, low_levels(): pl.pallas_call(low_kernel, grid=(bits,), in_specs=[pl.BlockSpec((groups,...  17.8 us
    all_to_all x4, starting transfers between devices, local(): lax.all_to_all(blocks, 'order', split_axis=0, concat_axis=0, tiled=True)  15.8 us
    unnamed x16, local copies, waits for them, and re-layouts  11.3 us
  transfers between devices with their start and end apart: 24, of which 15 were waited for; matrix products, arithmetic and copies ran while one was open for 0% of the time, Pallas kernels for 13%

profile of v1, /device:TPU:0, one launch (start us, length us, event | category | flops | bytes accessed | tf_op | source)
XLA Modules:
  0.0 375.3 jit_solution(2727104012981958821)
XLA Ops:
  9.4 8.6 %collective-permute-done.15.refs_0_ = bf16[4,4,32,256]{3,2,1,0:T(8,128)(2,1)S(1)} collective-permute-done((bf16[4,4,32,256]{3,2,1,0:T(8,128)(2,1)S(1)}, bf16[4,4,32,256]{3,2,1,0:T(8,128)(2,1)S(1)}, u32[]{:S(2)}, u32[]{:S(2)}) %collective-permute-start.15) | collective-permute-done | bytes 262176 | tf_op jit(solution)/shard_map/ppermute | solution.py:26
  18.0 10.2 %collective-permute-done.16.refs_1_ = bf16[4,4,32,256]{3,2,1,0:T(8,128)(2,1)S(1)} collective-permute-done((bf16[4,4,32,256]{3,2,1,0:T(8,128)(2,1)S(1)}, bf16[4,4,32,256]{3,2,1,0:T(8,128)(2,1)S(1)}, u32[]{:S(2)}, u32[]{:S(2)}) %collective-permute-start.16) | collective-permute-done | bytes 262176 | tf_op jit(solution)/shard_map/ppermute | solution.py:26
  37.1 4.8 %collective-permute-start.10 = (bf16[4,4,32,256]{3,2,1,0:T(8,128)(2,1)S(1)}, bf16[4,4,32,256]{3,2,1,0:T(8,128)(2,1)S(1)}, u32[]{:S(2)}, u32[]{:S(2)}) collective-permute-start(bf16[4,4,32,256]{3,2,1,0:T(8,128)(2,1)S(1)} %get-tuple-element.23), channel_id=1, source_target_pairs={{0,2},{2,0},{4,6},{6,4},{1,3},{3,1},{5,7},{7,5},{8,10},{10,8},{12,... | collective-permute-start | bytes 786440 | tf_op jit(solution)/shard_map/ppermute | solution.py:26
  44.4 6.4 %collective-permute-done.10.refs_0_ = bf16[4,4,32,256]{3,2,1,0:T(8,128)(2,1)S(1)} collective-permute-done((bf16[4,4,32,256]{3,2,1,0:T(8,128)(2,1)S(1)}, bf16[4,4,32,256]{3,2,1,0:T(8,128)(2,1)S(1)}, u32[]{:S(2)}, u32[]{:S(2)}) %collective-permute-start.10) | collective-permute-done | bytes 262176 | tf_op jit(solution)/shard_map/ppermute | solution.py:26
  50.8 12.5 %collective-permute-done.11.refs_1_ = bf16[4,4,32,256]{3,2,1,0:T(8,128)(2,1)S(1)} collective-permute-done((bf16[4,4,32,256]{3,2,1,0:T(8,128)(2,1)S(1)}, bf16[4,4,32,256]{3,2,1,0:T(8,128)(2,1)S(1)}, u32[]{:S(2)}, u32[]{:S(2)}) %collective-permute-start.11) | collective-permute-done | bytes 262176 | tf_op jit(solution)/shard_map/ppermute | solution.py:26
  65.5 3.9 %all-to-all-start.2 = ((bf16[4,16,32,256]{3,2,1,0:T(8,128)(2,1)}), bf16[4,16,32,256]{3,2,1,0:T(8,128)(2,1)S(1)}, u32[]{:S(2)}, u32[]{:S(2)}) async-start(bf16[4,16,32,256]{3,2,1,0:T(8,128)(2,1)} %bitcast.3), calls=%async_computation.2 | async-start | bytes 2097152 | tf_op jit(solution)/shard_map/all_to_all | solution.py:228
  78.3 4.4 %collective-permute-done.5.refs_0_ = bf16[4,4,32,256]{3,2,1,0:T(8,128)(2,1)S(1)} collective-permute-done((bf16[4,4,32,256]{3,2,1,0:T(8,128)(2,1)S(1)}, bf16[4,4,32,256]{3,2,1,0:T(8,128)(2,1)S(1)}, u32[]{:S(2)}, u32[]{:S(2)}) %collective-permute-start.5) | collective-permute-done | bytes 262176 | tf_op jit(solution)/shard_map/ppermute | solution.py:26
  82.7 13.1 %collective-permute-done.6.refs_1_ = bf16[4,4,32,256]{3,2,1,0:T(8,128)(2,1)S(1)} collective-permute-done((bf16[4,4,32,256]{3,2,1,0:T(8,128)(2,1)S(1)}, bf16[4,4,32,256]{3,2,1,0:T(8,128)(2,1)S(1)}, u32[]{:S(2)}, u32[]{:S(2)}) %collective-permute-start.6) | collective-permute-done | bytes 262176 | tf_op jit(solution)/shard_map/ppermute | solution.py:26
  97.6 3.9 %all-to-all-start.1 = ((bf16[4,16,32,256]{3,2,1,0:T(8,128)(2,1)}), bf16[4,16,32,256]{3,2,1,0:T(8,128)(2,1)S(1)}, u32[]{:S(2)}, u32[]{:S(2)}) async-start(bf16[4,16,32,256]{3,2,1,0:T(8,128)(2,1)} %bitcast.5), calls=%async_computation.1 | async-start | bytes 2097152 | tf_op jit(solution)/shard_map/all_to_all | solution.py:228
  111.0 4.7 %collective-permute-done.refs_0_ = bf16[4,4,32,256]{3,2,1,0:T(8,128)(2,1)S(1)} collective-permute-done((bf16[4,4,32,256]{3,2,1,0:T(8,128)(2,1)S(1)}, bf16[4,4,32,256]{3,2,1,0:T(8,128)(2,1)S(1)}, u32[]{:S(2)}, u32[]{:S(2)}) %collective-permute-start) | collective-permute-done | bytes 262176 | tf_op jit(solution)/shard_map/ppermute | solution.py:26
  115.7 12.9 %collective-permute-done.1.refs_1_ = bf16[4,4,32,256]{3,2,1,0:T(8,128)(2,1)S(1)} collective-permute-done((bf16[4,4,32,256]{3,2,1,0:T(8,128)(2,1)S(1)}, bf16[4,4,32,256]{3,2,1,0:T(8,128)(2,1)S(1)}, u32[]{:S(2)}, u32[]{:S(2)}) %collective-permute-start.1) | collective-permute-done | bytes 262176 | tf_op jit(solution)/shard_map/ppermute | solution.py:26
  130.3 4.2 %all-to-all-start = ((bf16[4,16,32,256]{3,2,1,0:T(8,128)(2,1)}), bf16[4,16,32,256]{3,2,1,0:T(8,128)(2,1)}, u32[]{:S(2)}, u32[]{:S(2)}) async-start(bf16[4,16,32,256]{3,2,1,0:T(8,128)(2,1)} %bitcast.6), calls=%async_computation | async-start | bytes 2097152 | tf_op jit(solution)/shard_map/all_to_all | solution.py:228
  134.6 4.9 %low_levels.7.own_ref = bf16[16,128,256]{2,1,0:T(8,128)(2,1)} custom-call(bf16[4,16,32,256]{3,2,1,0:T(8,128)(2,1)S(1)} %all-to-all-done.3.rows_ref, bf16[6,2,16,128,128]{4,3,2,1,0:T(8,128)(2,1)} %self_ref.23, bf16[6,2,16,128,128]{4,3,2,1,0:T(8,128)(2,1)} %pair_ref.23), custom_call_target="tpu_custom_call" | custom-call | flops 1073741824 | bytes 6291456 | tf_op jit(solution)/shard_map/low_levels/pallas_call | solution.py:143
  142.8 4.8 %low_levels.6.own_ref = bf16[16,128,256]{2,1,0:T(8,128)(2,1)} custom-call(bf16[4,16,32,256]{3,2,1,0:T(8,128)(2,1)S(1)} %all-to-all-done.2.rows_ref, bf16[6,2,16,128,128]{4,3,2,1,0:T(8,128)(2,1)} %self_ref.23, bf16[6,2,16,128,128]{4,3,2,1,0:T(8,128)(2,1)} %pair_ref.23), custom_call_target="tpu_custom_call" | custom-call | flops 1073741824 | bytes 6291456 | tf_op jit(solution)/shard_map/low_levels/pallas_call | solution.py:143
  147.7 3.9 %low_levels.5.own_ref = bf16[16,128,256]{2,1,0:T(8,128)(2,1)S(1)} custom-call(bf16[4,16,32,256]{3,2,1,0:T(8,128)(2,1)S(1)} %all-to-all-done.1.rows_ref, bf16[6,2,16,128,128]{4,3,2,1,0:T(8,128)(2,1)} %self_ref.23, bf16[6,2,16,128,128]{4,3,2,1,0:T(8,128)(2,1)} %pair_ref.23), custom_call_target="tpu_custom_call" | custom-call | flops 1073741824 | bytes 6291456 | tf_op jit(solution)/shard_map/low_levels/pallas_call | solution.py:143
  153.6 4.2 %low_levels.4.own_ref = bf16[16,128,256]{2,1,0:T(8,128)(2,1)S(1)} custom-call(bf16[4,16,32,256]{3,2,1,0:T(8,128)(2,1)} %all-to-all-done.rows_ref, bf16[6,2,16,128,128]{4,3,2,1,0:T(8,128)(2,1)} %self_ref.23, bf16[6,2,16,128,128]{4,3,2,1,0:T(8,128)(2,1)} %pair_ref.23), custom_call_target="tpu_custom_call" | custom-call | flops 1073741824 | bytes 6291456 | tf_op jit(solution)/shard_map/low_levels/pallas_call | solution.py:143
  158.0 9.2 %collective-permute-done.18.other_ref = bf16[16,128,256]{2,1,0:T(8,128)(2,1)} collective-permute-done((bf16[16,128,256]{2,1,0:T(8,128)(2,1)}, bf16[16,128,256]{2,1,0:T(8,128)(2,1)}, u32[]{:S(2)}, u32[]{:S(2)}) %collective-permute-start.18) | collective-permute-done | bytes 1048608 | tf_op jit(solution)/shard_map/ppermute | solution.py:26
  170.2 4.0 %collective-permute-start.19 = (bf16[16,128,256]{2,1,0:T(8,128)(2,1)S(1)}, bf16[16,128,256]{2,1,0:T(8,128)(2,1)S(1)}, u32[]{:S(2)}, u32[]{:S(2)}) collective-permute-start(bf16[16,128,256]{2,1,0:T(8,128)(2,1)S(1)} %high_level.11.own_ref), channel_id=1, source_target_pairs={{0,4},{2,6},{4,0},{6,2},{1,5},{3,7},{5,1},{7,3},{8,12},{10,14},{12... | collective-permute-start | bytes 3145736 | tf_op jit(solution)/shard_map/ppermute | solution.py:26
  174.3 37.9 %collective-permute-done.13.other_ref = bf16[16,128,256]{2,1,0:T(8,128)(2,1)} collective-permute-done((bf16[16,128,256]{2,1,0:T(8,128)(2,1)}, bf16[16,128,256]{2,1,0:T(8,128)(2,1)}, u32[]{:S(2)}, u32[]{:S(2)}) %collective-permute-start.13) | collective-permute-done | bytes 1048608 | tf_op jit(solution)/shard_map/ppermute | solution.py:26
  216.7 39.0 %collective-permute-done.8.other_ref = bf16[16,128,256]{2,1,0:T(8,128)(2,1)S(1)} collective-permute-done((bf16[16,128,256]{2,1,0:T(8,128)(2,1)S(1)}, bf16[16,128,256]{2,1,0:T(8,128)(2,1)S(1)}, u32[]{:S(2)}, u32[]{:S(2)}) %collective-permute-start.8) | collective-permute-done | bytes 1048608 | tf_op jit(solution)/shard_map/ppermute | solution.py:26
  258.5 17.3 %collective-permute-done.3.other_ref = bf16[16,128,256]{2,1,0:T(8,128)(2,1)S(1)} collective-permute-done((bf16[16,128,256]{2,1,0:T(8,128)(2,1)S(1)}, bf16[16,128,256]{2,1,0:T(8,128)(2,1)S(1)}, u32[]{:S(2)}, u32[]{:S(2)}) %collective-permute-start.3) | collective-permute-done | bytes 1048608 | tf_op jit(solution)/shard_map/ppermute | solution.py:26
  282.5 45.3 %collective-permute-done.14.other_ref = bf16[16,128,256]{2,1,0:T(8,128)(2,1)S(1)} collective-permute-done((bf16[16,128,256]{2,1,0:T(8,128)(2,1)S(1)}, bf16[16,128,256]{2,1,0:T(8,128)(2,1)S(1)}, u32[]{:S(2)}, u32[]{:S(2)}) %collective-permute-start.14) | collective-permute-done | bytes 1048608 | tf_op jit(solution)/shard_map/ppermute | solution.py:26
  331.6 18.6 %collective-permute-done.9.other_ref = bf16[16,128,256]{2,1,0:T(8,128)(2,1)S(1)} collective-permute-done((bf16[16,128,256]{2,1,0:T(8,128)(2,1)S(1)}, bf16[16,128,256]{2,1,0:T(8,128)(2,1)S(1)}, u32[]{:S(2)}, u32[]{:S(2)}) %collective-permute-start.9) | collective-permute-done | bytes 1048608 | tf_op jit(solution)/shard_map/ppermute | solution.py:26
  354.1 17.4 %collective-permute-done.4.other_ref = bf16[16,128,256]{2,1,0:T(8,128)(2,1)S(1)} collective-permute-done((bf16[16,128,256]{2,1,0:T(8,128)(2,1)S(1)}, bf16[16,128,256]{2,1,0:T(8,128)(2,1)S(1)}, u32[]{:S(2)}, u32[]{:S(2)}) %collective-permute-start.4) | collective-permute-done | bytes 1048608 | tf_op jit(solution)/shard_map/ppermute | solution.py:26
  (60 shorter events, 79.1 us)
Async XLA Ops:
  3.7 14.2 %collective-permute-start.15 = (bf16[4,4,32,256]{3,2,1,0:T(8,128)(2,1)S(1)}, bf16[4,4,32,256]{3,2,1,0:T(8,128)(2,1)S(1)}, u32[]{:S(2)}, u32[]{:S(2)}) collective-permute-start(bf16[4,4,32,256]{3,2,1,0:T(8,128)(2,1)S(1)} %get-tuple-element.26), channel_id=1, source_target_pairs={{0,2},{2,0},{4,6},{6,4},{1,3},{3,1},{5,7},{7,5},{8,10},{10,8},{12,... | collective-permute-start | bytes 786440 | tf_op jit(solution)/shard_map/ppermute | solution.py:26
  6.8 21.4 %collective-permute-start.16 = (bf16[4,4,32,256]{3,2,1,0:T(8,128)(2,1)S(1)}, bf16[4,4,32,256]{3,2,1,0:T(8,128)(2,1)S(1)}, u32[]{:S(2)}, u32[]{:S(2)}) collective-permute-start(bf16[4,4,32,256]{3,2,1,0:T(8,128)(2,1)S(1)} %get-tuple-element.27), channel_id=1, source_target_pairs={{0,4},{2,6},{4,0},{6,2},{1,5},{3,7},{5,1},{7,3},{8,12},{10,14},{12... | collective-permute-start | bytes 786440 | tf_op jit(solution)/shard_map/ppermute | solution.py:26
  9.4 18.8 %collective-permute-start.17 = (bf16[4,4,32,256]{3,2,1,0:T(8,128)(2,1)S(1)}, bf16[4,4,32,256]{3,2,1,0:T(8,128)(2,1)S(1)}, u32[]{:S(2)}, u32[]{:S(2)}) collective-permute-start(bf16[4,4,32,256]{3,2,1,0:T(8,128)(2,1)S(1)} %get-tuple-element.28), channel_id=1, source_target_pairs={{0,6},{2,4},{4,2},{6,0},{1,7},{3,5},{5,3},{7,1},{8,14},{10,12},{12... | collective-permute-start | bytes 786440 | tf_op jit(solution)/shard_map/ppermute | solution.py:26
  30.3 35.1 %all-to-all-start.3 = ((bf16[4,16,32,256]{3,2,1,0:T(8,128)(2,1)}), bf16[4,16,32,256]{3,2,1,0:T(8,128)(2,1)S(1)}, u32[]{:S(2)}, u32[]{:S(2)}) async-start(bf16[4,16,32,256]{3,2,1,0:T(8,128)(2,1)} %bitcast.4), calls=%async_computation.3 | async-start | bytes 2097152 | tf_op jit(solution)/shard_map/all_to_all | solution.py:228
  37.1 13.7 %collective-permute-start.10 = (bf16[4,4,32,256]{3,2,1,0:T(8,128)(2,1)S(1)}, bf16[4,4,32,256]{3,2,1,0:T(8,128)(2,1)S(1)}, u32[]{:S(2)}, u32[]{:S(2)}) collective-permute-start(bf16[4,4,32,256]{3,2,1,0:T(8,128)(2,1)S(1)} %get-tuple-element.23), channel_id=1, source_target_pairs={{0,2},{2,0},{4,6},{6,4},{1,3},{3,1},{5,7},{7,5},{8,10},{10,8},{12,... | collective-permute-start | bytes 786440 | tf_op jit(solution)/shard_map/ppermute | solution.py:26
  41.9 21.4 %collective-permute-start.11 = (bf16[4,4,32,256]{3,2,1,0:T(8,128)(2,1)S(1)}, bf16[4,4,32,256]{3,2,1,0:T(8,128)(2,1)S(1)}, u32[]{:S(2)}, u32[]{:S(2)}) collective-permute-start(bf16[4,4,32,256]{3,2,1,0:T(8,128)(2,1)S(1)} %get-tuple-element.24), channel_id=1, source_target_pairs={{0,4},{2,6},{4,0},{6,2},{1,5},{3,7},{5,1},{7,3},{8,12},{10,14},{12... | collective-permute-start | bytes 786440 | tf_op jit(solution)/shard_map/ppermute | solution.py:26
  43.0 20.3 %collective-permute-start.12 = (bf16[4,4,32,256]{3,2,1,0:T(8,128)(2,1)S(1)}, bf16[4,4,32,256]{3,2,1,0:T(8,128)(2,1)S(1)}, u32[]{:S(2)}, u32[]{:S(2)}) collective-permute-start(bf16[4,4,32,256]{3,2,1,0:T(8,128)(2,1)S(1)} %get-tuple-element.25), channel_id=1, source_target_pairs={{0,6},{2,4},{4,2},{6,0},{1,7},{3,5},{5,3},{7,1},{8,14},{10,12},{12... | collective-permute-start | bytes 786440 | tf_op jit(solution)/shard_map/ppermute | solution.py:26
  65.5 32.1 %all-to-all-start.2 = ((bf16[4,16,32,256]{3,2,1,0:T(8,128)(2,1)}), bf16[4,16,32,256]{3,2,1,0:T(8,128)(2,1)S(1)}, u32[]{:S(2)}, u32[]{:S(2)}) async-start(bf16[4,16,32,256]{3,2,1,0:T(8,128)(2,1)} %bitcast.3), calls=%async_computation.2 | async-start | bytes 2097152 | tf_op jit(solution)/shard_map/all_to_all | solution.py:228
  72.4 10.3 %collective-permute-start.5 = (bf16[4,4,32,256]{3,2,1,0:T(8,128)(2,1)S(1)}, bf16[4,4,32,256]{3,2,1,0:T(8,128)(2,1)S(1)}, u32[]{:S(2)}, u32[]{:S(2)}) collective-permute-start(bf16[4,4,32,256]{3,2,1,0:T(8,128)(2,1)S(1)} %get-tuple-element.20), channel_id=1, source_target_pairs={{0,2},{2,0},{4,6},{6,4},{1,3},{3,1},{5,7},{7,5},{8,10},{10,8},{12,... | collective-permute-start | bytes 786440 | tf_op jit(solution)/shard_map/ppermute | solution.py:26
  75.9 19.9 %collective-permute-start.6 = (bf16[4,4,32,256]{3,2,1,0:T(8,128)(2,1)S(1)}, bf16[4,4,32,256]{3,2,1,0:T(8,128)(2,1)S(1)}, u32[]{:S(2)}, u32[]{:S(2)}) collective-permute-start(bf16[4,4,32,256]{3,2,1,0:T(8,128)(2,1)S(1)} %get-tuple-element.21), channel_id=1, source_target_pairs={{0,4},{2,6},{4,0},{6,2},{1,5},{3,7},{5,1},{7,3},{8,12},{10,14},{12... | collective-permute-start | bytes 786440 | tf_op jit(solution)/shard_map/ppermute | solution.py:26
  77.0 18.8 %collective-permute-start.7 = (bf16[4,4,32,256]{3,2,1,0:T(8,128)(2,1)S(1)}, bf16[4,4,32,256]{3,2,1,0:T(8,128)(2,1)S(1)}, u32[]{:S(2)}, u32[]{:S(2)}) collective-permute-start(bf16[4,4,32,256]{3,2,1,0:T(8,128)(2,1)S(1)} %get-tuple-element.22), channel_id=1, source_target_pairs={{0,6},{2,4},{4,2},{6,0},{1,7},{3,5},{5,3},{7,1},{8,14},{10,12},{12... | collective-permute-start | bytes 786440 | tf_op jit(solution)/shard_map/ppermute | solution.py:26
  97.6 32.8 %all-to-all-start.1 = ((bf16[4,16,32,256]{3,2,1,0:T(8,128)(2,1)}), bf16[4,16,32,256]{3,2,1,0:T(8,128)(2,1)S(1)}, u32[]{:S(2)}, u32[]{:S(2)}) async-start(bf16[4,16,32,256]{3,2,1,0:T(8,128)(2,1)} %bitcast.5), calls=%async_computation.1 | async-start | bytes 2097152 | tf_op jit(solution)/shard_map/all_to_all | solution.py:228
  104.5 11.2 %collective-permute-start = (bf16[4,4,32,256]{3,2,1,0:T(8,128)(2,1)S(1)}, bf16[4,4,32,256]{3,2,1,0:T(8,128)(2,1)S(1)}, u32[]{:S(2)}, u32[]{:S(2)}) collective-permute-start(bf16[4,4,32,256]{3,2,1,0:T(8,128)(2,1)S(1)} %get-tuple-element.17), channel_id=1, source_target_pairs={{0,2},{2,0},{4,6},{6,4},{1,3},{3,1},{5,7},{7,5},{8,10},{10,8},{12,... | collective-permute-start | bytes 786440 | tf_op jit(solution)/shard_map/ppermute | solution.py:26
  107.9 20.6 %collective-permute-start.1 = (bf16[4,4,32,256]{3,2,1,0:T(8,128)(2,1)S(1)}, bf16[4,4,32,256]{3,2,1,0:T(8,128)(2,1)S(1)}, u32[]{:S(2)}, u32[]{:S(2)}) collective-permute-start(bf16[4,4,32,256]{3,2,1,0:T(8,128)(2,1)S(1)} %get-tuple-element.18), channel_id=1, source_target_pairs={{0,4},{2,6},{4,0},{6,2},{1,5},{3,7},{5,1},{7,3},{8,12},{10,14},{12... | collective-permute-start | bytes 786440 | tf_op jit(solution)/shard_map/ppermute | solution.py:26
  109.6 19.0 %collective-permute-start.2 = (bf16[4,4,32,256]{3,2,1,0:T(8,128)(2,1)S(1)}, bf16[4,4,32,256]{3,2,1,0:T(8,128)(2,1)S(1)}, u32[]{:S(2)}, u32[]{:S(2)}) collective-permute-start(bf16[4,4,32,256]{3,2,1,0:T(8,128)(2,1)S(1)} %get-tuple-element.19), channel_id=1, source_target_pairs={{0,6},{2,4},{4,2},{6,0},{1,7},{3,5},{5,3},{7,1},{8,14},{10,12},{12... | collective-permute-start | bytes 786440 | tf_op jit(solution)/shard_map/ppermute | solution.py:26
  130.3 23.3 %all-to-all-start = ((bf16[4,16,32,256]{3,2,1,0:T(8,128)(2,1)}), bf16[4,16,32,256]{3,2,1,0:T(8,128)(2,1)}, u32[]{:S(2)}, u32[]{:S(2)}) async-start(bf16[4,16,32,256]{3,2,1,0:T(8,128)(2,1)} %bitcast.6), calls=%async_computation | async-start | bytes 2097152 | tf_op jit(solution)/shard_map/all_to_all | solution.py:228
  139.5 27.8 %collective-permute-start.18 = (bf16[16,128,256]{2,1,0:T(8,128)(2,1)}, bf16[16,128,256]{2,1,0:T(8,128)(2,1)}, u32[]{:S(2)}, u32[]{:S(2)}) collective-permute-start(bf16[16,128,256]{2,1,0:T(8,128)(2,1)} %low_levels.7.own_ref), channel_id=1, source_target_pairs={{0,2},{2,0},{4,6},{6,4},{1,3},{3,1},{5,7},{7,5},{8,10},{10,8},{12,... | collective-permute-start | bytes 3145736 | tf_op jit(solution)/shard_map/ppermute | solution.py:26
  147.7 64.5 %collective-permute-start.13 = (bf16[16,128,256]{2,1,0:T(8,128)(2,1)}, bf16[16,128,256]{2,1,0:T(8,128)(2,1)}, u32[]{:S(2)}, u32[]{:S(2)}) collective-permute-start(bf16[16,128,256]{2,1,0:T(8,128)(2,1)} %low_levels.6.own_ref), channel_id=1, source_target_pairs={{0,2},{2,0},{4,6},{6,4},{1,3},{3,1},{5,7},{7,5},{8,10},{10,8},{12,... | collective-permute-start | bytes 3145736 | tf_op jit(solution)/shard_map/ppermute | solution.py:26
  151.5 104.2 %collective-permute-start.8 = (bf16[16,128,256]{2,1,0:T(8,128)(2,1)S(1)}, bf16[16,128,256]{2,1,0:T(8,128)(2,1)S(1)}, u32[]{:S(2)}, u32[]{:S(2)}) collective-permute-start(bf16[16,128,256]{2,1,0:T(8,128)(2,1)S(1)} %low_levels.5.own_ref), channel_id=1, source_target_pairs={{0,2},{2,0},{4,6},{6,4},{1,3},{3,1},{5,7},{7,5},{8,10},{10,8},{12,... | collective-permute-start | bytes 3145736 | tf_op jit(solution)/shard_map/ppermute | solution.py:26
  157.9 117.9 %collective-permute-start.3 = (bf16[16,128,256]{2,1,0:T(8,128)(2,1)S(1)}, bf16[16,128,256]{2,1,0:T(8,128)(2,1)S(1)}, u32[]{:S(2)}, u32[]{:S(2)}) collective-permute-start(bf16[16,128,256]{2,1,0:T(8,128)(2,1)S(1)} %low_levels.4.own_ref), channel_id=1, source_target_pairs={{0,2},{2,0},{4,6},{6,4},{1,3},{3,1},{5,7},{7,5},{8,10},{10,8},{12,... | collective-permute-start | bytes 3145736 | tf_op jit(solution)/shard_map/ppermute | solution.py:26
  170.2 108.4 %collective-permute-start.19 = (bf16[16,128,256]{2,1,0:T(8,128)(2,1)S(1)}, bf16[16,128,256]{2,1,0:T(8,128)(2,1)S(1)}, u32[]{:S(2)}, u32[]{:S(2)}) collective-permute-start(bf16[16,128,256]{2,1,0:T(8,128)(2,1)S(1)} %high_level.11.own_ref), channel_id=1, source_target_pairs={{0,4},{2,6},{4,0},{6,2},{1,5},{3,7},{5,1},{7,3},{8,12},{10,14},{12... | collective-permute-start | bytes 3145736 | tf_op jit(solution)/shard_map/ppermute | solution.py:26
  215.2 112.6 %collective-permute-start.14 = (bf16[16,128,256]{2,1,0:T(8,128)(2,1)S(1)}, bf16[16,128,256]{2,1,0:T(8,128)(2,1)S(1)}, u32[]{:S(2)}, u32[]{:S(2)}) collective-permute-start(bf16[16,128,256]{2,1,0:T(8,128)(2,1)S(1)} %high_level.10.own_ref), channel_id=1, source_target_pairs={{0,4},{2,6},{4,0},{6,2},{1,5},{3,7},{5,1},{7,3},{8,12},{10,14},{12... | collective-permute-start | bytes 3145736 | tf_op jit(solution)/shard_map/ppermute | solution.py:26
  258.4 91.8 %collective-permute-start.9 = (bf16[16,128,256]{2,1,0:T(8,128)(2,1)S(1)}, bf16[16,128,256]{2,1,0:T(8,128)(2,1)S(1)}, u32[]{:S(2)}, u32[]{:S(2)}) collective-permute-start(bf16[16,128,256]{2,1,0:T(8,128)(2,1)S(1)} %high_level.9.own_ref), channel_id=1, source_target_pairs={{0,4},{2,6},{4,0},{6,2},{1,5},{3,7},{5,1},{7,3},{8,12},{10,14},{12... | collective-permute-start | bytes 3145736 | tf_op jit(solution)/shard_map/ppermute | solution.py:26
  278.5 92.9 %collective-permute-start.4 = (bf16[16,128,256]{2,1,0:T(8,128)(2,1)S(1)}, bf16[16,128,256]{2,1,0:T(8,128)(2,1)S(1)}, u32[]{:S(2)}, u32[]{:S(2)}) collective-permute-start(bf16[16,128,256]{2,1,0:T(8,128)(2,1)S(1)} %high_level.8.own_ref), channel_id=1, source_target_pairs={{0,4},{2,6},{4,0},{6,2},{1,5},{3,7},{5,1},{7,3},{8,12},{10,14},{12... | collective-permute-start | bytes 3145736 | tf_op jit(solution)/shard_map/ppermute | solution.py:26
  (8 other events, 36.7 us)

commit v2 on v1

v2 whole, which is shorter than its diff:
```python
import functools

import jax
import jax.numpy as jnp
from jax import lax
from jax.experimental import pallas as pl
from jax.experimental.pallas import tpu as pltpu
from jax.sharding import PartitionSpec as P

VMEM = 48 * 1024 * 1024
COLUMN_PARTS = 2
TAKE, GATHER, LOW = "take", "gather", "low"
DIRECT, MIXED, PAIRS = "direct", "mixed", "pairs"
MODES = (DIRECT, DIRECT, DIRECT, MIXED,)
ORDER = (
    (TAKE, 0), (TAKE, 1), (LOW, 0), (TAKE, 2), (1, 0), (TAKE, 3), (LOW, 1), (1, 1), (LOW, 2),
    (GATHER, 3), (2, 0), (1, 2), (LOW, 3), (2, 1), (1, 3), (2, 2), (2, 3),
)


def run_order(count, steps, pairs):
    if count == len(MODES) and steps == 2 and pairs:
        return MODES, ORDER
    order = []
    for turn in range(count + steps + 2):
        jobs = [(TAKE, turn), (LOW, turn - 1)]
        jobs += [(step, turn - 1 - step) for step in range(1, steps + 1)]
        order += [job for job in jobs if 0 <= job[1] < count]
    return (DIRECT,) * count, order


def params(steps):
    return pltpu.CompilerParams(
        dimension_semantics=("arbitrary",) * steps, vmem_limit_bytes=VMEM
    )


def cost():
    return pl.CostEstimate(flops=0, bytes_accessed=1024, transcendentals=0)


def anywhere(values):
    return [pl.BlockSpec(memory_space=pl.ANY)] * len(values)


def swap(value, axis, mask):
    pairs = [(source, source ^ mask) for source in range(lax.axis_size(axis))]
    return lax.ppermute(value, axis, pairs)


def copy_kernel(count, level_ref, order_ref, slot_ref, *refs):
    for source, target in zip(refs[:count], refs[-count:]):
        target[...] = source[...].reshape(target.shape)


def take_rows(fourier, places, chunk, masks, order_count, after):
    slot, start, width = chunk
    _, blocks, _, rows, _ = fourier.shape
    slots_here = places[2].shape[0] // order_count
    group = blocks // lax.axis_size("level") if masks else blocks

    def source_map(mask, order, level, coordinate, slots):
        part = level[0] ^ mask if masks else 0
        return (slots[order * slots_here + slot], part, 0, 0, start // width)

    shape = (order_count, group, rows, width)
    return pl.pallas_call(
        functools.partial(copy_kernel, len(masks) or 1),
        grid_spec=pltpu.PrefetchScalarGridSpec(
            num_scalar_prefetch=3,
            grid=(order_count,),
            in_specs=[
                pl.BlockSpec((1, group, 1, rows, width), functools.partial(source_map, mask))
                for mask in masks or (0,)
            ]
            + anywhere(after),
            out_specs=[
                pl.BlockSpec((1,) + shape[1:], lambda order, *places: (order, 0, 0, 0))
                for _ in masks or (0,)
            ],
        ),
        out_shape=[jax.ShapeDtypeStruct(shape, fourier.dtype) for _ in masks or (0,)],
        compiler_params=params(1),
        cost_estimate=cost(),
        name="take_rows",
    )(*places, *[fourier] * (len(masks) or 1), *after)


def gather_kernel(sources, targets, level_ref, order_ref, slot_ref, *refs):
    for index, target in enumerate(refs[-targets:]):

        @pl.when((pl.program_id(0) == index) | (targets == 1))
        def _(target=target):
            for mask, source in enumerate(refs[:sources]):
                at = level_ref[0] ^ mask
                place = target.at[0, :, pl.ds(at, 1)] if targets == 1 else target.at[:, pl.ds(at, 1)]
                place[...] = source[...].reshape(place.shape)


def gather_blocks(fourier, received, places, chunk, order_count, apart, after):
    slot, start, width = chunk
    _, blocks, _, rows, _ = fourier.shape
    slots_here = places[2].shape[0] // order_count
    level_count = lax.axis_size("level")
    group = blocks // level_count

    def order_at(step, coordinate):
        return coordinate[0] ^ step if apart else step

    def own_map(step, level, coordinate, slots):
        order = order_at(step, coordinate)
        return (slots[order * slots_here + slot], level[0], 0, 0, start // width)

    def received_map(step, level, coordinate, slots):
        return (order_at(step, coordinate), 0, 0, 0)

    shape = (group, level_count, rows, width)
    if apart:
        out_specs = [pl.BlockSpec(shape, lambda step, *places: (0, 0, 0, 0))] * order_count
        out_shape = [jax.ShapeDtypeStruct(shape, fourier.dtype)] * order_count
    else:
        out_specs = [pl.BlockSpec((1,) + shape, lambda step, *places: (step, 0, 0, 0, 0))]
        out_shape = [jax.ShapeDtypeStruct((order_count,) + shape, fourier.dtype)]
    return pl.pallas_call(
        functools.partial(gather_kernel, level_count, len(out_shape)),
        grid_spec=pltpu.PrefetchScalarGridSpec(
            num_scalar_prefetch=3,
            grid=(order_count,),
            in_specs=[pl.BlockSpec((1, group, 1, rows, width), own_map)]
            + [pl.BlockSpec((1, group, rows, width), received_map) for _ in received]
            + anywhere(after),
            out_specs=out_specs,
        ),
        out_shape=out_shape,
        compiler_params=params(1),
        cost_estimate=cost(),
        name="gather_blocks",
    )(*places, fourier, *received, *after)


def low_kernel(source_first, count, order_ref, *refs):
    rows_refs, (self_ref, pair_ref) = refs[:count], refs[count : count + 2]
    out_ref, state = refs[-3:-1]
    rows_ref = refs[-1] if count > 1 else rows_refs[0]
    level = pl.program_id(0)
    blocks = out_ref.shape[0]
    bits = blocks.bit_length() - 1
    groups, first, second = rows_ref.shape[:3]

    def block_of(height, block):
        if height:
            return [state[block]]
        if source_first:
            at = (block % first, block // first)
        else:
            at = (block // second, block % second)
        return [rows_ref[(group,) + at] for group in range(groups)]

    for height in range(bits):

        @pl.when(level == height)
        def _(height=height):
            if height == 0 and count > 1:
                for mask, source in enumerate(rows_refs):
                    rows_ref[pl.ds(order_ref[0] ^ mask, 1)] = source[...].reshape(
                        (1,) + source.shape
                    )
            target = out_ref if height == bits - 1 else state
            for low in range(blocks):
                high = low ^ (1 << height)
                if high < low:
                    continue
                values = jnp.concatenate(block_of(height, low) + block_of(height, high), axis=0)
                factors = jnp.concatenate(
                    [
                        jnp.concatenate([self_ref[0, 0, low], pair_ref[0, 0, low]], axis=1),
                        jnp.concatenate([pair_ref[0, 0, high], self_ref[0, 0, high]], axis=1),
                    ],
                    axis=0,
                )
                mixed = jnp.dot(factors, values, preferred_element_type=jnp.float32)
                mixed = mixed.astype(target.dtype)
                target[low] = mixed[: mixed.shape[0] // 2]
                target[high] = mixed[mixed.shape[0] // 2 :]


def low_levels(rows, order, coeff_self, coeff_pair, slot, source_first, after):
    width = rows[0].shape[-1]
    blocks, cycle = coeff_self.shape[2:4]
    bits = blocks.bit_length() - 1
    factor = pl.BlockSpec((1, 1, blocks, cycle, cycle), lambda level, *order: (level, slot, 0, 0, 0))
    scratch = [pltpu.VMEM((blocks, cycle, width), rows[0].dtype)]
    scratch.append(
        pltpu.VMEM((len(rows),) + rows[0].shape if len(rows) > 1 else (8, 128), rows[0].dtype)
    )
    return pl.pallas_call(
        functools.partial(low_kernel, source_first, len(rows)),
        grid_spec=pltpu.PrefetchScalarGridSpec(
            num_scalar_prefetch=1,
            grid=(bits,),
            in_specs=[
                pl.BlockSpec(value.shape, lambda level, *order, rank=value.ndim: (0,) * rank)
                for value in rows
            ]
            + [factor, factor]
            + anywhere(after),
            out_specs=pl.BlockSpec((blocks, cycle, width), lambda level, *order: (0, 0, 0)),
            scratch_shapes=scratch,
        ),
        out_shape=jax.ShapeDtypeStruct((blocks, cycle, width), rows[0].dtype),
        compiler_params=params(1),
        cost_estimate=cost(),
        name="low_levels",
    )(order, *rows, coeff_self, coeff_pair, *after)


def high_kernel(own_ref, other_ref, self_ref, pair_ref, *refs):
    target = refs[-1]
    lead = len(target.shape) - 3
    for block in range(own_ref.shape[0]):
        factors = jnp.concatenate([self_ref[0, 0, block], pair_ref[0, 0, block]], axis=1)
        values = jnp.concatenate([own_ref[block], other_ref[block]], axis=0)
        mixed = jnp.dot(factors, values, preferred_element_type=jnp.float32)
        target[(0,) * lead + (block,)] = mixed.astype(target.dtype)


def high_level(own, other, coeff_self, coeff_pair, level, slot, after, final=None):
    blocks, cycle, width = own.shape
    step = min(4, blocks)
    value = pl.BlockSpec((step, cycle, width), lambda at: (at, 0, 0))
    factor = pl.BlockSpec((1, 1, step, cycle, cycle), lambda at: (level, slot, at, 0, 0))
    operands = [own, other, coeff_self, coeff_pair]
    in_specs = [value, value, factor, factor]
    aliases = {}
    if final is None:
        out_spec, out_shape = value, jax.ShapeDtypeStruct(own.shape, own.dtype)
    else:
        result, shape, part = final
        out_spec = pl.BlockSpec((1, step, cycle, width), lambda at: (slot, at, 0, part))
        out_shape = jax.ShapeDtypeStruct(shape, own.dtype)
        if result is not None:
            operands.append(result)
            in_specs += anywhere([result])
            aliases = {4: 0}
    return pl.pallas_call(
        high_kernel,
        grid=(blocks // step,),
        in_specs=in_specs + anywhere(after),
        out_specs=out_spec,
        out_shape=out_shape,
        input_output_aliases=aliases,
        compiler_params=params(1),
        cost_estimate=cost(),
        name="high_level",
    )(*operands, *after)


def local(fourier, order_slot, coeff_self, coeff_pair):
    order_count = lax.axis_size("order")
    level_count = lax.axis_size("level")
    levels, orders_here, blocks_here, cycle_rows, _ = coeff_self.shape
    rows_here, columns = fourier.shape[3:]
    local_bits = blocks_here.bit_length() - 1
    steps = levels - local_bits
    group = blocks_here // level_count
    width = columns // COLUMN_PARTS
    chunks = [
        (slot, part * width, width) for slot in range(orders_here) for part in range(COLUMN_PARTS)
    ]
    modes, order = run_order(len(chunks), steps, rows_here % 16 == 0)

    def place(axis):
        return lax.axis_index(axis).astype(jnp.int32).reshape(1)

    places = (place("level"), place("order"), order_slot)
    level_masks = tuple(range(1, level_count))
    shape = (orders_here, blocks_here, cycle_rows, columns)
    outgoing, rows, state = {}, {}, {}
    result = None
    last = []
    for kind, at in order:
        chunk, mode = chunks[at], modes[at]
        slot, start, _ = chunk
        if kind == TAKE:
            masks = () if mode == DIRECT else level_masks
            outgoing[at] = take_rows(fourier, places, chunk, masks, order_count, last)
            last = [outgoing[at][0]]
            if mode == DIRECT:
                value = outgoing[at][0].reshape(
                    order_count * level_count, group, rows_here, width
                )
                value = lax.all_to_all(
                    value, ("order", "level"), split_axis=0, concat_axis=0, tiled=True
                )
                value = value.reshape(order_count, level_count, group, rows_here, width)
                if rows_here % 16:
                    value = value.transpose(1, 2, 0, 3, 4).reshape(
                        1, level_count, group, cycle_rows, width
                    )
                rows[at] = [value]
        elif kind == GATHER:
            received = [swap(value, "level", mask) for value, mask in zip(outgoing[at], level_masks)]
            gathered = gather_blocks(
                fourier, received, places, chunk, order_count, mode == PAIRS, last
            )
            last = [gathered[0]]
            if mode == PAIRS:
                rows[at] = [gathered[0]] + [
                    swap(value, "order", mask) for mask, value in enumerate(gathered) if mask
                ]
            else:
                rows[at] = [
                    lax.all_to_all(gathered[0], "order", split_axis=0, concat_axis=0, tiled=True)
                ]
        elif kind == LOW:
            state[at] = low_levels(
                rows[at], places[1], coeff_self, coeff_pair, slot, mode == DIRECT, last
            )
            last = [state[at]]
        else:
            other = swap(state[at], "level", 1 << (kind - 1))
            final = None
            if kind == steps:
                final = (result, shape, start // width)
                last = [value for value in last if value is not result]
            state[at] = high_level(
                state[at], other, coeff_self, coeff_pair, local_bits + kind - 1, slot, last, final
            )
            last = [state[at]]
            if kind == steps:
                result = state[at]
    return result


def solution(mesh):
    placed = (
        P("freq", None, "level", "order", None),
        P(),
        P(None, "order", "level", None, None),
        P(None, "order", "level", None, None),
    )
    return jax.shard_map(
        local,
        mesh=mesh,
        in_specs=placed,
        out_specs=P(("freq", "order"), "level", None, None),
        check_vma=False,
    )
```

time: 377 us -> 314 us (0.83)
  waiting for transfers between devices: 257 us -> 213 us
  starting transfers between devices: 52.4 us -> 35.6 us
  local copies, waits for them, and re-layouts: 11.3 us -> 5.06 us
  Pallas kernels: 54 us -> 58.7 us
    ppermute x20 -> x11, waiting for transfers between devices: 257 us -> 172 us  [swap(): return lax.ppermute(value, axis, pairs)]
    all_to_all x4, waiting for transfers between devices: 0.01 us -> 40.8 us  [the longest x3 40.8 us: local(): lax.all_to_all(value, ('order', 'level'), split_axis=0, concat_axis=0, ti...]
    ppermute x20 -> x11, starting transfers between devices: 36.6 us -> 15.7 us  [swap(): return lax.ppermute(value, axis, pairs)]
    unnamed x16, local copies, waits for them, and re-layouts: 11.3 us -> 5.06 us
    pallas_call x20 -> x17, Pallas kernels: 54 us -> 58.7 us  [the longest x8 26.9 us: high_level(): pl.pallas_call(high_kernel, grid=(blocks // step,), in_specs=in_specs + a...]
    all_to_all x4, starting transfers between devices: 15.8 us -> 19.9 us  [the longest x3 15.6 us: local(): lax.all_to_all(value, ('order', 'level'), split_axis=0, concat_axis=0, ti...]
  transfers between devices with their start and end apart: 24 -> 15, of which waited for: 15 -> 11; matrix products, arithmetic and copies ran while one was open for 0% -> 0% of each run, Pallas kernels for 13% -> 17%
where the time goes in v2:
time: 314 us; the launch traced here: 312 us
  waiting for transfers between devices  213 us (68%)
  Pallas kernels  58.7 us (19%)
  starting transfers between devices  35.6 us (11%)
  local copies, waits for them, and re-layouts  5.06 us (2%)
    ppermute x11, waiting for transfers between devices, swap(): return lax.ppermute(value, axis, pairs)  172 us
    all_to_all x3, waiting for transfers between devices, local(): lax.all_to_all(value, ('order', 'level'), split_axis=0, concat_axis=0, ti...  40.8 us
    pallas_call x8, Pallas kernels, high_level(): pl.pallas_call(high_kernel, grid=(blocks // step,), in_specs=in_specs + a...  26.9 us
    pallas_call x4, Pallas kernels, low_levels(): pl.pallas_call(functools.partial(low_kernel, source_first, len(rows)), gr...  15.9 us
    ppermute x11, starting transfers between devices, swap(): return lax.ppermute(value, axis, pairs)  15.7 us
    all_to_all x3, starting transfers between devices, local(): lax.all_to_all(value, ('order', 'level'), split_axis=0, concat_axis=0, ti...  15.6 us
    pallas_call x4, Pallas kernels, take_rows(): pl.pallas_call(functools.partial(copy_kernel, len(masks) or 1), grid_spec...  12.1 us
  transfers between devices with their start and end apart: 15, of which 11 were waited for; matrix products, arithmetic and copies ran while one was open for 0% of the time, Pallas kernels for 17%

profile of v2, /device:TPU:0, one launch (start us, length us, event | category | flops | bytes accessed | tf_op | source)
XLA Modules:
  0.0 312.2 jit_solution(14310403726575300559)
XLA Ops:
  5.0 8.3 %all-to-all-start = ((bf16[16,4,32,256]{3,2,1,0:T(8,128)(2,1)}), bf16[16,4,32,256]{3,2,1,0:T(8,128)(2,1)S(1)}, u32[]{:S(2)}, u32[]{:S(2)}) async-start(bf16[16,4,32,256]{3,2,1,0:T(8,128)(2,1)} %bitcast.2), calls=%async_computation | async-start | bytes 2097152 | tf_op jit(solution)/shard_map/all_to_all | solution.py:292
  13.3 3.9 %take_rows.5.refs_3_ = bf16[4,16,32,256]{3,2,1,0:T(8,128)(2,1)} custom-call(s32[1]{0:T(128)} %bitcast.1.level_ref, s32[1]{0:T(128)} %bitcast.order_ref, s32[8]{0:T(128)S(1)} %copy-done.7, bf16[8,16,1,32,512]{4,3,2,1,0:T(8,128)(2,1)} %refs_0_.9, bf16[4,16,32,256]{3,2,1,0:T(8,128)(2,1)} %take_rows.4.refs_1_), custom_call_target="tpu_custom_call" | custom-call | bytes 1024 | tf_op jit(solution)/shard_map/take_rows/pallas_call | solution.py:67
  17.3 23.5 %all-to-all-done = bf16[16,4,32,256]{3,2,1,0:T(8,128)(2,1)S(1)} async-done(((bf16[16,4,32,256]{3,2,1,0:T(8,128)(2,1)}), bf16[16,4,32,256]{3,2,1,0:T(8,128)(2,1)S(1)}, u32[]{:S(2)}, u32[]{:S(2)}) %all-to-all-start) | async-done | bytes 1048608 | tf_op jit(solution)/shard_map/all_to_all | solution.py:292
  44.5 3.9 %low_levels.4.refs_1_.own_ref = bf16[16,128,256]{2,1,0:T(8,128)(2,1)S(1)} custom-call(s32[1]{0:T(128)} %bitcast.order_ref, bf16[4,4,4,32,256]{4,3,2,1,0:T(8,128)(2,1)S(1)} %bitcast.10, bf16[6,2,16,128,128]{4,3,2,1,0:T(8,128)(2,1)} %self_ref.15, bf16[6,2,16,128,128]{4,3,2,1,0:T(8,128)(2,1)} %pair_ref.15, bf16[4,16,32,256]{3,2,1,0:T(8,128)(2,1)} %take_rows.5.refs_3_), custom_call_target="tpu_custom_call" | custom-call | bytes 1024 | tf_op jit(solution)/shard_map/low_levels/pallas_call | solution.py:196
  50.2 3.9 %take_rows.6.refs_0_ = bf16[4,16,32,256]{3,2,1,0:T(8,128)(2,1)} custom-call(s32[1]{0:T(128)} %bitcast.1.level_ref, s32[1]{0:T(128)} %bitcast.order_ref, s32[8]{0:T(128)S(1)} %copy-done.7, bf16[8,16,1,32,512]{4,3,2,1,0:T(8,128)(2,1)} %refs_0_.9, bf16[16,128,256]{2,1,0:T(8,128)(2,1)S(1)} %low_levels.4.refs_1_.own_ref), custom_call_target="tpu_custom_call" | custom-call | bytes 1024 | tf_op jit(solution)/shard_map/take_rows/pallas_call | solution.py:67
  54.1 17.2 %all-to-all-done.2 = bf16[16,4,32,256]{3,2,1,0:T(8,128)(2,1)S(1)} async-done(((bf16[16,4,32,256]{3,2,1,0:T(8,128)(2,1)}), bf16[16,4,32,256]{3,2,1,0:T(8,128)(2,1)S(1)}, u32[]{:S(2)}, u32[]{:S(2)}) %all-to-all-start.2) | async-done | bytes 1048608 | tf_op jit(solution)/shard_map/all_to_all | solution.py:292
  75.1 17.1 %collective-permute-done.other_ref = bf16[16,128,256]{2,1,0:T(8,128)(2,1)} collective-permute-done((bf16[16,128,256]{2,1,0:T(8,128)(2,1)S(1)}, bf16[16,128,256]{2,1,0:T(8,128)(2,1)}, u32[]{:S(2)}, u32[]{:S(2)}) %collective-permute-start) | collective-permute-done | bytes 1048608 | tf_op jit(solution)/shard_map/ppermute | solution.py:48
  97.1 3.9 %low_levels.5.own_ref.refs_0_ = bf16[16,128,256]{2,1,0:T(8,128)(2,1)S(1)} custom-call(s32[1]{0:T(128)} %bitcast.order_ref, bf16[4,4,4,32,256]{4,3,2,1,0:T(8,128)(2,1)S(1)} %bitcast.9, bf16[6,2,16,128,128]{4,3,2,1,0:T(8,128)(2,1)} %self_ref.15, bf16[6,2,16,128,128]{4,3,2,1,0:T(8,128)(2,1)} %pair_ref.15, bf16[4,4,32,256]{3,2,1,0:T(8,128)(2,1)S(1)} %get-tuple-element.8.refs_3_), custom_call_target="tpu_custom_call" | custom-call | bytes 1024 | tf_op jit(solution)/shard_map/low_levels/pallas_call | solution.py:196
  103.1 4.9 %collective-permute-start.6 = (bf16[16,128,256]{2,1,0:T(8,128)(2,1)S(1)}, bf16[16,128,256]{2,1,0:T(8,128)(2,1)}, u32[]{:S(2)}, u32[]{:S(2)}) collective-permute-start(bf16[16,128,256]{2,1,0:T(8,128)(2,1)S(1)} %high_level.8.refs_3_.own_ref), channel_id=1, source_target_pairs={{0,4},{2,6},{4,0},{6,2},{1,5},{3,7},{5,1},{7,3},{8,12},{10,14},{12... | collective-permute-start | bytes 3145736 | tf_op jit(solution)/shard_map/ppermute | solution.py:48
  108.1 4.3 %collective-permute-start.3 = (bf16[4,4,32,256]{3,2,1,0:T(8,128)(2,1)}, bf16[4,4,32,256]{3,2,1,0:T(8,128)(2,1)}, u32[]{:S(2)}, u32[]{:S(2)}) collective-permute-start(bf16[4,4,32,256]{3,2,1,0:T(8,128)(2,1)} %get-tuple-element.10), channel_id=1, source_target_pairs={{0,6},{2,4},{4,2},{6,0},{1,7},{3,5},{5,3},{7,1},{8,14},{10,12},{12... | collective-permute-start | bytes 786440 | tf_op jit(solution)/shard_map/ppermute | solution.py:48
  112.4 39.0 %collective-permute-done.4.other_ref = bf16[16,128,256]{2,1,0:T(8,128)(2,1)S(1)} collective-permute-done((bf16[16,128,256]{2,1,0:T(8,128)(2,1)S(1)}, bf16[16,128,256]{2,1,0:T(8,128)(2,1)S(1)}, u32[]{:S(2)}, u32[]{:S(2)}) %collective-permute-start.4) | collective-permute-done | bytes 1048608 | tf_op jit(solution)/shard_map/ppermute | solution.py:48
  156.3 3.9 %low_levels.6.refs_4_.own_ref = bf16[16,128,256]{2,1,0:T(8,128)(2,1)S(1)} custom-call(s32[1]{0:T(128)} %bitcast.order_ref, bf16[4,4,4,32,256]{4,3,2,1,0:T(8,128)(2,1)S(1)} %bitcast.8, bf16[6,2,16,128,128]{4,3,2,1,0:T(8,128)(2,1)} %self_ref.15, bf16[6,2,16,128,128]{4,3,2,1,0:T(8,128)(2,1)} %pair_ref.15, bf16[16,128,256]{2,1,0:T(8,128)(2,1)S(1)} %high_level.9.refs_3_.own_ref), custom_call_target="tpu_custom_call" | custom-call | bytes 1024 | tf_op jit(solution)/shard_map/low_levels/pallas_call | solution.py:196
  160.3 6.5 %collective-permute-done.2.refs_2_ = bf16[4,4,32,256]{3,2,1,0:T(8,128)(2,1)} collective-permute-done((bf16[4,4,32,256]{3,2,1,0:T(8,128)(2,1)}, bf16[4,4,32,256]{3,2,1,0:T(8,128)(2,1)}, u32[]{:S(2)}, u32[]{:S(2)}) %collective-permute-start.2) | collective-permute-done | bytes 262176 | tf_op jit(solution)/shard_map/ppermute | solution.py:48
  166.8 4.2 %collective-permute-done.3.refs_3_ = bf16[4,4,32,256]{3,2,1,0:T(8,128)(2,1)} collective-permute-done((bf16[4,4,32,256]{3,2,1,0:T(8,128)(2,1)}, bf16[4,4,32,256]{3,2,1,0:T(8,128)(2,1)}, u32[]{:S(2)}, u32[]{:S(2)}) %collective-permute-start.3) | collective-permute-done | bytes 262176 | tf_op jit(solution)/shard_map/ppermute | solution.py:48
  171.0 3.9 %gather_blocks.1.refs_0_ = bf16[4,4,4,32,256]{4,3,2,1,0:T(8,128)(2,1)} custom-call(s32[1]{0:T(128)} %bitcast.1.level_ref, s32[1]{0:T(128)} %bitcast.order_ref, s32[8]{0:T(128)S(1)} %copy-done.7, bf16[8,16,1,32,512]{4,3,2,1,0:T(8,128)(2,1)} %refs_0_.9, bf16[4,4,32,256]{3,2,1,0:T(8,128)(2,1)} %collective-permute-done.1.refs_1_, ...), custom_call_target="tpu_custom_call" | custom-call | bytes 1024 | tf_op jit(solution)/shard_map/gather_blocks/pallas_call | solution.py:124
  174.9 4.3 %all-to-all-start.3 = ((bf16[4,4,4,32,256]{4,3,2,1,0:T(8,128)(2,1)}), bf16[4,4,4,32,256]{4,3,2,1,0:T(8,128)(2,1)}, u32[]{:S(2)}, u32[]{:S(2)}) async-start(bf16[4,4,4,32,256]{4,3,2,1,0:T(8,128)(2,1)} %gather_blocks.1.refs_0_), calls=%async_computation.3 | async-start | bytes 2097152 | tf_op jit(solution)/shard_map/all_to_all | solution.py:313
  180.1 4.0 %high_level.10.refs_0_ = bf16[2,16,128,512]{3,2,1,0:T(8,128)(2,1)} custom-call(bf16[16,128,256]{2,1,0:T(8,128)(2,1)S(1)} %high_level.8.refs_3_.own_ref, bf16[16,128,256]{2,1,0:T(8,128)(2,1)} %collective-permute-done.6.other_ref, bf16[6,2,16,128,128]{4,3,2,1,0:T(8,128)(2,1)} %self_ref.15, bf16[6,2,16,128,128]{4,3,2,1,0:T(8,128)(2,1)} %pair_ref.15, ...), custom_call_target="tpu_custom_call" | custom-call | bytes 1024 | tf_op jit(solution)/shard_map/high_level/pallas_call | solution.py:245
  184.1 20.5 %collective-permute-done.5.other_ref = bf16[16,128,256]{2,1,0:T(8,128)(2,1)} collective-permute-done((bf16[16,128,256]{2,1,0:T(8,128)(2,1)S(1)}, bf16[16,128,256]{2,1,0:T(8,128)(2,1)}, u32[]{:S(2)}, u32[]{:S(2)}) %collective-permute-start.5) | collective-permute-done | bytes 1048608 | tf_op jit(solution)/shard_map/ppermute | solution.py:48
  207.5 4.2 %low_levels.7.refs_1_.own_ref = bf16[16,128,256]{2,1,0:T(8,128)(2,1)S(1)} custom-call(s32[1]{0:T(128)} %bitcast.order_ref, bf16[4,4,4,32,256]{4,3,2,1,0:T(8,128)(2,1)} %all-to-all-done.3.refs_0_, bf16[6,2,16,128,128]{4,3,2,1,0:T(8,128)(2,1)} %self_ref.15, bf16[6,2,16,128,128]{4,3,2,1,0:T(8,128)(2,1)} %pair_ref.15, ...), custom_call_target="tpu_custom_call" | custom-call | bytes 1024 | tf_op jit(solution)/shard_map/low_levels/pallas_call | solution.py:196
  212.3 9.5 %collective-permute-done.8.other_ref = bf16[16,128,256]{2,1,0:T(8,128)(2,1)} collective-permute-done((bf16[16,128,256]{2,1,0:T(8,128)(2,1)S(1)}, bf16[16,128,256]{2,1,0:T(8,128)(2,1)}, u32[]{:S(2)}, u32[]{:S(2)}) %collective-permute-start.8) | collective-permute-done | bytes 1048608 | tf_op jit(solution)/shard_map/ppermute | solution.py:48
  221.9 4.0 %high_level.12.refs_0_ = bf16[2,16,128,512]{3,2,1,0:T(8,128)(2,1)} custom-call(bf16[16,128,256]{2,1,0:T(8,128)(2,1)S(1)} %high_level.9.refs_3_.own_ref, bf16[16,128,256]{2,1,0:T(8,128)(2,1)} %collective-permute-done.8.other_ref, bf16[6,2,16,128,128]{4,3,2,1,0:T(8,128)(2,1)} %self_ref.15, ...), custom_call_target="tpu_custom_call", output_to_operand_aliasing={{}: (4, {})} | custom-call | bytes 1024 | tf_op jit(solution)/shard_map/high_level/pallas_call | solution.py:245
  225.9 31.2 %collective-permute-done.7.other_ref = bf16[16,128,256]{2,1,0:T(8,128)(2,1)S(1)} collective-permute-done((bf16[16,128,256]{2,1,0:T(8,128)(2,1)S(1)}, bf16[16,128,256]{2,1,0:T(8,128)(2,1)S(1)}, u32[]{:S(2)}, u32[]{:S(2)}) %collective-permute-start.7) | collective-permute-done | bytes 1048608 | tf_op jit(solution)/shard_map/ppermute | solution.py:48
  262.7 3.8 %high_level.14.refs_0_ = bf16[2,16,128,512]{3,2,1,0:T(8,128)(2,1)} custom-call(bf16[16,128,256]{2,1,0:T(8,128)(2,1)S(1)} %high_level.11.refs_3_.own_ref, bf16[16,128,256]{2,1,0:T(8,128)(2,1)S(1)} %collective-permute-done.10.other_ref, bf16[6,2,16,128,128]{4,3,2,1,0:T(8,128)(2,1)} %self_ref.15, ...), custom_call_target="tpu_custom_call", output_to_operand_aliasing={{}: (4, {})} | custom-call | bytes 1024 | tf_op jit(solution)/shard_map/high_level/pallas_call | solution.py:245
  266.6 41.7 %collective-permute-done.9.other_ref = bf16[16,128,256]{2,1,0:T(8,128)(2,1)S(1)} collective-permute-done((bf16[16,128,256]{2,1,0:T(8,128)(2,1)S(1)}, bf16[16,128,256]{2,1,0:T(8,128)(2,1)S(1)}, u32[]{:S(2)}, u32[]{:S(2)}) %collective-permute-start.9) | collective-permute-done | bytes 1048608 | tf_op jit(solution)/shard_map/ppermute | solution.py:48
  (39 shorter events, 40.1 us)
Async XLA Ops:
  0.0 13.3 %copy-start.7 = (s32[8]{0:T(128)S(1)}, s32[8]{0:T(128)}, u32[]{:S(2)}) copy-start(s32[8]{0:T(128)} %slot_ref.9) | copy-start | bytes 100
  0.0 2.2 copy-start
  2.2 0.7 copy-start.6
  5.0 35.8 %all-to-all-start = ((bf16[16,4,32,256]{3,2,1,0:T(8,128)(2,1)}), bf16[16,4,32,256]{3,2,1,0:T(8,128)(2,1)S(1)}, u32[]{:S(2)}, u32[]{:S(2)}) async-start(bf16[16,4,32,256]{3,2,1,0:T(8,128)(2,1)} %bitcast.2), calls=%async_computation | async-start | bytes 2097152 | tf_op jit(solution)/shard_map/all_to_all | solution.py:292
  40.8 30.6 %all-to-all-start.2 = ((bf16[16,4,32,256]{3,2,1,0:T(8,128)(2,1)}), bf16[16,4,32,256]{3,2,1,0:T(8,128)(2,1)S(1)}, u32[]{:S(2)}, u32[]{:S(2)}) async-start(bf16[16,4,32,256]{3,2,1,0:T(8,128)(2,1)} %bitcast.6), calls=%async_computation.2 | async-start | bytes 2097152 | tf_op jit(solution)/shard_map/all_to_all | solution.py:292
  48.4 43.8 %collective-permute-start = (bf16[16,128,256]{2,1,0:T(8,128)(2,1)S(1)}, bf16[16,128,256]{2,1,0:T(8,128)(2,1)}, u32[]{:S(2)}, u32[]{:S(2)}) collective-permute-start(bf16[16,128,256]{2,1,0:T(8,128)(2,1)S(1)} %low_levels.4.refs_1_.own_ref), channel_id=1, source_target_pairs={{0,2},{2,0},{4,6},{6,4},{1,3},{3,1},{5,7},{7,5},{8,10},{10,8},{12,... | collective-permute-start | bytes 3145736 | tf_op jit(solution)/shard_map/ppermute | solution.py:48
  71.4 3.7 %copy-start.4 = (bf16[16,4,32,256]{3,2,1,0:T(8,128)(2,1)}, bf16[16,4,32,256]{3,2,1,0:T(8,128)(2,1)S(1)}, u32[]{:S(2)}) copy-start(bf16[16,4,32,256]{3,2,1,0:T(8,128)(2,1)S(1)} %all-to-all-done.2) | copy-start | bytes 3145732
  71.4 82.7 %all-to-all-start.1 = ((bf16[16,4,32,256]{3,2,1,0:T(8,128)(2,1)}), bf16[16,4,32,256]{3,2,1,0:T(8,128)(2,1)S(1)}, u32[]{:S(2)}, u32[]{:S(2)}) async-start(bf16[16,4,32,256]{3,2,1,0:T(8,128)(2,1)} %bitcast.4), calls=%async_computation.1 | async-start | bytes 2097152 | tf_op jit(solution)/shard_map/all_to_all | solution.py:292
  75.1 20.0 %copy-start.1 = (bf16[8,16,1,32,512]{4,3,2,1,0:T(8,128)(2,1)S(1)}, bf16[8,16,1,32,512]{4,3,2,1,0:T(8,128)(2,1)}, u32[]{:S(2)}) copy-start(bf16[8,16,1,32,512]{4,3,2,1,0:T(8,128)(2,1)} %refs_0_.9) | copy-start | bytes 12582916
  95.1 2.1 copy-start.5
  101.0 50.4 %collective-permute-start.4 = (bf16[16,128,256]{2,1,0:T(8,128)(2,1)S(1)}, bf16[16,128,256]{2,1,0:T(8,128)(2,1)S(1)}, u32[]{:S(2)}, u32[]{:S(2)}) collective-permute-start(bf16[16,128,256]{2,1,0:T(8,128)(2,1)S(1)} %low_levels.5.own_ref.refs_0_), channel_id=1, source_target_pairs={{0,2},{2,0},{4,6},{6,4},{1,3},{3,1},{5,7},{7,5},{8,10},{10,8},{12,... | collective-permute-start | bytes 3145736 | tf_op jit(solution)/shard_map/ppermute | solution.py:48
  101.1 59.2 %collective-permute-start.1 = (bf16[4,4,32,256]{3,2,1,0:T(8,128)(2,1)S(1)}, bf16[4,4,32,256]{3,2,1,0:T(8,128)(2,1)}, u32[]{:S(2)}, u32[]{:S(2)}) collective-permute-start(bf16[4,4,32,256]{3,2,1,0:T(8,128)(2,1)S(1)} %get-tuple-element.8.refs_3_), channel_id=1, source_target_pairs={{0,2},{2,0},{4,6},{6,4},{1,3},{3,1},{5,7},{7,5},{8,10},{10,8},{12,... | collective-permute-start | bytes 786440 | tf_op jit(solution)/shard_map/ppermute | solution.py:48
  103.1 76.9 %collective-permute-start.6 = (bf16[16,128,256]{2,1,0:T(8,128)(2,1)S(1)}, bf16[16,128,256]{2,1,0:T(8,128)(2,1)}, u32[]{:S(2)}, u32[]{:S(2)}) collective-permute-start(bf16[16,128,256]{2,1,0:T(8,128)(2,1)S(1)} %high_level.8.refs_3_.own_ref), channel_id=1, source_target_pairs={{0,4},{2,6},{4,0},{6,2},{1,5},{3,7},{5,1},{7,3},{8,12},{10,14},{12... | collective-permute-start | bytes 3145736 | tf_op jit(solution)/shard_map/ppermute | solution.py:48
  108.0 58.7 %collective-permute-start.2 = (bf16[4,4,32,256]{3,2,1,0:T(8,128)(2,1)}, bf16[4,4,32,256]{3,2,1,0:T(8,128)(2,1)}, u32[]{:S(2)}, u32[]{:S(2)}) collective-permute-start(bf16[4,4,32,256]{3,2,1,0:T(8,128)(2,1)} %get-tuple-element.9), channel_id=1, source_target_pairs={{0,4},{2,6},{4,0},{6,2},{1,5},{3,7},{5,1},{7,3},{8,12},{10,14},{12... | collective-permute-start | bytes 786440 | tf_op jit(solution)/shard_map/ppermute | solution.py:48
  108.1 62.9 %collective-permute-start.3 = (bf16[4,4,32,256]{3,2,1,0:T(8,128)(2,1)}, bf16[4,4,32,256]{3,2,1,0:T(8,128)(2,1)}, u32[]{:S(2)}, u32[]{:S(2)}) collective-permute-start(bf16[4,4,32,256]{3,2,1,0:T(8,128)(2,1)} %get-tuple-element.10), channel_id=1, source_target_pairs={{0,6},{2,4},{4,2},{6,0},{1,7},{3,5},{5,3},{7,1},{8,14},{10,12},{12... | collective-permute-start | bytes 786440 | tf_op jit(solution)/shard_map/ppermute | solution.py:48
  154.1 1.0 copy-start.2
  155.1 1.2 copy-start.3
  160.2 44.4 %collective-permute-start.5 = (bf16[16,128,256]{2,1,0:T(8,128)(2,1)S(1)}, bf16[16,128,256]{2,1,0:T(8,128)(2,1)}, u32[]{:S(2)}, u32[]{:S(2)}) collective-permute-start(bf16[16,128,256]{2,1,0:T(8,128)(2,1)S(1)} %low_levels.6.refs_4_.own_ref), channel_id=1, source_target_pairs={{0,2},{2,0},{4,6},{6,4},{1,3},{3,1},{5,7},{7,5},{8,10},{10,8},{12,... | collective-permute-start | bytes 3145736 | tf_op jit(solution)/shard_map/ppermute | solution.py:48
  174.9 32.6 %all-to-all-start.3 = ((bf16[4,4,4,32,256]{4,3,2,1,0:T(8,128)(2,1)}), bf16[4,4,4,32,256]{4,3,2,1,0:T(8,128)(2,1)}, u32[]{:S(2)}, u32[]{:S(2)}) async-start(bf16[4,4,4,32,256]{4,3,2,1,0:T(8,128)(2,1)} %gather_blocks.1.refs_0_), calls=%async_computation.3 | async-start | bytes 2097152 | tf_op jit(solution)/shard_map/all_to_all | solution.py:313
  179.1 42.8 %collective-permute-start.8 = (bf16[16,128,256]{2,1,0:T(8,128)(2,1)S(1)}, bf16[16,128,256]{2,1,0:T(8,128)(2,1)}, u32[]{:S(2)}, u32[]{:S(2)}) collective-permute-start(bf16[16,128,256]{2,1,0:T(8,128)(2,1)S(1)} %high_level.9.refs_3_.own_ref), channel_id=1, source_target_pairs={{0,4},{2,6},{4,0},{6,2},{1,5},{3,7},{5,1},{7,3},{8,12},{10,14},{12... | collective-permute-start | bytes 3145736 | tf_op jit(solution)/shard_map/ppermute | solution.py:48
  211.8 45.3 %collective-permute-start.7 = (bf16[16,128,256]{2,1,0:T(8,128)(2,1)S(1)}, bf16[16,128,256]{2,1,0:T(8,128)(2,1)S(1)}, u32[]{:S(2)}, u32[]{:S(2)}) collective-permute-start(bf16[16,128,256]{2,1,0:T(8,128)(2,1)S(1)} %low_levels.7.refs_1_.own_ref), channel_id=1, source_target_pairs={{0,2},{2,0},{4,6},{6,4},{1,3},{3,1},{5,7},{7,5},{8,10},{10,8},{12,... | collective-permute-start | bytes 3145736 | tf_op jit(solution)/shard_map/ppermute | solution.py:48
  211.8 50.9 %collective-permute-start.10 = (bf16[16,128,256]{2,1,0:T(8,128)(2,1)S(1)}, bf16[16,128,256]{2,1,0:T(8,128)(2,1)S(1)}, u32[]{:S(2)}, u32[]{:S(2)}) collective-permute-start(bf16[16,128,256]{2,1,0:T(8,128)(2,1)S(1)} %high_level.11.refs_3_.own_ref), channel_id=1, source_target_pairs={{0,4},{2,6},{4,0},{6,2},{1,5},{3,7},{5,1},{7,3},{8,12},{10,14},{12... | collective-permute-start | bytes 3145736 | tf_op jit(solution)/shard_map/ppermute | solution.py:48
  259.8 48.5 %collective-permute-start.9 = (bf16[16,128,256]{2,1,0:T(8,128)(2,1)S(1)}, bf16[16,128,256]{2,1,0:T(8,128)(2,1)S(1)}, u32[]{:S(2)}, u32[]{:S(2)}) collective-permute-start(bf16[16,128,256]{2,1,0:T(8,128)(2,1)S(1)} %high_level.13.refs_1_.own_ref), channel_id=1, source_target_pairs={{0,4},{2,6},{4,0},{6,2},{1,5},{3,7},{5,1},{7,3},{8,12},{10,14},{12... | collective-permute-start | bytes 3145736 | tf_op jit(solution)/shard_map/ppermute | solution.py:48

commit v3 on v2

--- a/solution.py
+++ b/solution.py
@@ -8,25 +8,28 @@
 from jax.sharding import PartitionSpec as P
 
 VMEM = 48 * 1024 * 1024
-COLUMN_PARTS = 2
 TAKE, GATHER, LOW = "take", "gather", "low"
 DIRECT, MIXED, PAIRS = "direct", "mixed", "pairs"
-MODES = (DIRECT, DIRECT, DIRECT, MIXED,)
+CHUNKS = ((0, 0, 2), (0, 2, 2), (1, 0, 2), (1, 2, 2))
+PIECES = (1, 1, 1, 1,)
+MODES = (DIRECT, DIRECT, DIRECT, MIXED)
 ORDER = (
     (TAKE, 0), (TAKE, 1), (LOW, 0), (TAKE, 2), (1, 0), (TAKE, 3), (LOW, 1), (1, 1), (LOW, 2),
     (GATHER, 3), (2, 0), (1, 2), (LOW, 3), (2, 1), (1, 3), (2, 2), (2, 3),
 )
 
 
-def run_order(count, steps, pairs):
-    if count == len(MODES) and steps == 2 and pairs:
-        return MODES, ORDER
+def plan(slots, steps, pairs):
+    if steps == 2 and pairs and slots == 1 + max(slot for slot, _, _ in CHUNKS):
+        return CHUNKS, PIECES, MODES, ORDER
+    chunks = [(slot, part, 2) for slot in range(slots) for part in (0, 2)]
+    count = len(chunks)
     order = []
     for turn in range(count + steps + 2):
         jobs = [(TAKE, turn), (LOW, turn - 1)]
         jobs += [(step, turn - 1 - step) for step in range(1, steps + 1)]
         order += [job for job in jobs if 0 <= job[1] < count]
-    return (DIRECT,) * count, order
+    return chunks, (1,) * count, (DIRECT,) * count, order
 
 
 def params(steps):
@@ -138,12 +141,12 @@
     )(*places, fourier, *received, *after)
 
 
-def low_kernel(source_first, count, order_ref, *refs):
+def low_kernel(source_first, count, pieces, order_ref, *refs):
     rows_refs, (self_ref, pair_ref) = refs[:count], refs[count : count + 2]
-    out_ref, state = refs[-3:-1]
+    out_refs, state = refs[-2 - pieces : -2], refs[-2]
     rows_ref = refs[-1] if count > 1 else rows_refs[0]
     level = pl.program_id(0)
-    blocks = out_ref.shape[0]
+    blocks = state.shape[0]
     bits = blocks.bit_length() - 1
     groups, first, second = rows_ref.shape[:3]
 
@@ -165,7 +168,7 @@
                     rows_ref[pl.ds(order_ref[0] ^ mask, 1)] = source[...].reshape(
                         (1,) + source.shape
                     )
-            target = out_ref if height == bits - 1 else state
+            targets = out_refs if height == bits - 1 else (state,)
             for low in range(blocks):
                 high = low ^ (1 << height)
                 if high < low:
@@ -179,22 +182,27 @@
                     axis=0,
                 )
                 mixed = jnp.dot(factors, values, preferred_element_type=jnp.float32)
-                mixed = mixed.astype(target.dtype)
-                target[low] = mixed[: mixed.shape[0] // 2]
-                target[high] = mixed[mixed.shape[0] // 2 :]
-
-
-def low_levels(rows, order, coeff_self, coeff_pair, slot, source_first, after):
+                mixed = mixed.astype(state.dtype)
+                half, width = mixed.shape[0] // 2, mixed.shape[1] // len(targets)
+                for piece, target in enumerate(targets):
+                    columns = slice(piece * width, (piece + 1) * width)
+                    target[low] = mixed[:half, columns]
+                    target[high] = mixed[half:, columns]
+
+
+def low_levels(rows, order, coeff_self, coeff_pair, slot, source_first, pieces, after):
+    rows = [pltpu.with_memory_space_constraint(value, pltpu.HBM) for value in rows]
     width = rows[0].shape[-1]
     blocks, cycle = coeff_self.shape[2:4]
     bits = blocks.bit_length() - 1
+    shape = (blocks, cycle, width // pieces)
     factor = pl.BlockSpec((1, 1, blocks, cycle, cycle), lambda level, *order: (level, slot, 0, 0, 0))
     scratch = [pltpu.VMEM((blocks, cycle, width), rows[0].dtype)]
     scratch.append(
         pltpu.VMEM((len(rows),) + rows[0].shape if len(rows) > 1 else (8, 128), rows[0].dtype)
     )
     return pl.pallas_call(
-        functools.partial(low_kernel, source_first, len(rows)),
+        functools.partial(low_kernel, source_first, len(rows), pieces),
         grid_spec=pltpu.PrefetchScalarGridSpec(
             num_scalar_prefetch=1,
             grid=(bits,),
@@ -204,10 +212,10 @@
             ]
             + [factor, factor]
             + anywhere(after),
-            out_specs=pl.BlockSpec((blocks, cycle, width), lambda level, *order: (0, 0, 0)),
+            out_specs=[pl.BlockSpec(shape, lambda level, *order: (0, 0, 0))] * pieces,
             scratch_shapes=scratch,
         ),
-        out_shape=jax.ShapeDtypeStruct((blocks, cycle, width), rows[0].dtype),
+        out_shape=[jax.ShapeDtypeStruct(shape, rows[0].dtype)] * pieces,
         compiler_params=params(1),
         cost_estimate=cost(),
         name="low_levels",
@@ -256,6 +264,7 @@
 
 
 def local(fourier, order_slot, coeff_self, coeff_pair):
+    fourier = pltpu.with_memory_space_constraint(fourier, pltpu.HBM)
     order_count = lax.axis_size("order")
     level_count = lax.axis_size("level")
     levels, orders_here, blocks_here, cycle_rows, _ = coeff_self.shape
@@ -263,11 +272,9 @@
     local_bits = blocks_here.bit_length() - 1
     steps = levels - local_bits
     group = blocks_here // level_count
-    width = columns // COLUMN_PARTS
-    chunks = [
-        (slot, part * width, width) for slot in range(orders_here) for part in range(COLUMN_PARTS)
-    ]
-    modes, order = run_order(len(chunks), steps, rows_here % 16 == 0)
+    parts, pieces, modes, order = plan(orders_here, steps, rows_here % 16 == 0)
+    quarter = columns // 4
+    chunks = [(slot, first * quarter, count * quarter) for slot, first, count in parts]
 
     def place(axis):
         return lax.axis_index(axis).astype(jnp.int32).reshape(1)
@@ -275,12 +282,18 @@
     places = (place("level"), place("order"), order_slot)
     level_masks = tuple(range(1, level_count))
     shape = (orders_here, blocks_here, cycle_rows, columns)
+    where = [
+        (at, slot, start + piece * (width // count), width // count)
+        for at, ((slot, start, width), count) in enumerate(zip(chunks, pieces))
+        for piece in range(count)
+    ]
     outgoing, rows, state = {}, {}, {}
     result = None
     last = []
     for kind, at in order:
-        chunk, mode = chunks[at], modes[at]
-        slot, start, _ = chunk
+        if kind in (TAKE, GATHER, LOW):
+            chunk, mode = chunks[at], modes[at]
+            slot, start, width = chunk
         if kind == TAKE:
             masks = () if mode == DIRECT else level_masks
             outgoing[at] = take_rows(fourier, places, chunk, masks, order_count, last)
@@ -313,11 +326,21 @@
                     lax.all_to_all(gathered[0], "order", split_axis=0, concat_axis=0, tiled=True)
                 ]
         elif kind == LOW:
-            state[at] = low_levels(
-                rows[at], places[1], coeff_self, coeff_pair, slot, mode == DIRECT, last
+            lowest = low_levels(
+                rows[at],
+                places[1],
+                coeff_self,
+                coeff_pair,
+                slot,
+                mode == DIRECT,
+                pieces[at],
+                last,
             )
-            last = [state[at]]
+            last = [lowest[0]]
+            first = [piece for piece, (chunk, *_) in enumerate(where) if chunk == at][0]
+            state.update(enumerate(lowest, first))
         else:
+            _, slot, start, width = where[at]
             other = swap(state[at], "level", 1 << (kind - 1))
             final = None
             if kind == steps:

time: 314 us -> 313 us (level)
  local copies, waits for them, and re-layouts: 5.06 us -> 0.74 us
  Pallas kernels: 58.7 us -> 63 us
  waiting for transfers between devices: 213 us -> 209 us
    unnamed x16 -> x8, local copies, waits for them, and re-layouts: 5.06 us -> 0.74 us
    pallas_call x4, Pallas kernels: 12.1 us -> 15.5 us  [take_rows(): pl.pallas_call(functools.partial(copy_kernel, len(masks) or 1), grid_spec...]
  transfers between devices with their start and end apart: 15 -> 15, of which waited for: 11 -> 11; matrix products, arithmetic and copies ran while one was open for 0% -> 0% of each run, Pallas kernels for 17% -> 18%
where the time goes in v3:
time: 313 us; the launch traced here: 311 us
  waiting for transfers between devices  209 us (67%)
  Pallas kernels  63 us (20%)
  starting transfers between devices  38.2 us (12%)
    ppermute x11, waiting for transfers between devices, swap(): return lax.ppermute(value, axis, pairs)  169 us
    all_to_all x3, waiting for transfers between devices, local(): lax.all_to_all(value, ('order', 'level'), split_axis=0, concat_axis=0, ti...  40.4 us
    pallas_call x8, Pallas kernels, high_level(): pl.pallas_call(high_kernel, grid=(blocks // step,), in_specs=in_specs + a...  26.7 us
    ppermute x11, starting transfers between devices, swap(): return lax.ppermute(value, axis, pairs)  17.7 us
    pallas_call x4, Pallas kernels, low_levels(): pl.pallas_call(functools.partial(low_kernel, source_first, len(rows), pie...  17 us
    all_to_all x3, starting transfers between devices, local(): lax.all_to_all(value, ('order', 'level'), split_axis=0, concat_axis=0, ti...  16.3 us
    pallas_call x4, Pallas kernels, take_rows(): pl.pallas_call(functools.partial(copy_kernel, len(masks) or 1), grid_spec...  15.5 us
  transfers between devices with their start and end apart: 15, of which 11 were waited for; matrix products, arithmetic and copies ran while one was open for 0% of the time, Pallas kernels for 18%

profile of v3, /device:TPU:0, one launch (start us, length us, event | category | flops | bytes accessed | tf_op | source)
XLA Modules:
  0.0 311.3 jit_solution(14965329652890475134)
XLA Ops:
  4.6 8.3 %all-to-all-start = ((bf16[16,4,32,256]{3,2,1,0:T(8,128)(2,1)}), bf16[16,4,32,256]{3,2,1,0:T(8,128)(2,1)S(1)}, u32[]{:S(2)}, u32[]{:S(2)}) async-start(bf16[16,4,32,256]{3,2,1,0:T(8,128)(2,1)} %bitcast.2), calls=%async_computation | async-start | bytes 2097152 | tf_op jit(solution)/shard_map/all_to_all | solution.py:305
  13.0 3.9 %take_rows.5.refs_3_ = bf16[4,16,32,256]{3,2,1,0:T(8,128)(2,1)} custom-call(s32[1]{0:T(128)} %bitcast.1.level_ref, s32[1]{0:T(128)} %bitcast.order_ref, s32[8]{0:T(128)S(1)} %copy-done.1, bf16[8,16,1,32,512]{4,3,2,1,0:T(8,128)(2,1)} %refs_0_.9, bf16[4,16,32,256]{3,2,1,0:T(8,128)(2,1)} %take_rows.4.refs_1_), custom_call_target="tpu_custom_call" | custom-call | bytes 1024 | tf_op jit(solution)/shard_map/take_rows/pallas_call | solution.py:70
  16.9 23.5 %all-to-all-done = bf16[16,4,32,256]{3,2,1,0:T(8,128)(2,1)S(1)} async-done(((bf16[16,4,32,256]{3,2,1,0:T(8,128)(2,1)}), bf16[16,4,32,256]{3,2,1,0:T(8,128)(2,1)S(1)}, u32[]{:S(2)}, u32[]{:S(2)}) %all-to-all-start) | async-done | bytes 1048608 | tf_op jit(solution)/shard_map/all_to_all | solution.py:305
  44.1 4.2 %low_levels.4.refs_1_.own_ref = bf16[16,128,256]{2,1,0:T(8,128)(2,1)S(1)} custom-call(s32[1]{0:T(128)} %bitcast.order_ref, bf16[4,4,4,32,256]{4,3,2,1,0:T(8,128)(2,1)} %bitcast.9, bf16[6,2,16,128,128]{4,3,2,1,0:T(8,128)(2,1)} %self_ref.15, bf16[6,2,16,128,128]{4,3,2,1,0:T(8,128)(2,1)} %pair_ref.15, bf16[4,16,32,256]{3,2,1,0:T(8,128)(2,1)} %take_rows.5.refs_3_), custom_call_target="tpu_custom_call" | custom-call | bytes 1024 | tf_op jit(solution)/shard_map/low_levels/pallas_call | solution.py:204
  50.2 3.9 %take_rows.6.refs_0_ = bf16[4,16,32,256]{3,2,1,0:T(8,128)(2,1)} custom-call(s32[1]{0:T(128)} %bitcast.1.level_ref, s32[1]{0:T(128)} %bitcast.order_ref, s32[8]{0:T(128)S(1)} %copy-done.1, bf16[8,16,1,32,512]{4,3,2,1,0:T(8,128)(2,1)} %refs_0_.9, bf16[16,128,256]{2,1,0:T(8,128)(2,1)S(1)} %low_levels.4.refs_1_.own_ref), custom_call_target="tpu_custom_call" | custom-call | bytes 1024 | tf_op jit(solution)/shard_map/take_rows/pallas_call | solution.py:70
  54.1 16.9 %all-to-all-done.2 = bf16[16,4,32,256]{3,2,1,0:T(8,128)(2,1)S(1)} async-done(((bf16[16,4,32,256]{3,2,1,0:T(8,128)(2,1)}), bf16[16,4,32,256]{3,2,1,0:T(8,128)(2,1)S(1)}, u32[]{:S(2)}, u32[]{:S(2)}) %all-to-all-start.2) | async-done | bytes 1048608 | tf_op jit(solution)/shard_map/all_to_all | solution.py:305
  71.0 4.3 %all-to-all-start.1 = ((bf16[16,4,32,256]{3,2,1,0:T(8,128)(2,1)}), bf16[16,4,32,256]{3,2,1,0:T(8,128)(2,1)}, u32[]{:S(2)}, u32[]{:S(2)}) async-start(bf16[16,4,32,256]{3,2,1,0:T(8,128)(2,1)} %bitcast.4), calls=%async_computation.1 | async-start | bytes 2097152 | tf_op jit(solution)/shard_map/all_to_all | solution.py:305
  75.4 16.3 %collective-permute-done.other_ref = bf16[16,128,256]{2,1,0:T(8,128)(2,1)S(1)} collective-permute-done((bf16[16,128,256]{2,1,0:T(8,128)(2,1)S(1)}, bf16[16,128,256]{2,1,0:T(8,128)(2,1)S(1)}, u32[]{:S(2)}, u32[]{:S(2)}) %collective-permute-start) | collective-permute-done | bytes 1048608 | tf_op jit(solution)/shard_map/ppermute | solution.py:51
  98.1 4.2 %low_levels.5.own_ref.refs_0_ = bf16[16,128,256]{2,1,0:T(8,128)(2,1)S(1)} custom-call(s32[1]{0:T(128)} %bitcast.order_ref, bf16[4,4,4,32,256]{4,3,2,1,0:T(8,128)(2,1)} %bitcast.8, bf16[6,2,16,128,128]{4,3,2,1,0:T(8,128)(2,1)} %self_ref.15, bf16[6,2,16,128,128]{4,3,2,1,0:T(8,128)(2,1)} %pair_ref.15, bf16[4,4,32,256]{3,2,1,0:T(8,128)(2,1)S(1)} %get-tuple-element.8.refs_3_), custom_call_target="tpu_custom_call" | custom-call | bytes 1024 | tf_op jit(solution)/shard_map/low_levels/pallas_call | solution.py:204
  104.5 4.9 %collective-permute-start.6 = (bf16[16,128,256]{2,1,0:T(8,128)(2,1)S(1)}, bf16[16,128,256]{2,1,0:T(8,128)(2,1)}, u32[]{:S(2)}, u32[]{:S(2)}) collective-permute-start(bf16[16,128,256]{2,1,0:T(8,128)(2,1)S(1)} %high_level.8.refs_3_.own_ref), channel_id=1, source_target_pairs={{0,4},{2,6},{4,0},{6,2},{1,5},{3,7},{5,1},{7,3},{8,12},{10,14},{12... | collective-permute-start | bytes 3145736 | tf_op jit(solution)/shard_map/ppermute | solution.py:51
  109.4 4.3 %collective-permute-start.3 = (bf16[4,4,32,256]{3,2,1,0:T(8,128)(2,1)}, bf16[4,4,32,256]{3,2,1,0:T(8,128)(2,1)}, u32[]{:S(2)}, u32[]{:S(2)}) collective-permute-start(bf16[4,4,32,256]{3,2,1,0:T(8,128)(2,1)} %get-tuple-element.10), channel_id=1, source_target_pairs={{0,6},{2,4},{4,2},{6,0},{1,7},{3,5},{5,3},{7,1},{8,14},{10,12},{12... | collective-permute-start | bytes 786440 | tf_op jit(solution)/shard_map/ppermute | solution.py:51
  113.7 38.6 %collective-permute-done.4.other_ref = bf16[16,128,256]{2,1,0:T(8,128)(2,1)S(1)} collective-permute-done((bf16[16,128,256]{2,1,0:T(8,128)(2,1)S(1)}, bf16[16,128,256]{2,1,0:T(8,128)(2,1)S(1)}, u32[]{:S(2)}, u32[]{:S(2)}) %collective-permute-start.4) | collective-permute-done | bytes 1048608 | tf_op jit(solution)/shard_map/ppermute | solution.py:51
  155.0 4.2 %low_levels.6.refs_4_.own_ref = bf16[16,128,256]{2,1,0:T(8,128)(2,1)S(1)} custom-call(s32[1]{0:T(128)} %bitcast.order_ref, bf16[4,4,4,32,256]{4,3,2,1,0:T(8,128)(2,1)} %bitcast.5.refs_0_, bf16[6,2,16,128,128]{4,3,2,1,0:T(8,128)(2,1)} %self_ref.15, bf16[6,2,16,128,128]{4,3,2,1,0:T(8,128)(2,1)} %pair_ref.15, bf16[16,128,256]{2,1,0:T(8,128)(2,1)S(1)} %high_level.9.refs_3_.own_ref), custom_call_target="tpu_custom_call" | custom-call | bytes 1024 | tf_op jit(solution)/shard_map/low_levels/pallas_call | solution.py:204
  159.3 8.2 %collective-permute-done.2.refs_2_ = bf16[4,4,32,256]{3,2,1,0:T(8,128)(2,1)} collective-permute-done((bf16[4,4,32,256]{3,2,1,0:T(8,128)(2,1)}, bf16[4,4,32,256]{3,2,1,0:T(8,128)(2,1)}, u32[]{:S(2)}, u32[]{:S(2)}) %collective-permute-start.2) | collective-permute-done | bytes 262176 | tf_op jit(solution)/shard_map/ppermute | solution.py:51
  167.5 4.8 %collective-permute-done.3.refs_3_ = bf16[4,4,32,256]{3,2,1,0:T(8,128)(2,1)} collective-permute-done((bf16[4,4,32,256]{3,2,1,0:T(8,128)(2,1)}, bf16[4,4,32,256]{3,2,1,0:T(8,128)(2,1)}, u32[]{:S(2)}, u32[]{:S(2)}) %collective-permute-start.3) | collective-permute-done | bytes 262176 | tf_op jit(solution)/shard_map/ppermute | solution.py:51
  176.2 4.2 %all-to-all-start.3 = ((bf16[4,4,4,32,256]{4,3,2,1,0:T(8,128)(2,1)}), bf16[4,4,4,32,256]{4,3,2,1,0:T(8,128)(2,1)}, u32[]{:S(2)}, u32[]{:S(2)}) async-start(bf16[4,4,4,32,256]{4,3,2,1,0:T(8,128)(2,1)} %gather_blocks.1.refs_0_), calls=%async_computation.3 | async-start | bytes 2097152 | tf_op jit(solution)/shard_map/all_to_all | solution.py:326
  181.5 4.0 %high_level.10.refs_0_ = bf16[2,16,128,512]{3,2,1,0:T(8,128)(2,1)} custom-call(bf16[16,128,256]{2,1,0:T(8,128)(2,1)S(1)} %high_level.8.refs_3_.own_ref, bf16[16,128,256]{2,1,0:T(8,128)(2,1)} %collective-permute-done.6.other_ref, bf16[6,2,16,128,128]{4,3,2,1,0:T(8,128)(2,1)} %self_ref.15, bf16[6,2,16,128,128]{4,3,2,1,0:T(8,128)(2,1)} %pair_ref.15, ...), custom_call_target="tpu_custom_call" | custom-call | bytes 1024 | tf_op jit(solution)/shard_map/high_level/pallas_call | solution.py:253
  185.5 17.0 %collective-permute-done.5.other_ref = bf16[16,128,256]{2,1,0:T(8,128)(2,1)} collective-permute-done((bf16[16,128,256]{2,1,0:T(8,128)(2,1)S(1)}, bf16[16,128,256]{2,1,0:T(8,128)(2,1)}, u32[]{:S(2)}, u32[]{:S(2)}) %collective-permute-start.5) | collective-permute-done | bytes 1048608 | tf_op jit(solution)/shard_map/ppermute | solution.py:51
  205.4 4.2 %low_levels.7.refs_1_.own_ref = bf16[16,128,256]{2,1,0:T(8,128)(2,1)S(1)} custom-call(s32[1]{0:T(128)} %bitcast.order_ref, bf16[4,4,4,32,256]{4,3,2,1,0:T(8,128)(2,1)} %all-to-all-done.3.refs_0_, bf16[6,2,16,128,128]{4,3,2,1,0:T(8,128)(2,1)} %self_ref.15, bf16[6,2,16,128,128]{4,3,2,1,0:T(8,128)(2,1)} %pair_ref.15, ...), custom_call_target="tpu_custom_call" | custom-call | bytes 1024 | tf_op jit(solution)/shard_map/low_levels/pallas_call | solution.py:204
  212.3 12.1 %collective-permute-done.8.other_ref = bf16[16,128,256]{2,1,0:T(8,128)(2,1)} collective-permute-done((bf16[16,128,256]{2,1,0:T(8,128)(2,1)S(1)}, bf16[16,128,256]{2,1,0:T(8,128)(2,1)}, u32[]{:S(2)}, u32[]{:S(2)}) %collective-permute-start.8) | collective-permute-done | bytes 1048608 | tf_op jit(solution)/shard_map/ppermute | solution.py:51
  224.5 4.0 %high_level.12.refs_0_ = bf16[2,16,128,512]{3,2,1,0:T(8,128)(2,1)} custom-call(bf16[16,128,256]{2,1,0:T(8,128)(2,1)S(1)} %high_level.9.refs_3_.own_ref, bf16[16,128,256]{2,1,0:T(8,128)(2,1)} %collective-permute-done.8.other_ref, bf16[6,2,16,128,128]{4,3,2,1,0:T(8,128)(2,1)} %self_ref.15, ...), custom_call_target="tpu_custom_call", output_to_operand_aliasing={{}: (4, {})} | custom-call | bytes 1024 | tf_op jit(solution)/shard_map/high_level/pallas_call | solution.py:253
  228.5 25.2 %collective-permute-done.7.other_ref = bf16[16,128,256]{2,1,0:T(8,128)(2,1)S(1)} collective-permute-done((bf16[16,128,256]{2,1,0:T(8,128)(2,1)S(1)}, bf16[16,128,256]{2,1,0:T(8,128)(2,1)S(1)}, u32[]{:S(2)}, u32[]{:S(2)}) %collective-permute-start.7) | collective-permute-done | bytes 1048608 | tf_op jit(solution)/shard_map/ppermute | solution.py:51
  257.1 32.2 %collective-permute-done.10.other_ref = bf16[16,128,256]{2,1,0:T(8,128)(2,1)S(1)} collective-permute-done((bf16[16,128,256]{2,1,0:T(8,128)(2,1)S(1)}, bf16[16,128,256]{2,1,0:T(8,128)(2,1)S(1)}, u32[]{:S(2)}, u32[]{:S(2)}) %collective-permute-start.10) | collective-permute-done | bytes 1048608 | tf_op jit(solution)/shard_map/ppermute | solution.py:51
  293.2 14.3 %collective-permute-done.9.other_ref = bf16[16,128,256]{2,1,0:T(8,128)(2,1)S(1)} collective-permute-done((bf16[16,128,256]{2,1,0:T(8,128)(2,1)S(1)}, bf16[16,128,256]{2,1,0:T(8,128)(2,1)S(1)}, u32[]{:S(2)}, u32[]{:S(2)}) %collective-permute-start.9) | collective-permute-done | bytes 1048608 | tf_op jit(solution)/shard_map/ppermute | solution.py:51
  (31 shorter events, 43.1 us)
Async XLA Ops:
  0.0 13.0 %copy-start.1 = (s32[8]{0:T(128)S(1)}, s32[8]{0:T(128)}, u32[]{:S(2)}) copy-start(s32[8]{0:T(128)} %slot_ref.9) | copy-start | bytes 100
  0.0 0.7 copy-start
  4.6 35.8 %all-to-all-start = ((bf16[16,4,32,256]{3,2,1,0:T(8,128)(2,1)}), bf16[16,4,32,256]{3,2,1,0:T(8,128)(2,1)S(1)}, u32[]{:S(2)}, u32[]{:S(2)}) async-start(bf16[16,4,32,256]{3,2,1,0:T(8,128)(2,1)} %bitcast.2), calls=%async_computation | async-start | bytes 2097152 | tf_op jit(solution)/shard_map/all_to_all | solution.py:305
  40.4 3.7 %copy-start.3 = (bf16[16,4,32,256]{3,2,1,0:T(8,128)(2,1)}, bf16[16,4,32,256]{3,2,1,0:T(8,128)(2,1)S(1)}, u32[]{:S(2)}) copy-start(bf16[16,4,32,256]{3,2,1,0:T(8,128)(2,1)S(1)} %all-to-all-done) | copy-start | bytes 3145732
  40.4 30.6 %all-to-all-start.2 = ((bf16[16,4,32,256]{3,2,1,0:T(8,128)(2,1)}), bf16[16,4,32,256]{3,2,1,0:T(8,128)(2,1)S(1)}, u32[]{:S(2)}, u32[]{:S(2)}) async-start(bf16[16,4,32,256]{3,2,1,0:T(8,128)(2,1)} %bitcast.6), calls=%async_computation.2 | async-start | bytes 2097152 | tf_op jit(solution)/shard_map/all_to_all | solution.py:305
  48.4 43.3 %collective-permute-start = (bf16[16,128,256]{2,1,0:T(8,128)(2,1)S(1)}, bf16[16,128,256]{2,1,0:T(8,128)(2,1)S(1)}, u32[]{:S(2)}, u32[]{:S(2)}) collective-permute-start(bf16[16,128,256]{2,1,0:T(8,128)(2,1)S(1)} %low_levels.4.refs_1_.own_ref), channel_id=1, source_target_pairs={{0,2},{2,0},{4,6},{6,4},{1,3},{3,1},{5,7},{7,5},{8,10},{10,8},{12,... | collective-permute-start | bytes 3145736 | tf_op jit(solution)/shard_map/ppermute | solution.py:51
  71.0 4.4 %copy-start.2 = (bf16[16,4,32,256]{3,2,1,0:T(8,128)(2,1)}, bf16[16,4,32,256]{3,2,1,0:T(8,128)(2,1)S(1)}, u32[]{:S(2)}) copy-start(bf16[16,4,32,256]{3,2,1,0:T(8,128)(2,1)S(1)} %all-to-all-done.2) | copy-start | bytes 3145732
  71.0 84.0 %all-to-all-start.1 = ((bf16[16,4,32,256]{3,2,1,0:T(8,128)(2,1)}), bf16[16,4,32,256]{3,2,1,0:T(8,128)(2,1)}, u32[]{:S(2)}, u32[]{:S(2)}) async-start(bf16[16,4,32,256]{3,2,1,0:T(8,128)(2,1)} %bitcast.4), calls=%async_computation.1 | async-start | bytes 2097152 | tf_op jit(solution)/shard_map/all_to_all | solution.py:305
  102.4 49.9 %collective-permute-start.4 = (bf16[16,128,256]{2,1,0:T(8,128)(2,1)S(1)}, bf16[16,128,256]{2,1,0:T(8,128)(2,1)S(1)}, u32[]{:S(2)}, u32[]{:S(2)}) collective-permute-start(bf16[16,128,256]{2,1,0:T(8,128)(2,1)S(1)} %low_levels.5.own_ref.refs_0_), channel_id=1, source_target_pairs={{0,2},{2,0},{4,6},{6,4},{1,3},{3,1},{5,7},{7,5},{8,10},{10,8},{12,... | collective-permute-start | bytes 3145736 | tf_op jit(solution)/shard_map/ppermute | solution.py:51
  102.4 56.9 %collective-permute-start.1 = (bf16[4,4,32,256]{3,2,1,0:T(8,128)(2,1)S(1)}, bf16[4,4,32,256]{3,2,1,0:T(8,128)(2,1)}, u32[]{:S(2)}, u32[]{:S(2)}) collective-permute-start(bf16[4,4,32,256]{3,2,1,0:T(8,128)(2,1)S(1)} %get-tuple-element.8.refs_3_), channel_id=1, source_target_pairs={{0,2},{2,0},{4,6},{6,4},{1,3},{3,1},{5,7},{7,5},{8,10},{10,8},{12,... | collective-permute-start | bytes 786440 | tf_op jit(solution)/shard_map/ppermute | solution.py:51
  104.5 77.0 %collective-permute-start.6 = (bf16[16,128,256]{2,1,0:T(8,128)(2,1)S(1)}, bf16[16,128,256]{2,1,0:T(8,128)(2,1)}, u32[]{:S(2)}, u32[]{:S(2)}) collective-permute-start(bf16[16,128,256]{2,1,0:T(8,128)(2,1)S(1)} %high_level.8.refs_3_.own_ref), channel_id=1, source_target_pairs={{0,4},{2,6},{4,0},{6,2},{1,5},{3,7},{5,1},{7,3},{8,12},{10,14},{12... | collective-permute-start | bytes 3145736 | tf_op jit(solution)/shard_map/ppermute | solution.py:51
  109.4 58.1 %collective-permute-start.2 = (bf16[4,4,32,256]{3,2,1,0:T(8,128)(2,1)}, bf16[4,4,32,256]{3,2,1,0:T(8,128)(2,1)}, u32[]{:S(2)}, u32[]{:S(2)}) collective-permute-start(bf16[4,4,32,256]{3,2,1,0:T(8,128)(2,1)} %get-tuple-element.9), channel_id=1, source_target_pairs={{0,4},{2,6},{4,0},{6,2},{1,5},{3,7},{5,1},{7,3},{8,12},{10,14},{12... | collective-permute-start | bytes 786440 | tf_op jit(solution)/shard_map/ppermute | solution.py:51
  109.4 62.9 %collective-permute-start.3 = (bf16[4,4,32,256]{3,2,1,0:T(8,128)(2,1)}, bf16[4,4,32,256]{3,2,1,0:T(8,128)(2,1)}, u32[]{:S(2)}, u32[]{:S(2)}) collective-permute-start(bf16[4,4,32,256]{3,2,1,0:T(8,128)(2,1)} %get-tuple-element.10), channel_id=1, source_target_pairs={{0,6},{2,4},{4,2},{6,0},{1,7},{3,5},{5,3},{7,1},{8,14},{10,12},{12... | collective-permute-start | bytes 786440 | tf_op jit(solution)/shard_map/ppermute | solution.py:51
  159.2 43.2 %collective-permute-start.5 = (bf16[16,128,256]{2,1,0:T(8,128)(2,1)S(1)}, bf16[16,128,256]{2,1,0:T(8,128)(2,1)}, u32[]{:S(2)}, u32[]{:S(2)}) collective-permute-start(bf16[16,128,256]{2,1,0:T(8,128)(2,1)S(1)} %low_levels.6.refs_4_.own_ref), channel_id=1, source_target_pairs={{0,2},{2,0},{4,6},{6,4},{1,3},{3,1},{5,7},{7,5},{8,10},{10,8},{12,... | collective-permute-start | bytes 3145736 | tf_op jit(solution)/shard_map/ppermute | solution.py:51
  176.2 29.2 %all-to-all-start.3 = ((bf16[4,4,4,32,256]{4,3,2,1,0:T(8,128)(2,1)}), bf16[4,4,4,32,256]{4,3,2,1,0:T(8,128)(2,1)}, u32[]{:S(2)}, u32[]{:S(2)}) async-start(bf16[4,4,4,32,256]{4,3,2,1,0:T(8,128)(2,1)} %gather_blocks.1.refs_0_), calls=%async_computation.3 | async-start | bytes 2097152 | tf_op jit(solution)/shard_map/all_to_all | solution.py:326
  180.4 44.0 %collective-permute-start.8 = (bf16[16,128,256]{2,1,0:T(8,128)(2,1)S(1)}, bf16[16,128,256]{2,1,0:T(8,128)(2,1)}, u32[]{:S(2)}, u32[]{:S(2)}) collective-permute-start(bf16[16,128,256]{2,1,0:T(8,128)(2,1)S(1)} %high_level.9.refs_3_.own_ref), channel_id=1, source_target_pairs={{0,4},{2,6},{4,0},{6,2},{1,5},{3,7},{5,1},{7,3},{8,12},{10,14},{12... | collective-permute-start | bytes 3145736 | tf_op jit(solution)/shard_map/ppermute | solution.py:51
  209.6 44.1 %collective-permute-start.7 = (bf16[16,128,256]{2,1,0:T(8,128)(2,1)S(1)}, bf16[16,128,256]{2,1,0:T(8,128)(2,1)S(1)}, u32[]{:S(2)}, u32[]{:S(2)}) collective-permute-start(bf16[16,128,256]{2,1,0:T(8,128)(2,1)S(1)} %low_levels.7.refs_1_.own_ref), channel_id=1, source_target_pairs={{0,2},{2,0},{4,6},{6,4},{1,3},{3,1},{5,7},{7,5},{8,10},{10,8},{12,... | collective-permute-start | bytes 3145736 | tf_op jit(solution)/shard_map/ppermute | solution.py:51
  209.7 79.6 %collective-permute-start.10 = (bf16[16,128,256]{2,1,0:T(8,128)(2,1)S(1)}, bf16[16,128,256]{2,1,0:T(8,128)(2,1)S(1)}, u32[]{:S(2)}, u32[]{:S(2)}) collective-permute-start(bf16[16,128,256]{2,1,0:T(8,128)(2,1)S(1)} %high_level.11.refs_3_.own_ref), channel_id=1, source_target_pairs={{0,4},{2,6},{4,0},{6,2},{1,5},{3,7},{5,1},{7,3},{8,12},{10,14},{12... | collective-permute-start | bytes 3145736 | tf_op jit(solution)/shard_map/ppermute | solution.py:51
  256.4 51.0 %collective-permute-start.9 = (bf16[16,128,256]{2,1,0:T(8,128)(2,1)S(1)}, bf16[16,128,256]{2,1,0:T(8,128)(2,1)S(1)}, u32[]{:S(2)}, u32[]{:S(2)}) collective-permute-start(bf16[16,128,256]{2,1,0:T(8,128)(2,1)S(1)} %high_level.13.refs_1_.own_ref), channel_id=1, source_target_pairs={{0,4},{2,6},{4,0},{6,2},{1,5},{3,7},{5,1},{7,3},{8,12},{10,14},{12... | collective-permute-start | bytes 3145736 | tf_op jit(solution)/shard_map/ppermute | solution.py:51

commit v4 on v3

--- a/solution.py
+++ b/solution.py
@@ -234,7 +234,7 @@
 
 def high_level(own, other, coeff_self, coeff_pair, level, slot, after, final=None):
     blocks, cycle, width = own.shape
-    step = min(4, blocks)
+    step = min(8, blocks)
     value = pl.BlockSpec((step, cycle, width), lambda at: (at, 0, 0))
     factor = pl.BlockSpec((1, 1, step, cycle, cycle), lambda at: (level, slot, at, 0, 0))
     operands = [own, other, coeff_self, coeff_pair]

time: 313 us -> 311 us (level)
  waiting for transfers between devices: 209 us -> 219 us
  Pallas kernels: 63 us -> 53.5 us
    ppermute x11, waiting for transfers between devices: 169 us -> 178 us  [swap(): return lax.ppermute(value, axis, pairs)]
    pallas_call x8, Pallas kernels: 26.7 us -> 17.1 us  [high_level(): pl.pallas_call(high_kernel, grid=(blocks // step,), in_specs=in_specs + a...]
  transfers between devices with their start and end apart: 15 -> 15, of which waited for: 11 -> 11; matrix products, arithmetic and copies ran while one was open for 0% -> 0% of each run, Pallas kernels for 18% -> 15%
where the time goes in v4:
time: 311 us; the launch traced here: 309 us
  waiting for transfers between devices  219 us (70%)
  Pallas kernels  53.5 us (17%)
  starting transfers between devices  36.2 us (12%)
    ppermute x11, waiting for transfers between devices, swap(): return lax.ppermute(value, axis, pairs)  178 us
    all_to_all x3, waiting for transfers between devices, local(): lax.all_to_all(value, ('order', 'level'), split_axis=0, concat_axis=0, ti...  40.4 us
    pallas_call x8, Pallas kernels, high_level(): pl.pallas_call(high_kernel, grid=(blocks // step,), in_specs=in_specs + a...  17.1 us
    pallas_call x4, Pallas kernels, low_levels(): pl.pallas_call(functools.partial(low_kernel, source_first, len(rows), pie...  17 us
    all_to_all x3, starting transfers between devices, local(): lax.all_to_all(value, ('order', 'level'), split_axis=0, concat_axis=0, ti...  16.3 us
    ppermute x11, starting transfers between devices, swap(): return lax.ppermute(value, axis, pairs)  15.6 us
    pallas_call x4, Pallas kernels, take_rows(): pl.pallas_call(functools.partial(copy_kernel, len(masks) or 1), grid_spec...  15.5 us
  transfers between devices with their start and end apart: 15, of which 11 were waited for; matrix products, arithmetic and copies ran while one was open for 0% of the time, Pallas kernels for 15%

profile of v4, /device:TPU:0, one launch (start us, length us, event | category | flops | bytes accessed | tf_op | source)
XLA Modules:
  0.0 309.3 jit_solution(6674067062357036598)
XLA Ops:
  0.7 3.9 %take_rows.4.refs_1_ = bf16[4,16,32,256]{3,2,1,0:T(8,128)(2,1)} custom-call(s32[1]{0:T(128)} %bitcast.1.level_ref, s32[1]{0:T(128)} %bitcast.order_ref, s32[8]{0:T(128)S(1)} %copy-done, bf16[8,16,1,32,512]{4,3,2,1,0:T(8,128)(2,1)} %refs_0_.9), custom_call_target="tpu_custom_call" | custom-call | bytes 1024 | tf_op jit(solution)/shard_map/take_rows/pallas_call | solution.py:70
  4.6 8.3 %all-to-all-start = ((bf16[16,4,32,256]{3,2,1,0:T(8,128)(2,1)}), bf16[16,4,32,256]{3,2,1,0:T(8,128)(2,1)S(1)}, u32[]{:S(2)}, u32[]{:S(2)}) async-start(bf16[16,4,32,256]{3,2,1,0:T(8,128)(2,1)} %bitcast.2), calls=%async_computation | async-start | bytes 2097152 | tf_op jit(solution)/shard_map/all_to_all | solution.py:305
  13.0 3.9 %take_rows.5.refs_3_ = bf16[4,16,32,256]{3,2,1,0:T(8,128)(2,1)} custom-call(s32[1]{0:T(128)} %bitcast.1.level_ref, s32[1]{0:T(128)} %bitcast.order_ref, s32[8]{0:T(128)S(1)} %copy-done.1, bf16[8,16,1,32,512]{4,3,2,1,0:T(8,128)(2,1)} %refs_0_.9, bf16[4,16,32,256]{3,2,1,0:T(8,128)(2,1)} %take_rows.4.refs_1_), custom_call_target="tpu_custom_call" | custom-call | bytes 1024 | tf_op jit(solution)/shard_map/take_rows/pallas_call | solution.py:70
  16.9 23.5 %all-to-all-done = bf16[16,4,32,256]{3,2,1,0:T(8,128)(2,1)S(1)} async-done(((bf16[16,4,32,256]{3,2,1,0:T(8,128)(2,1)}), bf16[16,4,32,256]{3,2,1,0:T(8,128)(2,1)S(1)}, u32[]{:S(2)}, u32[]{:S(2)}) %all-to-all-start) | async-done | bytes 1048608 | tf_op jit(solution)/shard_map/all_to_all | solution.py:305
  44.1 4.2 %low_levels.4.refs_1_.own_ref = bf16[16,128,256]{2,1,0:T(8,128)(2,1)S(1)} custom-call(s32[1]{0:T(128)} %bitcast.order_ref, bf16[4,4,4,32,256]{4,3,2,1,0:T(8,128)(2,1)} %bitcast.9, bf16[6,2,16,128,128]{4,3,2,1,0:T(8,128)(2,1)} %self_ref.15, bf16[6,2,16,128,128]{4,3,2,1,0:T(8,128)(2,1)} %pair_ref.15, bf16[4,16,32,256]{3,2,1,0:T(8,128)(2,1)} %take_rows.5.refs_3_), custom_call_target="tpu_custom_call" | custom-call | bytes 1024 | tf_op jit(solution)/shard_map/low_levels/pallas_call | solution.py:204
  50.2 3.9 %take_rows.6.refs_0_ = bf16[4,16,32,256]{3,2,1,0:T(8,128)(2,1)} custom-call(s32[1]{0:T(128)} %bitcast.1.level_ref, s32[1]{0:T(128)} %bitcast.order_ref, s32[8]{0:T(128)S(1)} %copy-done.1, bf16[8,16,1,32,512]{4,3,2,1,0:T(8,128)(2,1)} %refs_0_.9, bf16[16,128,256]{2,1,0:T(8,128)(2,1)S(1)} %low_levels.4.refs_1_.own_ref), custom_call_target="tpu_custom_call" | custom-call | bytes 1024 | tf_op jit(solution)/shard_map/take_rows/pallas_call | solution.py:70
  54.1 16.9 %all-to-all-done.2 = bf16[16,4,32,256]{3,2,1,0:T(8,128)(2,1)S(1)} async-done(((bf16[16,4,32,256]{3,2,1,0:T(8,128)(2,1)}), bf16[16,4,32,256]{3,2,1,0:T(8,128)(2,1)S(1)}, u32[]{:S(2)}, u32[]{:S(2)}) %all-to-all-start.2) | async-done | bytes 1048608 | tf_op jit(solution)/shard_map/all_to_all | solution.py:305
  71.0 4.3 %all-to-all-start.1 = ((bf16[16,4,32,256]{3,2,1,0:T(8,128)(2,1)}), bf16[16,4,32,256]{3,2,1,0:T(8,128)(2,1)}, u32[]{:S(2)}, u32[]{:S(2)}) async-start(bf16[16,4,32,256]{3,2,1,0:T(8,128)(2,1)} %bitcast.4), calls=%async_computation.1 | async-start | bytes 2097152 | tf_op jit(solution)/shard_map/all_to_all | solution.py:305
  75.4 16.3 %collective-permute-done.other_ref = bf16[16,128,256]{2,1,0:T(8,128)(2,1)S(1)} collective-permute-done((bf16[16,128,256]{2,1,0:T(8,128)(2,1)S(1)}, bf16[16,128,256]{2,1,0:T(8,128)(2,1)S(1)}, u32[]{:S(2)}, u32[]{:S(2)}) %collective-permute-start) | collective-permute-done | bytes 1048608 | tf_op jit(solution)/shard_map/ppermute | solution.py:51
  97.1 4.2 %low_levels.5.own_ref.refs_0_ = bf16[16,128,256]{2,1,0:T(8,128)(2,1)S(1)} custom-call(s32[1]{0:T(128)} %bitcast.order_ref, bf16[4,4,4,32,256]{4,3,2,1,0:T(8,128)(2,1)} %bitcast.8, bf16[6,2,16,128,128]{4,3,2,1,0:T(8,128)(2,1)} %self_ref.15, bf16[6,2,16,128,128]{4,3,2,1,0:T(8,128)(2,1)} %pair_ref.15, bf16[4,4,32,256]{3,2,1,0:T(8,128)(2,1)S(1)} %get-tuple-element.8.refs_3_), custom_call_target="tpu_custom_call" | custom-call | bytes 1024 | tf_op jit(solution)/shard_map/low_levels/pallas_call | solution.py:204
  103.4 4.9 %collective-permute-start.6 = (bf16[16,128,256]{2,1,0:T(8,128)(2,1)S(1)}, bf16[16,128,256]{2,1,0:T(8,128)(2,1)}, u32[]{:S(2)}, u32[]{:S(2)}) collective-permute-start(bf16[16,128,256]{2,1,0:T(8,128)(2,1)S(1)} %high_level.8.refs_3_.own_ref), channel_id=1, source_target_pairs={{0,4},{2,6},{4,0},{6,2},{1,5},{3,7},{5,1},{7,3},{8,12},{10,14},{12... | collective-permute-start | bytes 3145736 | tf_op jit(solution)/shard_map/ppermute | solution.py:51
  108.4 4.3 %collective-permute-start.3 = (bf16[4,4,32,256]{3,2,1,0:T(8,128)(2,1)}, bf16[4,4,32,256]{3,2,1,0:T(8,128)(2,1)}, u32[]{:S(2)}, u32[]{:S(2)}) collective-permute-start(bf16[4,4,32,256]{3,2,1,0:T(8,128)(2,1)} %get-tuple-element.10), channel_id=1, source_target_pairs={{0,6},{2,4},{4,2},{6,0},{1,7},{3,5},{5,3},{7,1},{8,14},{10,12},{12... | collective-permute-start | bytes 786440 | tf_op jit(solution)/shard_map/ppermute | solution.py:51
  112.7 38.9 %collective-permute-done.4.other_ref = bf16[16,128,256]{2,1,0:T(8,128)(2,1)S(1)} collective-permute-done((bf16[16,128,256]{2,1,0:T(8,128)(2,1)S(1)}, bf16[16,128,256]{2,1,0:T(8,128)(2,1)S(1)}, u32[]{:S(2)}, u32[]{:S(2)}) %collective-permute-start.4) | collective-permute-done | bytes 1048608 | tf_op jit(solution)/shard_map/ppermute | solution.py:51
  153.2 4.2 %low_levels.6.refs_4_.own_ref = bf16[16,128,256]{2,1,0:T(8,128)(2,1)S(1)} custom-call(s32[1]{0:T(128)} %bitcast.order_ref, bf16[4,4,4,32,256]{4,3,2,1,0:T(8,128)(2,1)} %bitcast.5.refs_0_, bf16[6,2,16,128,128]{4,3,2,1,0:T(8,128)(2,1)} %self_ref.15, bf16[6,2,16,128,128]{4,3,2,1,0:T(8,128)(2,1)} %pair_ref.15, bf16[16,128,256]{2,1,0:T(8,128)(2,1)S(1)} %high_level.9.refs_3_.own_ref), custom_call_target="tpu_custom_call" | custom-call | bytes 1024 | tf_op jit(solution)/shard_map/low_levels/pallas_call | solution.py:204
  157.6 9.4 %collective-permute-done.2.refs_2_ = bf16[4,4,32,256]{3,2,1,0:T(8,128)(2,1)} collective-permute-done((bf16[4,4,32,256]{3,2,1,0:T(8,128)(2,1)}, bf16[4,4,32,256]{3,2,1,0:T(8,128)(2,1)}, u32[]{:S(2)}, u32[]{:S(2)}) %collective-permute-start.2) | collective-permute-done | bytes 262176 | tf_op jit(solution)/shard_map/ppermute | solution.py:51
  167.0 4.3 %collective-permute-done.3.refs_3_ = bf16[4,4,32,256]{3,2,1,0:T(8,128)(2,1)} collective-permute-done((bf16[4,4,32,256]{3,2,1,0:T(8,128)(2,1)}, bf16[4,4,32,256]{3,2,1,0:T(8,128)(2,1)}, u32[]{:S(2)}, u32[]{:S(2)}) %collective-permute-start.3) | collective-permute-done | bytes 262176 | tf_op jit(solution)/shard_map/ppermute | solution.py:51
  171.3 3.9 %gather_blocks.1.refs_0_ = bf16[4,4,4,32,256]{4,3,2,1,0:T(8,128)(2,1)} custom-call(s32[1]{0:T(128)} %bitcast.1.level_ref, s32[1]{0:T(128)} %bitcast.order_ref, s32[8]{0:T(128)S(1)} %copy-done.1, bf16[8,16,1,32,512]{4,3,2,1,0:T(8,128)(2,1)} %refs_0_.9, bf16[4,4,32,256]{3,2,1,0:T(8,128)(2,1)} %collective-permute-done.1.refs_1_, ...), custom_call_target="tpu_custom_call" | custom-call | bytes 1024 | tf_op jit(solution)/shard_map/gather_blocks/pallas_call | solution.py:127
  175.2 4.2 %all-to-all-start.3 = ((bf16[4,4,4,32,256]{4,3,2,1,0:T(8,128)(2,1)}), bf16[4,4,4,32,256]{4,3,2,1,0:T(8,128)(2,1)}, u32[]{:S(2)}, u32[]{:S(2)}) async-start(bf16[4,4,4,32,256]{4,3,2,1,0:T(8,128)(2,1)} %gather_blocks.1.refs_0_), calls=%async_computation.3 | async-start | bytes 2097152 | tf_op jit(solution)/shard_map/all_to_all | solution.py:326
  182.5 20.3 %collective-permute-done.5.other_ref = bf16[16,128,256]{2,1,0:T(8,128)(2,1)} collective-permute-done((bf16[16,128,256]{2,1,0:T(8,128)(2,1)S(1)}, bf16[16,128,256]{2,1,0:T(8,128)(2,1)}, u32[]{:S(2)}, u32[]{:S(2)}) %collective-permute-start.5) | collective-permute-done | bytes 1048608 | tf_op jit(solution)/shard_map/ppermute | solution.py:51
  204.7 4.2 %low_levels.7.refs_1_.own_ref = bf16[16,128,256]{2,1,0:T(8,128)(2,1)S(1)} custom-call(s32[1]{0:T(128)} %bitcast.order_ref, bf16[4,4,4,32,256]{4,3,2,1,0:T(8,128)(2,1)} %all-to-all-done.3.refs_0_, bf16[6,2,16,128,128]{4,3,2,1,0:T(8,128)(2,1)} %self_ref.15, bf16[6,2,16,128,128]{4,3,2,1,0:T(8,128)(2,1)} %pair_ref.15, ...), custom_call_target="tpu_custom_call" | custom-call | bytes 1024 | tf_op jit(solution)/shard_map/low_levels/pallas_call | solution.py:204
  210.5 12.7 %collective-permute-done.8.other_ref = bf16[16,128,256]{2,1,0:T(8,128)(2,1)} collective-permute-done((bf16[16,128,256]{2,1,0:T(8,128)(2,1)S(1)}, bf16[16,128,256]{2,1,0:T(8,128)(2,1)}, u32[]{:S(2)}, u32[]{:S(2)}) %collective-permute-start.8) | collective-permute-done | bytes 1048608 | tf_op jit(solution)/shard_map/ppermute | solution.py:51
  225.9 28.0 %collective-permute-done.7.other_ref = bf16[16,128,256]{2,1,0:T(8,128)(2,1)S(1)} collective-permute-done((bf16[16,128,256]{2,1,0:T(8,128)(2,1)S(1)}, bf16[16,128,256]{2,1,0:T(8,128)(2,1)S(1)}, u32[]{:S(2)}, u32[]{:S(2)}) %collective-permute-start.7) | collective-permute-done | bytes 1048608 | tf_op jit(solution)/shard_map/ppermute | solution.py:51
  255.9 32.9 %collective-permute-done.10.other_ref = bf16[16,128,256]{2,1,0:T(8,128)(2,1)S(1)} collective-permute-done((bf16[16,128,256]{2,1,0:T(8,128)(2,1)S(1)}, bf16[16,128,256]{2,1,0:T(8,128)(2,1)S(1)}, u32[]{:S(2)}, u32[]{:S(2)}) %collective-permute-start.10) | collective-permute-done | bytes 1048608 | tf_op jit(solution)/shard_map/ppermute | solution.py:51
  291.3 15.6 %collective-permute-done.9.other_ref = bf16[16,128,256]{2,1,0:T(8,128)(2,1)S(1)} collective-permute-done((bf16[16,128,256]{2,1,0:T(8,128)(2,1)S(1)}, bf16[16,128,256]{2,1,0:T(8,128)(2,1)S(1)}, u32[]{:S(2)}, u32[]{:S(2)}) %collective-permute-start.9) | collective-permute-done | bytes 1048608 | tf_op jit(solution)/shard_map/ppermute | solution.py:51
  (31 shorter events, 31.7 us)
Async XLA Ops:
  0.0 13.0 %copy-start.1 = (s32[8]{0:T(128)S(1)}, s32[8]{0:T(128)}, u32[]{:S(2)}) copy-start(s32[8]{0:T(128)} %slot_ref.9) | copy-start | bytes 100
  0.0 0.7 copy-start
  4.6 35.8 %all-to-all-start = ((bf16[16,4,32,256]{3,2,1,0:T(8,128)(2,1)}), bf16[16,4,32,256]{3,2,1,0:T(8,128)(2,1)S(1)}, u32[]{:S(2)}, u32[]{:S(2)}) async-start(bf16[16,4,32,256]{3,2,1,0:T(8,128)(2,1)} %bitcast.2), calls=%async_computation | async-start | bytes 2097152 | tf_op jit(solution)/shard_map/all_to_all | solution.py:305
  40.4 3.7 %copy-start.3 = (bf16[16,4,32,256]{3,2,1,0:T(8,128)(2,1)}, bf16[16,4,32,256]{3,2,1,0:T(8,128)(2,1)S(1)}, u32[]{:S(2)}) copy-start(bf16[16,4,32,256]{3,2,1,0:T(8,128)(2,1)S(1)} %all-to-all-done) | copy-start | bytes 3145732
  40.4 30.6 %all-to-all-start.2 = ((bf16[16,4,32,256]{3,2,1,0:T(8,128)(2,1)}), bf16[16,4,32,256]{3,2,1,0:T(8,128)(2,1)S(1)}, u32[]{:S(2)}, u32[]{:S(2)}) async-start(bf16[16,4,32,256]{3,2,1,0:T(8,128)(2,1)} %bitcast.6), calls=%async_computation.2 | async-start | bytes 2097152 | tf_op jit(solution)/shard_map/all_to_all | solution.py:305
  48.4 43.3 %collective-permute-start = (bf16[16,128,256]{2,1,0:T(8,128)(2,1)S(1)}, bf16[16,128,256]{2,1,0:T(8,128)(2,1)S(1)}, u32[]{:S(2)}, u32[]{:S(2)}) collective-permute-start(bf16[16,128,256]{2,1,0:T(8,128)(2,1)S(1)} %low_levels.4.refs_1_.own_ref), channel_id=1, source_target_pairs={{0,2},{2,0},{4,6},{6,4},{1,3},{3,1},{5,7},{7,5},{8,10},{10,8},{12,... | collective-permute-start | bytes 3145736 | tf_op jit(solution)/shard_map/ppermute | solution.py:51
  71.0 4.4 %copy-start.2 = (bf16[16,4,32,256]{3,2,1,0:T(8,128)(2,1)}, bf16[16,4,32,256]{3,2,1,0:T(8,128)(2,1)S(1)}, u32[]{:S(2)}) copy-start(bf16[16,4,32,256]{3,2,1,0:T(8,128)(2,1)S(1)} %all-to-all-done.2) | copy-start | bytes 3145732
  71.0 82.2 %all-to-all-start.1 = ((bf16[16,4,32,256]{3,2,1,0:T(8,128)(2,1)}), bf16[16,4,32,256]{3,2,1,0:T(8,128)(2,1)}, u32[]{:S(2)}, u32[]{:S(2)}) async-start(bf16[16,4,32,256]{3,2,1,0:T(8,128)(2,1)} %bitcast.4), calls=%async_computation.1 | async-start | bytes 2097152 | tf_op jit(solution)/shard_map/all_to_all | solution.py:305
  101.3 50.2 %collective-permute-start.4 = (bf16[16,128,256]{2,1,0:T(8,128)(2,1)S(1)}, bf16[16,128,256]{2,1,0:T(8,128)(2,1)S(1)}, u32[]{:S(2)}, u32[]{:S(2)}) collective-permute-start(bf16[16,128,256]{2,1,0:T(8,128)(2,1)S(1)} %low_levels.5.own_ref.refs_0_), channel_id=1, source_target_pairs={{0,2},{2,0},{4,6},{6,4},{1,3},{3,1},{5,7},{7,5},{8,10},{10,8},{12,... | collective-permute-start | bytes 3145736 | tf_op jit(solution)/shard_map/ppermute | solution.py:51
  101.4 56.1 %collective-permute-start.1 = (bf16[4,4,32,256]{3,2,1,0:T(8,128)(2,1)S(1)}, bf16[4,4,32,256]{3,2,1,0:T(8,128)(2,1)}, u32[]{:S(2)}, u32[]{:S(2)}) collective-permute-start(bf16[4,4,32,256]{3,2,1,0:T(8,128)(2,1)S(1)} %get-tuple-element.8.refs_3_), channel_id=1, source_target_pairs={{0,2},{2,0},{4,6},{6,4},{1,3},{3,1},{5,7},{7,5},{8,10},{10,8},{12,... | collective-permute-start | bytes 786440 | tf_op jit(solution)/shard_map/ppermute | solution.py:51
  103.4 76.5 %collective-permute-start.6 = (bf16[16,128,256]{2,1,0:T(8,128)(2,1)S(1)}, bf16[16,128,256]{2,1,0:T(8,128)(2,1)}, u32[]{:S(2)}, u32[]{:S(2)}) collective-permute-start(bf16[16,128,256]{2,1,0:T(8,128)(2,1)S(1)} %high_level.8.refs_3_.own_ref), channel_id=1, source_target_pairs={{0,4},{2,6},{4,0},{6,2},{1,5},{3,7},{5,1},{7,3},{8,12},{10,14},{12... | collective-permute-start | bytes 3145736 | tf_op jit(solution)/shard_map/ppermute | solution.py:51
  108.3 58.6 %collective-permute-start.2 = (bf16[4,4,32,256]{3,2,1,0:T(8,128)(2,1)}, bf16[4,4,32,256]{3,2,1,0:T(8,128)(2,1)}, u32[]{:S(2)}, u32[]{:S(2)}) collective-permute-start(bf16[4,4,32,256]{3,2,1,0:T(8,128)(2,1)} %get-tuple-element.9), channel_id=1, source_target_pairs={{0,4},{2,6},{4,0},{6,2},{1,5},{3,7},{5,1},{7,3},{8,12},{10,14},{12... | collective-permute-start | bytes 786440 | tf_op jit(solution)/shard_map/ppermute | solution.py:51
  108.4 62.9 %collective-permute-start.3 = (bf16[4,4,32,256]{3,2,1,0:T(8,128)(2,1)}, bf16[4,4,32,256]{3,2,1,0:T(8,128)(2,1)}, u32[]{:S(2)}, u32[]{:S(2)}) collective-permute-start(bf16[4,4,32,256]{3,2,1,0:T(8,128)(2,1)} %get-tuple-element.10), channel_id=1, source_target_pairs={{0,6},{2,4},{4,2},{6,0},{1,7},{3,5},{5,3},{7,1},{8,14},{10,12},{12... | collective-permute-start | bytes 786440 | tf_op jit(solution)/shard_map/ppermute | solution.py:51
  157.5 45.3 %collective-permute-start.5 = (bf16[16,128,256]{2,1,0:T(8,128)(2,1)S(1)}, bf16[16,128,256]{2,1,0:T(8,128)(2,1)}, u32[]{:S(2)}, u32[]{:S(2)}) collective-permute-start(bf16[16,128,256]{2,1,0:T(8,128)(2,1)S(1)} %low_levels.6.refs_4_.own_ref), channel_id=1, source_target_pairs={{0,2},{2,0},{4,6},{6,4},{1,3},{3,1},{5,7},{7,5},{8,10},{10,8},{12,... | collective-permute-start | bytes 3145736 | tf_op jit(solution)/shard_map/ppermute | solution.py:51
  175.2 29.5 %all-to-all-start.3 = ((bf16[4,4,4,32,256]{4,3,2,1,0:T(8,128)(2,1)}), bf16[4,4,4,32,256]{4,3,2,1,0:T(8,128)(2,1)}, u32[]{:S(2)}, u32[]{:S(2)}) async-start(bf16[4,4,4,32,256]{4,3,2,1,0:T(8,128)(2,1)} %gather_blocks.1.refs_0_), calls=%async_computation.3 | async-start | bytes 2097152 | tf_op jit(solution)/shard_map/all_to_all | solution.py:326
  179.4 43.9 %collective-permute-start.8 = (bf16[16,128,256]{2,1,0:T(8,128)(2,1)S(1)}, bf16[16,128,256]{2,1,0:T(8,128)(2,1)}, u32[]{:S(2)}, u32[]{:S(2)}) collective-permute-start(bf16[16,128,256]{2,1,0:T(8,128)(2,1)S(1)} %high_level.9.refs_3_.own_ref), channel_id=1, source_target_pairs={{0,4},{2,6},{4,0},{6,2},{1,5},{3,7},{5,1},{7,3},{8,12},{10,14},{12... | collective-permute-start | bytes 3145736 | tf_op jit(solution)/shard_map/ppermute | solution.py:51
  208.9 45.0 %collective-permute-start.7 = (bf16[16,128,256]{2,1,0:T(8,128)(2,1)S(1)}, bf16[16,128,256]{2,1,0:T(8,128)(2,1)S(1)}, u32[]{:S(2)}, u32[]{:S(2)}) collective-permute-start(bf16[16,128,256]{2,1,0:T(8,128)(2,1)S(1)} %low_levels.7.refs_1_.own_ref), channel_id=1, source_target_pairs={{0,2},{2,0},{4,6},{6,4},{1,3},{3,1},{5,7},{7,5},{8,10},{10,8},{12,... | collective-permute-start | bytes 3145736 | tf_op jit(solution)/shard_map/ppermute | solution.py:51
  209.0 79.8 %collective-permute-start.10 = (bf16[16,128,256]{2,1,0:T(8,128)(2,1)S(1)}, bf16[16,128,256]{2,1,0:T(8,128)(2,1)S(1)}, u32[]{:S(2)}, u32[]{:S(2)}) collective-permute-start(bf16[16,128,256]{2,1,0:T(8,128)(2,1)S(1)} %high_level.11.refs_3_.own_ref), channel_id=1, source_target_pairs={{0,4},{2,6},{4,0},{6,2},{1,5},{3,7},{5,1},{7,3},{8,12},{10,14},{12... | collective-permute-start | bytes 3145736 | tf_op jit(solution)/shard_map/ppermute | solution.py:51
  255.6 51.3 %collective-permute-start.9 = (bf16[16,128,256]{2,1,0:T(8,128)(2,1)S(1)}, bf16[16,128,256]{2,1,0:T(8,128)(2,1)S(1)}, u32[]{:S(2)}, u32[]{:S(2)}) collective-permute-start(bf16[16,128,256]{2,1,0:T(8,128)(2,1)S(1)} %high_level.13.refs_1_.own_ref), channel_id=1, source_target_pairs={{0,4},{2,6},{4,0},{6,2},{1,5},{3,7},{5,1},{7,3},{8,12},{10,14},{12... | collective-permute-start | bytes 3145736 | tf_op jit(solution)/shard_map/ppermute | solution.py:51

commit v5 on v4

--- a/solution.py
+++ b/solution.py
@@ -14,7 +14,7 @@
 PIECES = (1, 1, 1, 1,)
 MODES = (DIRECT, DIRECT, DIRECT, MIXED)
 ORDER = (
-    (TAKE, 0), (TAKE, 1), (LOW, 0), (TAKE, 2), (1, 0), (TAKE, 3), (LOW, 1), (1, 1), (LOW, 2),
+    (TAKE, 0), (TAKE, 1), (LOW, 0), (TAKE, 3), (TAKE, 2), (1, 0), (LOW, 1), (1, 1), (LOW, 2),
     (GATHER, 3), (2, 0), (1, 2), (LOW, 3), (2, 1), (1, 3), (2, 2), (2, 3),
 )
 

time: 311 us -> 310 us (level)
  waiting for transfers between devices: 219 us -> 214 us
    all_to_all x3, waiting for transfers between devices: 40.4 us -> 36.7 us  [local(): lax.all_to_all(value, ('order', 'level'), split_axis=0, concat_axis=0, ti...]
  transfers between devices with their start and end apart: 15 -> 15, of which waited for: 11 -> 9; matrix products, arithmetic and copies ran while one was open for 0% -> 0% of each run, Pallas kernels for 15% -> 15%
where the time goes in v5:
time: 310 us; the launch traced here: 308 us
  waiting for transfers between devices  214 us (69%)
  Pallas kernels  52.3 us (17%)
  starting transfers between devices  38.8 us (13%)
    ppermute x11, waiting for transfers between devices, swap(): return lax.ppermute(value, axis, pairs)  177 us
    all_to_all x3, waiting for transfers between devices, local(): lax.all_to_all(value, ('order', 'level'), split_axis=0, concat_axis=0, ti...  36.7 us
    ppermute x11, starting transfers between devices, swap(): return lax.ppermute(value, axis, pairs)  18.2 us
    pallas_call x8, Pallas kernels, high_level(): pl.pallas_call(high_kernel, grid=(blocks // step,), in_specs=in_specs + a...  17.1 us
    pallas_call x4, Pallas kernels, low_levels(): pl.pallas_call(functools.partial(low_kernel, source_first, len(rows), pie...  17 us
    all_to_all x3, starting transfers between devices, local(): lax.all_to_all(value, ('order', 'level'), split_axis=0, concat_axis=0, ti...  16.3 us
    pallas_call x4, Pallas kernels, take_rows(): pl.pallas_call(functools.partial(copy_kernel, len(masks) or 1), grid_spec...  15.5 us
  transfers between devices with their start and end apart: 15, of which 9 were waited for; matrix products, arithmetic and copies ran while one was open for 0% of the time, Pallas kernels for 15%

profile of v5, /device:TPU:0, one launch (start us, length us, event | category | flops | bytes accessed | tf_op | source)
XLA Modules:
  0.0 308.3 jit_solution(2273702954701929662)
XLA Ops:
  0.7 3.9 %take_rows.4.refs_1_ = bf16[4,16,32,256]{3,2,1,0:T(8,128)(2,1)} custom-call(s32[1]{0:T(128)} %bitcast.1.level_ref, s32[1]{0:T(128)} %bitcast.order_ref, s32[8]{0:T(128)S(1)} %copy-done.2, bf16[8,16,1,32,512]{4,3,2,1,0:T(8,128)(2,1)} %refs_0_.9), custom_call_target="tpu_custom_call" | custom-call | bytes 1024 | tf_op jit(solution)/shard_map/take_rows/pallas_call | solution.py:70
  4.6 8.3 %all-to-all-start = ((bf16[16,4,32,256]{3,2,1,0:T(8,128)(2,1)}), bf16[16,4,32,256]{3,2,1,0:T(8,128)(2,1)S(1)}, u32[]{:S(2)}, u32[]{:S(2)}) async-start(bf16[16,4,32,256]{3,2,1,0:T(8,128)(2,1)} %bitcast.2), calls=%async_computation | async-start | bytes 2097152 | tf_op jit(solution)/shard_map/all_to_all | solution.py:305
  13.0 3.9 %take_rows.5.refs_3_ = bf16[4,16,32,256]{3,2,1,0:T(8,128)(2,1)} custom-call(s32[1]{0:T(128)} %bitcast.1.level_ref, s32[1]{0:T(128)} %bitcast.order_ref, s32[8]{0:T(128)S(1)} %copy-done.3, bf16[8,16,1,32,512]{4,3,2,1,0:T(8,128)(2,1)} %refs_0_.9, bf16[4,16,32,256]{3,2,1,0:T(8,128)(2,1)} %take_rows.4.refs_1_), custom_call_target="tpu_custom_call" | custom-call | bytes 1024 | tf_op jit(solution)/shard_map/take_rows/pallas_call | solution.py:70
  16.9 23.5 %all-to-all-done = bf16[16,4,32,256]{3,2,1,0:T(8,128)(2,1)S(1)} async-done(((bf16[16,4,32,256]{3,2,1,0:T(8,128)(2,1)}), bf16[16,4,32,256]{3,2,1,0:T(8,128)(2,1)S(1)}, u32[]{:S(2)}, u32[]{:S(2)}) %all-to-all-start) | async-done | bytes 1048608 | tf_op jit(solution)/shard_map/all_to_all | solution.py:305
  40.4 3.7 %all-to-all-start.2 = ((bf16[16,4,32,256]{3,2,1,0:T(8,128)(2,1)}), bf16[16,4,32,256]{3,2,1,0:T(8,128)(2,1)S(1)}, u32[]{:S(2)}, u32[]{:S(2)}) async-start(bf16[16,4,32,256]{3,2,1,0:T(8,128)(2,1)} %bitcast.6), calls=%async_computation.2 | async-start | bytes 2097152 | tf_op jit(solution)/shard_map/all_to_all | solution.py:305
  44.1 4.2 %low_levels.4.refs_3_.own_ref = bf16[16,128,256]{2,1,0:T(8,128)(2,1)S(1)} custom-call(s32[1]{0:T(128)} %bitcast.order_ref, bf16[4,4,4,32,256]{4,3,2,1,0:T(8,128)(2,1)} %bitcast.9, bf16[6,2,16,128,128]{4,3,2,1,0:T(8,128)(2,1)} %self_ref.15, bf16[6,2,16,128,128]{4,3,2,1,0:T(8,128)(2,1)} %pair_ref.15, bf16[4,16,32,256]{3,2,1,0:T(8,128)(2,1)} %take_rows.5.refs_3_), custom_call_target="tpu_custom_call" | custom-call | bytes 1024 | tf_op jit(solution)/shard_map/low_levels/pallas_call | solution.py:204
  50.2 3.7 %take_rows.6 = (bf16[4,4,32,256]{3,2,1,0:T(8,128)(2,1)S(1)}, bf16[4,4,32,256]{3,2,1,0:T(8,128)(2,1)}, bf16[4,4,32,256]{3,2,1,0:T(8,128)(2,1)}) custom-call(s32[1]{0:T(128)} %bitcast.1.level_ref, s32[1]{0:T(128)} %bitcast.order_ref, s32[8]{0:T(128)S(1)} %copy-done.3, bf16[8,16,1,32,512]{4,3,2,1,0:T(8,128)(2,1)} %refs_0_.9, ...), custom_call_target="tpu_custom_call" | custom-call | bytes 1024 | tf_op jit(solution)/shard_map/take_rows/pallas_call | solution.py:70
  53.9 3.9 %take_rows.7.refs_0_ = bf16[4,16,32,256]{3,2,1,0:T(8,128)(2,1)} custom-call(s32[1]{0:T(128)} %bitcast.1.level_ref, s32[1]{0:T(128)} %bitcast.order_ref, s32[8]{0:T(128)S(1)} %copy-done.3, bf16[8,16,1,32,512]{4,3,2,1,0:T(8,128)(2,1)} %refs_0_.9, bf16[4,4,32,256]{3,2,1,0:T(8,128)(2,1)S(1)} %get-tuple-element.8.refs_1_), custom_call_target="tpu_custom_call" | custom-call | bytes 1024 | tf_op jit(solution)/shard_map/take_rows/pallas_call | solution.py:70
  57.9 13.1 %all-to-all-done.2 = bf16[16,4,32,256]{3,2,1,0:T(8,128)(2,1)S(1)} async-done(((bf16[16,4,32,256]{3,2,1,0:T(8,128)(2,1)}), bf16[16,4,32,256]{3,2,1,0:T(8,128)(2,1)S(1)}, u32[]{:S(2)}, u32[]{:S(2)}) %all-to-all-start.2) | async-done | bytes 1048608 | tf_op jit(solution)/shard_map/all_to_all | solution.py:305
  71.0 4.3 %all-to-all-start.1 = ((bf16[16,4,32,256]{3,2,1,0:T(8,128)(2,1)}), bf16[16,4,32,256]{3,2,1,0:T(8,128)(2,1)}, u32[]{:S(2)}, u32[]{:S(2)}) async-start(bf16[16,4,32,256]{3,2,1,0:T(8,128)(2,1)} %bitcast.4), calls=%async_computation.1 | async-start | bytes 2097152 | tf_op jit(solution)/shard_map/all_to_all | solution.py:305
  75.4 16.3 %collective-permute-done.3.other_ref = bf16[16,128,256]{2,1,0:T(8,128)(2,1)S(1)} collective-permute-done((bf16[16,128,256]{2,1,0:T(8,128)(2,1)S(1)}, bf16[16,128,256]{2,1,0:T(8,128)(2,1)S(1)}, u32[]{:S(2)}, u32[]{:S(2)}) %collective-permute-start.3) | collective-permute-done | bytes 1048608 | tf_op jit(solution)/shard_map/ppermute | solution.py:51
  93.4 4.2 %low_levels.5.own_ref.refs_0_ = bf16[16,128,256]{2,1,0:T(8,128)(2,1)S(1)} custom-call(s32[1]{0:T(128)} %bitcast.order_ref, bf16[4,4,4,32,256]{4,3,2,1,0:T(8,128)(2,1)} %bitcast.8, bf16[6,2,16,128,128]{4,3,2,1,0:T(8,128)(2,1)} %self_ref.15, bf16[6,2,16,128,128]{4,3,2,1,0:T(8,128)(2,1)} %pair_ref.15, bf16[16,128,256]{2,1,0:T(8,128)(2,1)S(1)} %high_level.8.refs_3_.own_ref), custom_call_target="tpu_custom_call" | custom-call | bytes 1024 | tf_op jit(solution)/shard_map/low_levels/pallas_call | solution.py:204
  99.7 4.9 %collective-permute-start.1 = (bf16[4,4,32,256]{3,2,1,0:T(8,128)(2,1)}, bf16[4,4,32,256]{3,2,1,0:T(8,128)(2,1)}, u32[]{:S(2)}, u32[]{:S(2)}) collective-permute-start(bf16[4,4,32,256]{3,2,1,0:T(8,128)(2,1)} %get-tuple-element.9), channel_id=1, source_target_pairs={{0,4},{2,6},{4,0},{6,2},{1,5},{3,7},{5,1},{7,3},{8,12},{10,14},{12... | collective-permute-start | bytes 786440 | tf_op jit(solution)/shard_map/ppermute | solution.py:51
  108.1 47.0 %collective-permute-done.4.other_ref = bf16[16,128,256]{2,1,0:T(8,128)(2,1)S(1)} collective-permute-done((bf16[16,128,256]{2,1,0:T(8,128)(2,1)S(1)}, bf16[16,128,256]{2,1,0:T(8,128)(2,1)S(1)}, u32[]{:S(2)}, u32[]{:S(2)}) %collective-permute-start.4) | collective-permute-done | bytes 1048608 | tf_op jit(solution)/shard_map/ppermute | solution.py:51
  156.7 4.2 %low_levels.6.refs_4_.own_ref = bf16[16,128,256]{2,1,0:T(8,128)(2,1)S(1)} custom-call(s32[1]{0:T(128)} %bitcast.order_ref, bf16[4,4,4,32,256]{4,3,2,1,0:T(8,128)(2,1)} %bitcast.5.refs_0_, bf16[6,2,16,128,128]{4,3,2,1,0:T(8,128)(2,1)} %self_ref.15, bf16[6,2,16,128,128]{4,3,2,1,0:T(8,128)(2,1)} %pair_ref.15, bf16[16,128,256]{2,1,0:T(8,128)(2,1)S(1)} %high_level.9.refs_3_.own_ref), custom_call_target="tpu_custom_call" | custom-call | bytes 1024 | tf_op jit(solution)/shard_map/low_levels/pallas_call | solution.py:204
  161.1 2.7 gather_blocks.1.refs_0_
  164.8 4.2 %all-to-all-start.3 = ((bf16[4,4,4,32,256]{4,3,2,1,0:T(8,128)(2,1)}), bf16[4,4,4,32,256]{4,3,2,1,0:T(8,128)(2,1)}, u32[]{:S(2)}, u32[]{:S(2)}) async-start(bf16[4,4,4,32,256]{4,3,2,1,0:T(8,128)(2,1)} %copy-done), calls=%async_computation.3 | async-start | bytes 2097152 | tf_op jit(solution)/shard_map/all_to_all | solution.py:326
  169.0 3.1 collective-permute-start.8
  173.3 2.6 high_level.10.refs_0_
  175.9 29.9 %collective-permute-done.5.other_ref = bf16[16,128,256]{2,1,0:T(8,128)(2,1)} collective-permute-done((bf16[16,128,256]{2,1,0:T(8,128)(2,1)S(1)}, bf16[16,128,256]{2,1,0:T(8,128)(2,1)}, u32[]{:S(2)}, u32[]{:S(2)}) %collective-permute-start.5) | collective-permute-done | bytes 1048608 | tf_op jit(solution)/shard_map/ppermute | solution.py:51
  207.7 4.2 %low_levels.7.refs_1_.own_ref = bf16[16,128,256]{2,1,0:T(8,128)(2,1)S(1)} custom-call(s32[1]{0:T(128)} %bitcast.order_ref, bf16[4,4,4,32,256]{4,3,2,1,0:T(8,128)(2,1)} %all-to-all-done.3.refs_0_, bf16[6,2,16,128,128]{4,3,2,1,0:T(8,128)(2,1)} %self_ref.15, bf16[6,2,16,128,128]{4,3,2,1,0:T(8,128)(2,1)} %pair_ref.15, ...), custom_call_target="tpu_custom_call" | custom-call | bytes 1024 | tf_op jit(solution)/shard_map/low_levels/pallas_call | solution.py:204
  212.9 5.3 %collective-permute-done.8.other_ref = bf16[16,128,256]{2,1,0:T(8,128)(2,1)} collective-permute-done((bf16[16,128,256]{2,1,0:T(8,128)(2,1)S(1)}, bf16[16,128,256]{2,1,0:T(8,128)(2,1)}, u32[]{:S(2)}, u32[]{:S(2)}) %collective-permute-start.8) | collective-permute-done | bytes 1048608 | tf_op jit(solution)/shard_map/ppermute | solution.py:51
  220.9 34.7 %collective-permute-done.7.other_ref = bf16[16,128,256]{2,1,0:T(8,128)(2,1)S(1)} collective-permute-done((bf16[16,128,256]{2,1,0:T(8,128)(2,1)S(1)}, bf16[16,128,256]{2,1,0:T(8,128)(2,1)S(1)}, u32[]{:S(2)}, u32[]{:S(2)}) %collective-permute-start.7) | collective-permute-done | bytes 1048608 | tf_op jit(solution)/shard_map/ppermute | solution.py:51
  263.1 42.7 %collective-permute-done.9.other_ref = bf16[16,128,256]{2,1,0:T(8,128)(2,1)S(1)} collective-permute-done((bf16[16,128,256]{2,1,0:T(8,128)(2,1)S(1)}, bf16[16,128,256]{2,1,0:T(8,128)(2,1)S(1)}, u32[]{:S(2)}, u32[]{:S(2)}) %collective-permute-start.9) | collective-permute-done | bytes 1048608 | tf_op jit(solution)/shard_map/ppermute | solution.py:51
  (35 shorter events, 29.2 us)
Async XLA Ops:
  0.0 13.0 %copy-start.3 = (s32[8]{0:T(128)S(1)}, s32[8]{0:T(128)}, u32[]{:S(2)}) copy-start(s32[8]{0:T(128)} %slot_ref.9) | copy-start | bytes 100
  0.0 0.7 copy-start.2
  4.6 35.8 %all-to-all-start = ((bf16[16,4,32,256]{3,2,1,0:T(8,128)(2,1)}), bf16[16,4,32,256]{3,2,1,0:T(8,128)(2,1)S(1)}, u32[]{:S(2)}, u32[]{:S(2)}) async-start(bf16[16,4,32,256]{3,2,1,0:T(8,128)(2,1)} %bitcast.2), calls=%async_computation | async-start | bytes 2097152 | tf_op jit(solution)/shard_map/all_to_all | solution.py:305
  40.4 3.7 %copy-start.5 = (bf16[16,4,32,256]{3,2,1,0:T(8,128)(2,1)}, bf16[16,4,32,256]{3,2,1,0:T(8,128)(2,1)S(1)}, u32[]{:S(2)}) copy-start(bf16[16,4,32,256]{3,2,1,0:T(8,128)(2,1)S(1)} %all-to-all-done) | copy-start | bytes 3145732
  40.4 30.6 %all-to-all-start.2 = ((bf16[16,4,32,256]{3,2,1,0:T(8,128)(2,1)}), bf16[16,4,32,256]{3,2,1,0:T(8,128)(2,1)S(1)}, u32[]{:S(2)}, u32[]{:S(2)}) async-start(bf16[16,4,32,256]{3,2,1,0:T(8,128)(2,1)} %bitcast.6), calls=%async_computation.2 | async-start | bytes 2097152 | tf_op jit(solution)/shard_map/all_to_all | solution.py:305
  48.4 43.3 %collective-permute-start.3 = (bf16[16,128,256]{2,1,0:T(8,128)(2,1)S(1)}, bf16[16,128,256]{2,1,0:T(8,128)(2,1)S(1)}, u32[]{:S(2)}, u32[]{:S(2)}) collective-permute-start(bf16[16,128,256]{2,1,0:T(8,128)(2,1)S(1)} %low_levels.4.refs_3_.own_ref), channel_id=1, source_target_pairs={{0,2},{2,0},{4,6},{6,4},{1,3},{3,1},{5,7},{7,5},{8,10},{10,8},{12,... | collective-permute-start | bytes 3145736 | tf_op jit(solution)/shard_map/ppermute | solution.py:51
  71.0 4.4 %copy-start.4 = (bf16[16,4,32,256]{3,2,1,0:T(8,128)(2,1)}, bf16[16,4,32,256]{3,2,1,0:T(8,128)(2,1)S(1)}, u32[]{:S(2)}) copy-start(bf16[16,4,32,256]{3,2,1,0:T(8,128)(2,1)S(1)} %all-to-all-done.2) | copy-start | bytes 3145732
  71.0 85.7 %all-to-all-start.1 = ((bf16[16,4,32,256]{3,2,1,0:T(8,128)(2,1)}), bf16[16,4,32,256]{3,2,1,0:T(8,128)(2,1)}, u32[]{:S(2)}, u32[]{:S(2)}) async-start(bf16[16,4,32,256]{3,2,1,0:T(8,128)(2,1)} %bitcast.4), calls=%async_computation.1 | async-start | bytes 2097152 | tf_op jit(solution)/shard_map/all_to_all | solution.py:305
  97.6 57.4 %collective-permute-start.4 = (bf16[16,128,256]{2,1,0:T(8,128)(2,1)S(1)}, bf16[16,128,256]{2,1,0:T(8,128)(2,1)S(1)}, u32[]{:S(2)}, u32[]{:S(2)}) collective-permute-start(bf16[16,128,256]{2,1,0:T(8,128)(2,1)S(1)} %low_levels.5.own_ref.refs_0_), channel_id=1, source_target_pairs={{0,2},{2,0},{4,6},{6,4},{1,3},{3,1},{5,7},{7,5},{8,10},{10,8},{12,... | collective-permute-start | bytes 3145736 | tf_op jit(solution)/shard_map/ppermute | solution.py:51
  97.7 63.3 %collective-permute-start = (bf16[4,4,32,256]{3,2,1,0:T(8,128)(2,1)S(1)}, bf16[4,4,32,256]{3,2,1,0:T(8,128)(2,1)}, u32[]{:S(2)}, u32[]{:S(2)}) collective-permute-start(bf16[4,4,32,256]{3,2,1,0:T(8,128)(2,1)S(1)} %get-tuple-element.8.refs_1_), channel_id=1, source_target_pairs={{0,2},{2,0},{4,6},{6,4},{1,3},{3,1},{5,7},{7,5},{8,10},{10,8},{12,... | collective-permute-start | bytes 786440 | tf_op jit(solution)/shard_map/ppermute | solution.py:51
  99.7 61.3 %collective-permute-start.1 = (bf16[4,4,32,256]{3,2,1,0:T(8,128)(2,1)}, bf16[4,4,32,256]{3,2,1,0:T(8,128)(2,1)}, u32[]{:S(2)}, u32[]{:S(2)}) collective-permute-start(bf16[4,4,32,256]{3,2,1,0:T(8,128)(2,1)} %get-tuple-element.9), channel_id=1, source_target_pairs={{0,4},{2,6},{4,0},{6,2},{1,5},{3,7},{5,1},{7,3},{8,12},{10,14},{12... | collective-permute-start | bytes 786440 | tf_op jit(solution)/shard_map/ppermute | solution.py:51
  104.6 56.4 %collective-permute-start.2 = (bf16[4,4,32,256]{3,2,1,0:T(8,128)(2,1)}, bf16[4,4,32,256]{3,2,1,0:T(8,128)(2,1)}, u32[]{:S(2)}, u32[]{:S(2)}) collective-permute-start(bf16[4,4,32,256]{3,2,1,0:T(8,128)(2,1)} %get-tuple-element.10), channel_id=1, source_target_pairs={{0,6},{2,4},{4,2},{6,0},{1,7},{3,5},{5,3},{7,1},{8,14},{10,12},{12... | collective-permute-start | bytes 786440 | tf_op jit(solution)/shard_map/ppermute | solution.py:51
  106.0 66.0 %collective-permute-start.6 = (bf16[16,128,256]{2,1,0:T(8,128)(2,1)S(1)}, bf16[16,128,256]{2,1,0:T(8,128)(2,1)}, u32[]{:S(2)}, u32[]{:S(2)}) collective-permute-start(bf16[16,128,256]{2,1,0:T(8,128)(2,1)S(1)} %high_level.8.refs_3_.own_ref), channel_id=1, source_target_pairs={{0,4},{2,6},{4,0},{6,2},{1,5},{3,7},{5,1},{7,3},{8,12},{10,14},{12... | collective-permute-start | bytes 3145736 | tf_op jit(solution)/shard_map/ppermute | solution.py:51
  161.0 44.9 %collective-permute-start.5 = (bf16[16,128,256]{2,1,0:T(8,128)(2,1)S(1)}, bf16[16,128,256]{2,1,0:T(8,128)(2,1)}, u32[]{:S(2)}, u32[]{:S(2)}) collective-permute-start(bf16[16,128,256]{2,1,0:T(8,128)(2,1)S(1)} %low_levels.6.refs_4_.own_ref), channel_id=1, source_target_pairs={{0,2},{2,0},{4,6},{6,4},{1,3},{3,1},{5,7},{7,5},{8,10},{10,8},{12,... | collective-permute-start | bytes 3145736 | tf_op jit(solution)/shard_map/ppermute | solution.py:51
  163.8 1.0 copy-start
  164.8 42.9 %all-to-all-start.3 = ((bf16[4,4,4,32,256]{4,3,2,1,0:T(8,128)(2,1)}), bf16[4,4,4,32,256]{4,3,2,1,0:T(8,128)(2,1)}, u32[]{:S(2)}, u32[]{:S(2)}) async-start(bf16[4,4,4,32,256]{4,3,2,1,0:T(8,128)(2,1)} %copy-done), calls=%async_computation.3 | async-start | bytes 2097152 | tf_op jit(solution)/shard_map/all_to_all | solution.py:326
  169.0 49.2 %collective-permute-start.8 = (bf16[16,128,256]{2,1,0:T(8,128)(2,1)S(1)}, bf16[16,128,256]{2,1,0:T(8,128)(2,1)}, u32[]{:S(2)}, u32[]{:S(2)}) collective-permute-start(bf16[16,128,256]{2,1,0:T(8,128)(2,1)S(1)} %high_level.9.refs_3_.own_ref), channel_id=1, source_target_pairs={{0,4},{2,6},{4,0},{6,2},{1,5},{3,7},{5,1},{7,3},{8,12},{10,14},{12... | collective-permute-start | bytes 3145736 | tf_op jit(solution)/shard_map/ppermute | solution.py:51
  172.1 1.2 copy-start.1
  212.0 43.6 %collective-permute-start.7 = (bf16[16,128,256]{2,1,0:T(8,128)(2,1)S(1)}, bf16[16,128,256]{2,1,0:T(8,128)(2,1)S(1)}, u32[]{:S(2)}, u32[]{:S(2)}) collective-permute-start(bf16[16,128,256]{2,1,0:T(8,128)(2,1)S(1)} %low_levels.7.refs_1_.own_ref), channel_id=1, source_target_pairs={{0,2},{2,0},{4,6},{6,4},{1,3},{3,1},{5,7},{7,5},{8,10},{10,8},{12,... | collective-permute-start | bytes 3145736 | tf_op jit(solution)/shard_map/ppermute | solution.py:51
  212.1 48.6 %collective-permute-start.10 = (bf16[16,128,256]{2,1,0:T(8,128)(2,1)S(1)}, bf16[16,128,256]{2,1,0:T(8,128)(2,1)S(1)}, u32[]{:S(2)}, u32[]{:S(2)}) collective-permute-start(bf16[16,128,256]{2,1,0:T(8,128)(2,1)S(1)} %high_level.11.refs_3_.own_ref), channel_id=1, source_target_pairs={{0,4},{2,6},{4,0},{6,2},{1,5},{3,7},{5,1},{7,3},{8,12},{10,14},{12... | collective-permute-start | bytes 3145736 | tf_op jit(solution)/shard_map/ppermute | solution.py:51
  257.3 48.5 %collective-permute-start.9 = (bf16[16,128,256]{2,1,0:T(8,128)(2,1)S(1)}, bf16[16,128,256]{2,1,0:T(8,128)(2,1)S(1)}, u32[]{:S(2)}, u32[]{:S(2)}) collective-permute-start(bf16[16,128,256]{2,1,0:T(8,128)(2,1)S(1)} %high_level.13.refs_1_.own_ref), channel_id=1, source_target_pairs={{0,4},{2,6},{4,0},{6,2},{1,5},{3,7},{5,1},{7,3},{8,12},{10,14},{12... | collective-permute-start | bytes 3145736 | tf_op jit(solution)/shard_map/ppermute | solution.py:51

commit v6 on v5

--- a/solution.py
+++ b/solution.py
@@ -148,6 +148,7 @@
     level = pl.program_id(0)
     blocks = state.shape[0]
     bits = blocks.bit_length() - 1
+    fold = self_ref.shape[0]
     groups, first, second = rows_ref.shape[:3]
 
     def block_of(height, block):
@@ -161,7 +162,7 @@
 
     for height in range(bits):
 
-        @pl.when(level == height)
+        @pl.when(level == height // fold)
         def _(height=height):
             if height == 0 and count > 1:
                 for mask, source in enumerate(rows_refs):
@@ -169,6 +170,7 @@
                         (1,) + source.shape
                     )
             targets = out_refs if height == bits - 1 else (state,)
+            at = height % fold
             for low in range(blocks):
                 high = low ^ (1 << height)
                 if high < low:
@@ -176,8 +178,8 @@
                 values = jnp.concatenate(block_of(height, low) + block_of(height, high), axis=0)
                 factors = jnp.concatenate(
                     [
-                        jnp.concatenate([self_ref[0, 0, low], pair_ref[0, 0, low]], axis=1),
-                        jnp.concatenate([pair_ref[0, 0, high], self_ref[0, 0, high]], axis=1),
+                        jnp.concatenate([self_ref[at, 0, low], pair_ref[at, 0, low]], axis=1),
+                        jnp.concatenate([pair_ref[at, 0, high], self_ref[at, 0, high]], axis=1),
                     ],
                     axis=0,
                 )
@@ -196,7 +198,10 @@
     blocks, cycle = coeff_self.shape[2:4]
     bits = blocks.bit_length() - 1
     shape = (blocks, cycle, width // pieces)
-    factor = pl.BlockSpec((1, 1, blocks, cycle, cycle), lambda level, *order: (level, slot, 0, 0, 0))
+    fold = 2 if bits % 2 == 0 else 1
+    factor = pl.BlockSpec(
+        (fold, 1, blocks, cycle, cycle), lambda level, *order: (level, slot, 0, 0, 0)
+    )
     scratch = [pltpu.VMEM((blocks, cycle, width), rows[0].dtype)]
     scratch.append(
         pltpu.VMEM((len(rows),) + rows[0].shape if len(rows) > 1 else (8, 128), rows[0].dtype)
@@ -205,7 +210,7 @@
         functools.partial(low_kernel, source_first, len(rows), pieces),
         grid_spec=pltpu.PrefetchScalarGridSpec(
             num_scalar_prefetch=1,
-            grid=(bits,),
+            grid=(bits // fold,),
             in_specs=[
                 pl.BlockSpec(value.shape, lambda level, *order, rank=value.ndim: (0,) * rank)
                 for value in rows

time: 310 us -> 309 us (level)
  waiting for transfers between devices: 214 us -> 219 us
  Pallas kernels: 52.3 us -> 48.9 us
    ppermute x11, waiting for transfers between devices: 177 us -> 181 us  [swap(): return lax.ppermute(value, axis, pairs)]
    pallas_call x4, Pallas kernels: 17 us -> 13.6 us  [low_levels(): pl.pallas_call(functools.partial(low_kernel, source_first, len(rows), pie...]
  transfers between devices with their start and end apart: 15 -> 15, of which waited for: 9 -> 9; matrix products, arithmetic and copies ran while one was open for 0% -> 0% of each run, Pallas kernels for 15% -> 14%
where the time goes in v6:
time: 309 us; the launch traced here: 308 us
  waiting for transfers between devices  219 us (71%)
  Pallas kernels  48.9 us (16%)
  starting transfers between devices  37.1 us (12%)
    ppermute x11, waiting for transfers between devices, swap(): return lax.ppermute(value, axis, pairs)  181 us
    all_to_all x3, waiting for transfers between devices, local(): lax.all_to_all(value, ('order', 'level'), split_axis=0, concat_axis=0, ti...  37.5 us
    pallas_call x8, Pallas kernels, high_level(): pl.pallas_call(high_kernel, grid=(blocks // step,), in_specs=in_specs + a...  17.1 us
    ppermute x11, starting transfers between devices, swap(): return lax.ppermute(value, axis, pairs)  16.6 us
    all_to_all x3, starting transfers between devices, local(): lax.all_to_all(value, ('order', 'level'), split_axis=0, concat_axis=0, ti...  16.3 us
    pallas_call x4, Pallas kernels, take_rows(): pl.pallas_call(functools.partial(copy_kernel, len(masks) or 1), grid_spec...  15.5 us
    pallas_call x4, Pallas kernels, low_levels(): pl.pallas_call(functools.partial(low_kernel, source_first, len(rows), pie...  13.6 us
  transfers between devices with their start and end apart: 15, of which 9 were waited for; matrix products, arithmetic and copies ran while one was open for 0% of the time, Pallas kernels for 14%

profile of v6, /device:TPU:0, one launch (start us, length us, event | category | flops | bytes accessed | tf_op | source)
XLA Modules:
  0.0 308.1 jit_solution(5320346380958532193)
XLA Ops:
  0.7 3.9 %take_rows.4.refs_1_ = bf16[4,16,32,256]{3,2,1,0:T(8,128)(2,1)} custom-call(s32[1]{0:T(128)} %bitcast.1.level_ref, s32[1]{0:T(128)} %bitcast.order_ref, s32[8]{0:T(128)S(1)} %copy-done.2, bf16[8,16,1,32,512]{4,3,2,1,0:T(8,128)(2,1)} %refs_0_.9), custom_call_target="tpu_custom_call" | custom-call | bytes 1024 | tf_op jit(solution)/shard_map/take_rows/pallas_call | solution.py:70
  4.6 8.3 %all-to-all-start = ((bf16[16,4,32,256]{3,2,1,0:T(8,128)(2,1)}), bf16[16,4,32,256]{3,2,1,0:T(8,128)(2,1)S(1)}, u32[]{:S(2)}, u32[]{:S(2)}) async-start(bf16[16,4,32,256]{3,2,1,0:T(8,128)(2,1)} %bitcast.2), calls=%async_computation | async-start | bytes 2097152 | tf_op jit(solution)/shard_map/all_to_all | solution.py:310
  13.0 3.9 %take_rows.5.refs_3_ = bf16[4,16,32,256]{3,2,1,0:T(8,128)(2,1)} custom-call(s32[1]{0:T(128)} %bitcast.1.level_ref, s32[1]{0:T(128)} %bitcast.order_ref, s32[8]{0:T(128)S(1)} %copy-done.3, bf16[8,16,1,32,512]{4,3,2,1,0:T(8,128)(2,1)} %refs_0_.9, bf16[4,16,32,256]{3,2,1,0:T(8,128)(2,1)} %take_rows.4.refs_1_), custom_call_target="tpu_custom_call" | custom-call | bytes 1024 | tf_op jit(solution)/shard_map/take_rows/pallas_call | solution.py:70
  16.9 23.5 %all-to-all-done = bf16[16,4,32,256]{3,2,1,0:T(8,128)(2,1)S(1)} async-done(((bf16[16,4,32,256]{3,2,1,0:T(8,128)(2,1)}), bf16[16,4,32,256]{3,2,1,0:T(8,128)(2,1)S(1)}, u32[]{:S(2)}, u32[]{:S(2)}) %all-to-all-start) | async-done | bytes 1048608 | tf_op jit(solution)/shard_map/all_to_all | solution.py:310
  40.4 3.7 %all-to-all-start.2 = ((bf16[16,4,32,256]{3,2,1,0:T(8,128)(2,1)}), bf16[16,4,32,256]{3,2,1,0:T(8,128)(2,1)S(1)}, u32[]{:S(2)}, u32[]{:S(2)}) async-start(bf16[16,4,32,256]{3,2,1,0:T(8,128)(2,1)} %bitcast.6), calls=%async_computation.2 | async-start | bytes 2097152 | tf_op jit(solution)/shard_map/all_to_all | solution.py:310
  44.1 3.4 %low_levels.4.refs_3_.own_ref = bf16[16,128,256]{2,1,0:T(8,128)(2,1)S(1)} custom-call(s32[1]{0:T(128)} %bitcast.order_ref, bf16[4,4,4,32,256]{4,3,2,1,0:T(8,128)(2,1)} %bitcast.9, bf16[6,2,16,128,128]{4,3,2,1,0:T(8,128)(2,1)} %self_ref.15, bf16[6,2,16,128,128]{4,3,2,1,0:T(8,128)(2,1)} %pair_ref.15, bf16[4,16,32,256]{3,2,1,0:T(8,128)(2,1)} %take_rows.5.refs_3_), custom_call_target="tpu_custom_call" | custom-call | bytes 1024 | tf_op jit(solution)/shard_map/low_levels/pallas_call | solution.py:209
  49.4 3.7 %take_rows.6 = (bf16[4,4,32,256]{3,2,1,0:T(8,128)(2,1)S(1)}, bf16[4,4,32,256]{3,2,1,0:T(8,128)(2,1)}, bf16[4,4,32,256]{3,2,1,0:T(8,128)(2,1)}) custom-call(s32[1]{0:T(128)} %bitcast.1.level_ref, s32[1]{0:T(128)} %bitcast.order_ref, s32[8]{0:T(128)S(1)} %copy-done.3, bf16[8,16,1,32,512]{4,3,2,1,0:T(8,128)(2,1)} %refs_0_.9, ...), custom_call_target="tpu_custom_call" | custom-call | bytes 1024 | tf_op jit(solution)/shard_map/take_rows/pallas_call | solution.py:70
  53.1 3.9 %take_rows.7.refs_0_ = bf16[4,16,32,256]{3,2,1,0:T(8,128)(2,1)} custom-call(s32[1]{0:T(128)} %bitcast.1.level_ref, s32[1]{0:T(128)} %bitcast.order_ref, s32[8]{0:T(128)S(1)} %copy-done.3, bf16[8,16,1,32,512]{4,3,2,1,0:T(8,128)(2,1)} %refs_0_.9, bf16[4,4,32,256]{3,2,1,0:T(8,128)(2,1)S(1)} %get-tuple-element.8.refs_1_), custom_call_target="tpu_custom_call" | custom-call | bytes 1024 | tf_op jit(solution)/shard_map/take_rows/pallas_call | solution.py:70
  57.0 14.0 %all-to-all-done.2 = bf16[16,4,32,256]{3,2,1,0:T(8,128)(2,1)S(1)} async-done(((bf16[16,4,32,256]{3,2,1,0:T(8,128)(2,1)}), bf16[16,4,32,256]{3,2,1,0:T(8,128)(2,1)S(1)}, u32[]{:S(2)}, u32[]{:S(2)}) %all-to-all-start.2) | async-done | bytes 1048608 | tf_op jit(solution)/shard_map/all_to_all | solution.py:310
  71.0 4.3 %all-to-all-start.1 = ((bf16[16,4,32,256]{3,2,1,0:T(8,128)(2,1)}), bf16[16,4,32,256]{3,2,1,0:T(8,128)(2,1)}, u32[]{:S(2)}, u32[]{:S(2)}) async-start(bf16[16,4,32,256]{3,2,1,0:T(8,128)(2,1)} %bitcast.4), calls=%async_computation.1 | async-start | bytes 2097152 | tf_op jit(solution)/shard_map/all_to_all | solution.py:310
  75.4 16.3 %collective-permute-done.3.other_ref = bf16[16,128,256]{2,1,0:T(8,128)(2,1)S(1)} collective-permute-done((bf16[16,128,256]{2,1,0:T(8,128)(2,1)S(1)}, bf16[16,128,256]{2,1,0:T(8,128)(2,1)S(1)}, u32[]{:S(2)}, u32[]{:S(2)}) %collective-permute-start.3) | collective-permute-done | bytes 1048608 | tf_op jit(solution)/shard_map/ppermute | solution.py:51
  93.4 3.4 %low_levels.5.own_ref.refs_0_ = bf16[16,128,256]{2,1,0:T(8,128)(2,1)S(1)} custom-call(s32[1]{0:T(128)} %bitcast.order_ref, bf16[4,4,4,32,256]{4,3,2,1,0:T(8,128)(2,1)} %bitcast.8, bf16[6,2,16,128,128]{4,3,2,1,0:T(8,128)(2,1)} %self_ref.15, bf16[6,2,16,128,128]{4,3,2,1,0:T(8,128)(2,1)} %pair_ref.15, bf16[16,128,256]{2,1,0:T(8,128)(2,1)S(1)} %high_level.8.refs_3_.own_ref), custom_call_target="tpu_custom_call" | custom-call | bytes 1024 | tf_op jit(solution)/shard_map/low_levels/pallas_call | solution.py:209
  98.9 4.9 %collective-permute-start.1 = (bf16[4,4,32,256]{3,2,1,0:T(8,128)(2,1)}, bf16[4,4,32,256]{3,2,1,0:T(8,128)(2,1)}, u32[]{:S(2)}, u32[]{:S(2)}) collective-permute-start(bf16[4,4,32,256]{3,2,1,0:T(8,128)(2,1)} %get-tuple-element.9), channel_id=1, source_target_pairs={{0,4},{2,6},{4,0},{6,2},{1,5},{3,7},{5,1},{7,3},{8,12},{10,14},{12... | collective-permute-start | bytes 786440 | tf_op jit(solution)/shard_map/ppermute | solution.py:51
  107.2 48.2 %collective-permute-done.4.other_ref = bf16[16,128,256]{2,1,0:T(8,128)(2,1)S(1)} collective-permute-done((bf16[16,128,256]{2,1,0:T(8,128)(2,1)S(1)}, bf16[16,128,256]{2,1,0:T(8,128)(2,1)S(1)}, u32[]{:S(2)}, u32[]{:S(2)}) %collective-permute-start.4) | collective-permute-done | bytes 1048608 | tf_op jit(solution)/shard_map/ppermute | solution.py:51
  157.2 3.4 %low_levels.6.refs_4_.own_ref = bf16[16,128,256]{2,1,0:T(8,128)(2,1)S(1)} custom-call(s32[1]{0:T(128)} %bitcast.order_ref, bf16[4,4,4,32,256]{4,3,2,1,0:T(8,128)(2,1)} %bitcast.5.refs_0_, bf16[6,2,16,128,128]{4,3,2,1,0:T(8,128)(2,1)} %self_ref.15, bf16[6,2,16,128,128]{4,3,2,1,0:T(8,128)(2,1)} %pair_ref.15, bf16[16,128,256]{2,1,0:T(8,128)(2,1)S(1)} %high_level.9.refs_3_.own_ref), custom_call_target="tpu_custom_call" | custom-call | bytes 1024 | tf_op jit(solution)/shard_map/low_levels/pallas_call | solution.py:209
  160.7 2.7 gather_blocks.1.refs_0_
  164.4 4.2 %all-to-all-start.3 = ((bf16[4,4,4,32,256]{4,3,2,1,0:T(8,128)(2,1)}), bf16[4,4,4,32,256]{4,3,2,1,0:T(8,128)(2,1)}, u32[]{:S(2)}, u32[]{:S(2)}) async-start(bf16[4,4,4,32,256]{4,3,2,1,0:T(8,128)(2,1)} %copy-done), calls=%async_computation.3 | async-start | bytes 2097152 | tf_op jit(solution)/shard_map/all_to_all | solution.py:331
  175.1 29.9 %collective-permute-done.5.other_ref = bf16[16,128,256]{2,1,0:T(8,128)(2,1)} collective-permute-done((bf16[16,128,256]{2,1,0:T(8,128)(2,1)S(1)}, bf16[16,128,256]{2,1,0:T(8,128)(2,1)}, u32[]{:S(2)}, u32[]{:S(2)}) %collective-permute-start.5) | collective-permute-done | bytes 1048608 | tf_op jit(solution)/shard_map/ppermute | solution.py:51
  206.9 3.4 %low_levels.7.refs_1_.own_ref = bf16[16,128,256]{2,1,0:T(8,128)(2,1)S(1)} custom-call(s32[1]{0:T(128)} %bitcast.order_ref, bf16[4,4,4,32,256]{4,3,2,1,0:T(8,128)(2,1)} %all-to-all-done.3.refs_0_, bf16[6,2,16,128,128]{4,3,2,1,0:T(8,128)(2,1)} %self_ref.15, bf16[6,2,16,128,128]{4,3,2,1,0:T(8,128)(2,1)} %pair_ref.15, ...), custom_call_target="tpu_custom_call" | custom-call | bytes 1024 | tf_op jit(solution)/shard_map/low_levels/pallas_call | solution.py:209
  211.6 6.7 %collective-permute-done.8.other_ref = bf16[16,128,256]{2,1,0:T(8,128)(2,1)} collective-permute-done((bf16[16,128,256]{2,1,0:T(8,128)(2,1)S(1)}, bf16[16,128,256]{2,1,0:T(8,128)(2,1)}, u32[]{:S(2)}, u32[]{:S(2)}) %collective-permute-start.8) | collective-permute-done | bytes 1048608 | tf_op jit(solution)/shard_map/ppermute | solution.py:51
  218.3 2.6 high_level.12.refs_0_
  221.0 33.5 %collective-permute-done.7.other_ref = bf16[16,128,256]{2,1,0:T(8,128)(2,1)S(1)} collective-permute-done((bf16[16,128,256]{2,1,0:T(8,128)(2,1)S(1)}, bf16[16,128,256]{2,1,0:T(8,128)(2,1)S(1)}, u32[]{:S(2)}, u32[]{:S(2)}) %collective-permute-start.7) | collective-permute-done | bytes 1048608 | tf_op jit(solution)/shard_map/ppermute | solution.py:51
  256.4 28.8 %collective-permute-done.10.other_ref = bf16[16,128,256]{2,1,0:T(8,128)(2,1)S(1)} collective-permute-done((bf16[16,128,256]{2,1,0:T(8,128)(2,1)S(1)}, bf16[16,128,256]{2,1,0:T(8,128)(2,1)S(1)}, u32[]{:S(2)}, u32[]{:S(2)}) %collective-permute-start.10) | collective-permute-done | bytes 1048608 | tf_op jit(solution)/shard_map/ppermute | solution.py:51
  287.7 17.9 %collective-permute-done.9.other_ref = bf16[16,128,256]{2,1,0:T(8,128)(2,1)S(1)} collective-permute-done((bf16[16,128,256]{2,1,0:T(8,128)(2,1)S(1)}, bf16[16,128,256]{2,1,0:T(8,128)(2,1)S(1)}, u32[]{:S(2)}, u32[]{:S(2)}) %collective-permute-start.9) | collective-permute-done | bytes 1048608 | tf_op jit(solution)/shard_map/ppermute | solution.py:51
  (35 shorter events, 29.1 us)
Async XLA Ops:
  0.0 13.0 %copy-start.3 = (s32[8]{0:T(128)S(1)}, s32[8]{0:T(128)}, u32[]{:S(2)}) copy-start(s32[8]{0:T(128)} %slot_ref.9) | copy-start | bytes 100
  0.0 0.7 copy-start.2
  4.6 35.8 %all-to-all-start = ((bf16[16,4,32,256]{3,2,1,0:T(8,128)(2,1)}), bf16[16,4,32,256]{3,2,1,0:T(8,128)(2,1)S(1)}, u32[]{:S(2)}, u32[]{:S(2)}) async-start(bf16[16,4,32,256]{3,2,1,0:T(8,128)(2,1)} %bitcast.2), calls=%async_computation | async-start | bytes 2097152 | tf_op jit(solution)/shard_map/all_to_all | solution.py:310
  40.4 3.7 %copy-start.5 = (bf16[16,4,32,256]{3,2,1,0:T(8,128)(2,1)}, bf16[16,4,32,256]{3,2,1,0:T(8,128)(2,1)S(1)}, u32[]{:S(2)}) copy-start(bf16[16,4,32,256]{3,2,1,0:T(8,128)(2,1)S(1)} %all-to-all-done) | copy-start | bytes 3145732
  40.4 30.6 %all-to-all-start.2 = ((bf16[16,4,32,256]{3,2,1,0:T(8,128)(2,1)}), bf16[16,4,32,256]{3,2,1,0:T(8,128)(2,1)S(1)}, u32[]{:S(2)}, u32[]{:S(2)}) async-start(bf16[16,4,32,256]{3,2,1,0:T(8,128)(2,1)} %bitcast.6), calls=%async_computation.2 | async-start | bytes 2097152 | tf_op jit(solution)/shard_map/all_to_all | solution.py:310
  47.5 44.2 %collective-permute-start.3 = (bf16[16,128,256]{2,1,0:T(8,128)(2,1)S(1)}, bf16[16,128,256]{2,1,0:T(8,128)(2,1)S(1)}, u32[]{:S(2)}, u32[]{:S(2)}) collective-permute-start(bf16[16,128,256]{2,1,0:T(8,128)(2,1)S(1)} %low_levels.4.refs_3_.own_ref), channel_id=1, source_target_pairs={{0,2},{2,0},{4,6},{6,4},{1,3},{3,1},{5,7},{7,5},{8,10},{10,8},{12,... | collective-permute-start | bytes 3145736 | tf_op jit(solution)/shard_map/ppermute | solution.py:51
  71.0 4.4 %copy-start.4 = (bf16[16,4,32,256]{3,2,1,0:T(8,128)(2,1)}, bf16[16,4,32,256]{3,2,1,0:T(8,128)(2,1)S(1)}, u32[]{:S(2)}) copy-start(bf16[16,4,32,256]{3,2,1,0:T(8,128)(2,1)S(1)} %all-to-all-done.2) | copy-start | bytes 3145732
  71.0 86.1 %all-to-all-start.1 = ((bf16[16,4,32,256]{3,2,1,0:T(8,128)(2,1)}), bf16[16,4,32,256]{3,2,1,0:T(8,128)(2,1)}, u32[]{:S(2)}, u32[]{:S(2)}) async-start(bf16[16,4,32,256]{3,2,1,0:T(8,128)(2,1)} %bitcast.4), calls=%async_computation.1 | async-start | bytes 2097152 | tf_op jit(solution)/shard_map/all_to_all | solution.py:310
  96.8 58.7 %collective-permute-start.4 = (bf16[16,128,256]{2,1,0:T(8,128)(2,1)S(1)}, bf16[16,128,256]{2,1,0:T(8,128)(2,1)S(1)}, u32[]{:S(2)}, u32[]{:S(2)}) collective-permute-start(bf16[16,128,256]{2,1,0:T(8,128)(2,1)S(1)} %low_levels.5.own_ref.refs_0_), channel_id=1, source_target_pairs={{0,2},{2,0},{4,6},{6,4},{1,3},{3,1},{5,7},{7,5},{8,10},{10,8},{12,... | collective-permute-start | bytes 3145736 | tf_op jit(solution)/shard_map/ppermute | solution.py:51
  96.9 63.8 %collective-permute-start = (bf16[4,4,32,256]{3,2,1,0:T(8,128)(2,1)S(1)}, bf16[4,4,32,256]{3,2,1,0:T(8,128)(2,1)}, u32[]{:S(2)}, u32[]{:S(2)}) collective-permute-start(bf16[4,4,32,256]{3,2,1,0:T(8,128)(2,1)S(1)} %get-tuple-element.8.refs_1_), channel_id=1, source_target_pairs={{0,2},{2,0},{4,6},{6,4},{1,3},{3,1},{5,7},{7,5},{8,10},{10,8},{12,... | collective-permute-start | bytes 786440 | tf_op jit(solution)/shard_map/ppermute | solution.py:51
  98.9 61.8 %collective-permute-start.1 = (bf16[4,4,32,256]{3,2,1,0:T(8,128)(2,1)}, bf16[4,4,32,256]{3,2,1,0:T(8,128)(2,1)}, u32[]{:S(2)}, u32[]{:S(2)}) collective-permute-start(bf16[4,4,32,256]{3,2,1,0:T(8,128)(2,1)} %get-tuple-element.9), channel_id=1, source_target_pairs={{0,4},{2,6},{4,0},{6,2},{1,5},{3,7},{5,1},{7,3},{8,12},{10,14},{12... | collective-permute-start | bytes 786440 | tf_op jit(solution)/shard_map/ppermute | solution.py:51
  103.8 56.9 %collective-permute-start.2 = (bf16[4,4,32,256]{3,2,1,0:T(8,128)(2,1)}, bf16[4,4,32,256]{3,2,1,0:T(8,128)(2,1)}, u32[]{:S(2)}, u32[]{:S(2)}) collective-permute-start(bf16[4,4,32,256]{3,2,1,0:T(8,128)(2,1)} %get-tuple-element.10), channel_id=1, source_target_pairs={{0,6},{2,4},{4,2},{6,0},{1,7},{3,5},{5,3},{7,1},{8,14},{10,12},{12... | collective-permute-start | bytes 786440 | tf_op jit(solution)/shard_map/ppermute | solution.py:51
  105.2 66.0 %collective-permute-start.6 = (bf16[16,128,256]{2,1,0:T(8,128)(2,1)S(1)}, bf16[16,128,256]{2,1,0:T(8,128)(2,1)}, u32[]{:S(2)}, u32[]{:S(2)}) collective-permute-start(bf16[16,128,256]{2,1,0:T(8,128)(2,1)S(1)} %high_level.8.refs_3_.own_ref), channel_id=1, source_target_pairs={{0,4},{2,6},{4,0},{6,2},{1,5},{3,7},{5,1},{7,3},{8,12},{10,14},{12... | collective-permute-start | bytes 3145736 | tf_op jit(solution)/shard_map/ppermute | solution.py:51
  160.6 44.5 %collective-permute-start.5 = (bf16[16,128,256]{2,1,0:T(8,128)(2,1)S(1)}, bf16[16,128,256]{2,1,0:T(8,128)(2,1)}, u32[]{:S(2)}, u32[]{:S(2)}) collective-permute-start(bf16[16,128,256]{2,1,0:T(8,128)(2,1)S(1)} %low_levels.6.refs_4_.own_ref), channel_id=1, source_target_pairs={{0,2},{2,0},{4,6},{6,4},{1,3},{3,1},{5,7},{7,5},{8,10},{10,8},{12,... | collective-permute-start | bytes 3145736 | tf_op jit(solution)/shard_map/ppermute | solution.py:51
  163.4 1.0 copy-start
  164.4 42.5 %all-to-all-start.3 = ((bf16[4,4,4,32,256]{4,3,2,1,0:T(8,128)(2,1)}), bf16[4,4,4,32,256]{4,3,2,1,0:T(8,128)(2,1)}, u32[]{:S(2)}, u32[]{:S(2)}) async-start(bf16[4,4,4,32,256]{4,3,2,1,0:T(8,128)(2,1)} %copy-done), calls=%async_computation.3 | async-start | bytes 2097152 | tf_op jit(solution)/shard_map/all_to_all | solution.py:331
  168.6 49.7 %collective-permute-start.8 = (bf16[16,128,256]{2,1,0:T(8,128)(2,1)S(1)}, bf16[16,128,256]{2,1,0:T(8,128)(2,1)}, u32[]{:S(2)}, u32[]{:S(2)}) collective-permute-start(bf16[16,128,256]{2,1,0:T(8,128)(2,1)S(1)} %high_level.9.refs_3_.own_ref), channel_id=1, source_target_pairs={{0,4},{2,6},{4,0},{6,2},{1,5},{3,7},{5,1},{7,3},{8,12},{10,14},{12... | collective-permute-start | bytes 3145736 | tf_op jit(solution)/shard_map/ppermute | solution.py:51
  171.2 1.2 copy-start.1
  210.3 44.2 %collective-permute-start.7 = (bf16[16,128,256]{2,1,0:T(8,128)(2,1)S(1)}, bf16[16,128,256]{2,1,0:T(8,128)(2,1)S(1)}, u32[]{:S(2)}, u32[]{:S(2)}) collective-permute-start(bf16[16,128,256]{2,1,0:T(8,128)(2,1)S(1)} %low_levels.7.refs_1_.own_ref), channel_id=1, source_target_pairs={{0,2},{2,0},{4,6},{6,4},{1,3},{3,1},{5,7},{7,5},{8,10},{10,8},{12,... | collective-permute-start | bytes 3145736 | tf_op jit(solution)/shard_map/ppermute | solution.py:51
  210.4 74.9 %collective-permute-start.10 = (bf16[16,128,256]{2,1,0:T(8,128)(2,1)S(1)}, bf16[16,128,256]{2,1,0:T(8,128)(2,1)S(1)}, u32[]{:S(2)}, u32[]{:S(2)}) collective-permute-start(bf16[16,128,256]{2,1,0:T(8,128)(2,1)S(1)} %high_level.11.refs_3_.own_ref), channel_id=1, source_target_pairs={{0,4},{2,6},{4,0},{6,2},{1,5},{3,7},{5,1},{7,3},{8,12},{10,14},{12... | collective-permute-start | bytes 3145736 | tf_op jit(solution)/shard_map/ppermute | solution.py:51
  256.2 49.4 %collective-permute-start.9 = (bf16[16,128,256]{2,1,0:T(8,128)(2,1)S(1)}, bf16[16,128,256]{2,1,0:T(8,128)(2,1)S(1)}, u32[]{:S(2)}, u32[]{:S(2)}) collective-permute-start(bf16[16,128,256]{2,1,0:T(8,128)(2,1)S(1)} %high_level.13.refs_1_.own_ref), channel_id=1, source_target_pairs={{0,4},{2,6},{4,0},{6,2},{1,5},{3,7},{5,1},{7,3},{8,12},{10,14},{12... | collective-permute-start | bytes 3145736 | tf_op jit(solution)/shard_map/ppermute | solution.py:51
